TPU v7x, 256 devices: a whole 4x4x8 slice. The times are simulated.
256 devices in a mesh: tile: 16 (over y_lo, x, core), tracer: 16 (over y_hi, z).
Axes of the slice: x: 4, y: 4 (y_hi: 2, y_lo: 2; y = y_hi * 2 + y_lo), z: 8, core: 2. Of those that a mesh axis runs over, the one named last changes fastest.
Arguments:
- tracers: float32 [32, 24, 512, 256], P('tracer', None, 'tile'), may hold values from 0.1 to 4
- east_speed: float32 [24, 512, 256], P(None, 'tile'), may hold values from -2.5 to 2.5
- north_speed: float32 [24, 512, 256], P(None, 'tile'), may hold values from -2.5 to 2.5
- land_mask: int32 [512, 256], P('tile'), may hold values 0 or 1
- bottom_level: int32 [512, 256], P('tile'), may hold values from 1 to 24
- in_weight: bfloat16 [32, 512], replicated, may hold values from -1 to 1
- in_bias: float32 [512], replicated, may hold values from -4 to 4
- mid_weight: bfloat16 [512, 512], replicated, may hold values from -0.25 to 0.25
- mid_bias: float32 [512], replicated, may hold values from -4 to 4
- out_weight: bfloat16 [512, 32], replicated, may hold values from -0.25 to 0.25
Outputs:
- advanced: float32 [32, 24, 512, 256], P('tracer', None, 'tile')
All inputs are finite; a program needn't handle non-finite values. No bound on the sum of `land_mask` on one device may be relied on, other than what follows from the above.
Results may differ from a plain program's by a relative error of at most 0.002.
Values may be sent and summed in bfloat16 or wider, within the bound.
No kernel may reach another device: no remote copies, remote signals or barrier semaphores. Data moves between devices by JAX's collectives and lax.ppermute only.
A program may use at most 192 MiB of HBM per device.

v0:
```python
import math

import jax
import jax.numpy as jnp
from jax import lax
from jax.sharding import PartitionSpec as P

STEPS = 2


diffusion = 0.2
time_step = 0.2


def with_halo(value, sides, width):
    for axis, dim in sides:
        size, length = (lax.axis_size(axis), value.shape[dim])
        up = [(i, (i + 1) % size) for i in range(size - 1)]
        down = [(j, i) for i, j in up]
        last = lax.slice_in_dim(value, length - width, length, axis=dim)
        initial = lax.slice_in_dim(value, 0, width, axis=dim)
        before = lax.ppermute(last, axis, up)
        after = lax.ppermute(initial, axis, down)
        value = jnp.concatenate([before, value, after], axis=dim)
    return value


def as_sent(value):
    return jax.tree.map(lambda a: a.astype(jnp.bfloat16) if a.dtype == jnp.float32 else a, value)


def face_flux(behind_cells, ahead_cells, flow_speed, opened):
    moved = jnp.maximum(flow_speed, 0.0) * behind_cells + jnp.minimum(flow_speed, 0.0) * ahead_cells
    return opened * (moved - diffusion * (ahead_cells - behind_cells))


def network(inputs, in_weight, in_bias, mid_weight, mid_bias, out_weight):
    kinds, depth, rows, cols = inputs.shape
    cells = depth * rows * cols
    turns = math.gcd(cells, 8)
    blocked = jnp.moveaxis(inputs.reshape(kinds, turns, cells // turns), 1, 0)

    def one_block(cell_block):
        first_hidden = (
            jnp.einsum("tn,th->nh", cell_block, in_weight, preferred_element_type=jnp.float32)
            + in_bias
        )
        first_hidden = jax.nn.silu(first_hidden).astype(jnp.bfloat16)
        second_hidden = (
            jnp.einsum("nh,hk->nk", first_hidden, mid_weight, preferred_element_type=jnp.float32)
            + mid_bias
        )
        second_hidden = jax.nn.silu(second_hidden).astype(jnp.bfloat16)
        return jnp.einsum(
            "nh,ht->tn", second_hidden, out_weight, preferred_element_type=jnp.float32
        ).astype(jnp.bfloat16)

    result = jnp.moveaxis(lax.map(one_block, blocked), 0, 1)
    return result.reshape(result.shape[0], depth, rows, cols)


def body(
    tracers,
    east_speed,
    north_speed,
    land_mask,
    bottom_level,
    in_weight,
    in_bias,
    mid_weight,
    mid_bias,
    out_weight,
):
    levels = east_speed.shape[0]
    depth = jnp.arange(levels, dtype=jnp.int32)[:, None, None]
    wet_cells = ((land_mask[None] == 1) & (depth < bottom_level[None])).astype(jnp.float32)
    geometry = with_halo(
        jnp.stack([east_speed, wet_cells]).astype(jnp.bfloat16), (("tile", 2),), 1
    ).astype(jnp.float32)
    flow_x = geometry[0, :, :-1]
    wet_x = geometry[1]
    opened_x = wet_x[:, :-1] * wet_x[:, 1:]
    flow_y = jnp.pad(north_speed, ((0, 0), (0, 0), (1, 0)))
    wet_y = jnp.pad(wet_cells, ((0, 0), (0, 0), (1, 1)))
    opened_y = wet_y[..., :-1] * wet_y[..., 1:]
    field = tracers
    for step in range(STEPS):
        padded = with_halo(as_sent(field), (("tile", 2),), 1).astype(field.dtype)
        inputs = field.astype(jnp.bfloat16)
        local_sources = network(
            lax.all_to_all(inputs, "tracer", split_axis=2, concat_axis=0, tiled=True),
            in_weight,
            in_bias,
            mid_weight,
            mid_bias,
            out_weight,
        )
        sources = lax.all_to_all(local_sources, "tracer", split_axis=0, concat_axis=2, tiled=True)
        x_flux = face_flux(padded[:, :, :-1], padded[:, :, 1:], flow_x, opened_x)
        cells_y = jnp.pad(field, ((0, 0), (0, 0), (0, 0), (1, 1)))
        y_flux = face_flux(cells_y[..., :-1], cells_y[..., 1:], flow_y, opened_y)
        tendency = x_flux[:, :, :-1] - x_flux[:, :, 1:] + (y_flux[..., :-1] - y_flux[..., 1:])
        field = wet_cells[None] * (field + time_step * (tendency + sources.astype(jnp.float32)))
    return field


def solution(mesh):
    return jax.shard_map(
        body,
        mesh=mesh,
        in_specs=(
            P("tracer", None, "tile", None),
            P(None, "tile", None),
            P(None, "tile", None),
            P("tile", None),
            P("tile", None),
            P(),
            P(),
            P(),
            P(),
            P(),
        ),
        out_specs=P("tracer", None, "tile", None),
        check_vma=False,
    )
```

profile of v0, /device:TPU:2, one launch (start us, length us, event | category | flops | bytes accessed | tf_op | source)
XLA Modules:
  0.0 254.7 jit_solution(3107881122704696486)
XLA Ops:
  3.3 11.2 %all-to-all-start = ((bf16[2,24,32,256]{3,1,0,2:T(8,128)(2,1)}), bf16[2,24,32,256]{3,1,0,2:T(8,128)(2,1)}, u32[]{:S(2)}, u32[]{:S(2)}) async-start(bf16[2,24,32,256]{3,1,0,2:T(8,128)(2,1)} %copy.66), calls=%async_computation | async-start | bytes 1572864 | tf_op jit(solution)/shard_map/all_to_all | solution.py:91
  20.5 3.2 %collective-permute-start.1 = (bf16[2,24,1,256]{3,2,1,0:T(2,128)(2,1)S(1)}, bf16[2,24,1,256]{3,2,1,0:T(2,128)(2,1)S(1)}, u32[]{:S(2)}, u32[]{:S(2)}) collective-permute-start(bf16[2,24,1,256]{3,2,1,0:T(2,128)(2,1)S(1)} %get-tuple-element.194), channel_id=1, source_target_pairs={{16,0},{32,16},{48,32},{64,48},{80,64},{96,80},{112,96},{128,112},... | collective-permute-start | bytes 73736 | tf_op jit(solution)/shard_map/ppermute | solution.py:23
  40.0 3.2 %reshape.46 = bf16[32,8,1536]{2,1,0:T(8,128)(2,1)} reshape(bf16[16,2,24,2,256]{4,3,2,1,0:T(2,128)(2,1)} %bitcast.84) | data formatting | bytes 1572864 | tf_op jit(solution)/shard_map/reshape | solution.py:41
  46.5 55.6 %while.20 = (s32[]{:T(128)}, bf16[8,32,1536]{2,1,0:T(8,128)(2,1)}, bf16[8,32,1536]{2,1,0:T(8,128)(2,1)}, bf16[32,512]{1,0:T(8,128)(2,1)S(1)}, f32[512]{0:T(512)S...) while((s32[]{:T(128)}, bf16[8,32,1536]{2,1,0:T(8,128)(2,1)}, ...), condition=%wide.region_1.2_spmd, body=%wide.region_0.1_spmd.sunk | while | flops 915456000 | bytes 3936365 | solution.py:58
  46.5 3.1 %multiply_convert_fusion.6 = bf16[1536,512]{1,0:T(8,128)(2,1)} fusion(bf16[32,512]{1,0:T(8,128)(2,1)S(1)} %get-tuple-element.318, f32[512]{0:T(512)S(1)} %get-tuple-element.319, bf16[8,32,1536]{2,1,0:T(8,128)(2,1)} %get-tuple-element.317, s32[]{:T(128)S(6)} %copy.92), kind=kOutput, calls=%fused_computation.3.clone.1 | convolution fusion | flops 55050240 | bytes 1705988 | tf_op jit(solution)/shard_map/while/body/eval_jaxpr/tn,th->nh/dot_general | solution.py:45
  49.6 3.9 %fusion.55 = bf16[8,32,1536]{2,1,0:T(8,128)(2,1)} fusion(bf16[8,32,1536]{2,1,0:T(8,128)(2,1)} %get-tuple-element.307, s32[]{:T(128)S(6)} %copy.92, bf16[512,32]{0,1:T(8,128)(2,1)S(1)} %get-tuple-element.322, bf16[1536,512]{1,0:T(8,128)(2,1)} %multiply_convert_fusion.6, bf16[512,512]{1,0:T(8,128)(2,1)} %get-tuple-element.320, ...), kind=kOutput, calls=%fused_computation.6.clone.1 | convolution fusion | flops 860405760 | bytes 2230276 | tf_op jit(solution)/shard_map/while/body/eval_jaxpr/nh,ht->tn/dot_general | solution.py:54
  53.5 3.1 %multiply_convert_fusion.6 = bf16[1536,512]{1,0:T(8,128)(2,1)} fusion(bf16[32,512]{1,0:T(8,128)(2,1)S(1)} %get-tuple-element.318, f32[512]{0:T(512)S(1)} %get-tuple-element.319, bf16[8,32,1536]{2,1,0:T(8,128)(2,1)} %get-tuple-element.317, s32[]{:T(128)S(6)} %copy.92), kind=kOutput, calls=%fused_computation.3.clone.1 | convolution fusion | flops 55050240 | bytes 1705988 | tf_op jit(solution)/shard_map/while/body/eval_jaxpr/tn,th->nh/dot_general | solution.py:45
  56.5 3.9 %fusion.55 = bf16[8,32,1536]{2,1,0:T(8,128)(2,1)} fusion(bf16[8,32,1536]{2,1,0:T(8,128)(2,1)} %get-tuple-element.307, s32[]{:T(128)S(6)} %copy.92, bf16[512,32]{0,1:T(8,128)(2,1)S(1)} %get-tuple-element.322, bf16[1536,512]{1,0:T(8,128)(2,1)} %multiply_convert_fusion.6, bf16[512,512]{1,0:T(8,128)(2,1)} %get-tuple-element.320, ...), kind=kOutput, calls=%fused_computation.6.clone.1 | convolution fusion | flops 860405760 | bytes 2230276 | tf_op jit(solution)/shard_map/while/body/eval_jaxpr/nh,ht->tn/dot_general | solution.py:54
  63.5 3.9 %fusion.55 = bf16[8,32,1536]{2,1,0:T(8,128)(2,1)} fusion(bf16[8,32,1536]{2,1,0:T(8,128)(2,1)} %get-tuple-element.307, s32[]{:T(128)S(6)} %copy.92, bf16[512,32]{0,1:T(8,128)(2,1)S(1)} %get-tuple-element.322, bf16[1536,512]{1,0:T(8,128)(2,1)} %multiply_convert_fusion.6, bf16[512,512]{1,0:T(8,128)(2,1)} %get-tuple-element.320, ...), kind=kOutput, calls=%fused_computation.6.clone.1 | convolution fusion | flops 860405760 | bytes 2230276 | tf_op jit(solution)/shard_map/while/body/eval_jaxpr/nh,ht->tn/dot_general | solution.py:54
  67.3 3.1 %multiply_convert_fusion.6 = bf16[1536,512]{1,0:T(8,128)(2,1)} fusion(bf16[32,512]{1,0:T(8,128)(2,1)S(1)} %get-tuple-element.318, f32[512]{0:T(512)S(1)} %get-tuple-element.319, bf16[8,32,1536]{2,1,0:T(8,128)(2,1)} %get-tuple-element.317, s32[]{:T(128)S(6)} %copy.92), kind=kOutput, calls=%fused_computation.3.clone.1 | convolution fusion | flops 55050240 | bytes 1705988 | tf_op jit(solution)/shard_map/while/body/eval_jaxpr/tn,th->nh/dot_general | solution.py:45
  70.4 3.9 %fusion.55 = bf16[8,32,1536]{2,1,0:T(8,128)(2,1)} fusion(bf16[8,32,1536]{2,1,0:T(8,128)(2,1)} %get-tuple-element.307, s32[]{:T(128)S(6)} %copy.92, bf16[512,32]{0,1:T(8,128)(2,1)S(1)} %get-tuple-element.322, bf16[1536,512]{1,0:T(8,128)(2,1)} %multiply_convert_fusion.6, bf16[512,512]{1,0:T(8,128)(2,1)} %get-tuple-element.320, ...), kind=kOutput, calls=%fused_computation.6.clone.1 | convolution fusion | flops 860405760 | bytes 2230276 | tf_op jit(solution)/shard_map/while/body/eval_jaxpr/nh,ht->tn/dot_general | solution.py:54
  74.3 3.1 %multiply_convert_fusion.6 = bf16[1536,512]{1,0:T(8,128)(2,1)} fusion(bf16[32,512]{1,0:T(8,128)(2,1)S(1)} %get-tuple-element.318, f32[512]{0:T(512)S(1)} %get-tuple-element.319, bf16[8,32,1536]{2,1,0:T(8,128)(2,1)} %get-tuple-element.317, s32[]{:T(128)S(6)} %copy.92), kind=kOutput, calls=%fused_computation.3.clone.1 | convolution fusion | flops 55050240 | bytes 1705988 | tf_op jit(solution)/shard_map/while/body/eval_jaxpr/tn,th->nh/dot_general | solution.py:45
  77.4 3.8 %fusion.55 = bf16[8,32,1536]{2,1,0:T(8,128)(2,1)} fusion(bf16[8,32,1536]{2,1,0:T(8,128)(2,1)} %get-tuple-element.307, s32[]{:T(128)S(6)} %copy.92, bf16[512,32]{0,1:T(8,128)(2,1)S(1)} %get-tuple-element.322, bf16[1536,512]{1,0:T(8,128)(2,1)} %multiply_convert_fusion.6, bf16[512,512]{1,0:T(8,128)(2,1)} %get-tuple-element.320, ...), kind=kOutput, calls=%fused_computation.6.clone.1 | convolution fusion | flops 860405760 | bytes 2230276 | tf_op jit(solution)/shard_map/while/body/eval_jaxpr/nh,ht->tn/dot_general | solution.py:54
  81.2 3.1 %multiply_convert_fusion.6 = bf16[1536,512]{1,0:T(8,128)(2,1)} fusion(bf16[32,512]{1,0:T(8,128)(2,1)S(1)} %get-tuple-element.318, f32[512]{0:T(512)S(1)} %get-tuple-element.319, bf16[8,32,1536]{2,1,0:T(8,128)(2,1)} %get-tuple-element.317, s32[]{:T(128)S(6)} %copy.92), kind=kOutput, calls=%fused_computation.3.clone.1 | convolution fusion | flops 55050240 | bytes 1705988 | tf_op jit(solution)/shard_map/while/body/eval_jaxpr/tn,th->nh/dot_general | solution.py:45
  84.3 3.9 %fusion.55 = bf16[8,32,1536]{2,1,0:T(8,128)(2,1)} fusion(bf16[8,32,1536]{2,1,0:T(8,128)(2,1)} %get-tuple-element.307, s32[]{:T(128)S(6)} %copy.92, bf16[512,32]{0,1:T(8,128)(2,1)S(1)} %get-tuple-element.322, bf16[1536,512]{1,0:T(8,128)(2,1)} %multiply_convert_fusion.6, bf16[512,512]{1,0:T(8,128)(2,1)} %get-tuple-element.320, ...), kind=kOutput, calls=%fused_computation.6.clone.1 | convolution fusion | flops 860405760 | bytes 2230276 | tf_op jit(solution)/shard_map/while/body/eval_jaxpr/nh,ht->tn/dot_general | solution.py:54
  91.2 3.9 %fusion.55 = bf16[8,32,1536]{2,1,0:T(8,128)(2,1)} fusion(bf16[8,32,1536]{2,1,0:T(8,128)(2,1)} %get-tuple-element.307, s32[]{:T(128)S(6)} %copy.92, bf16[512,32]{0,1:T(8,128)(2,1)S(1)} %get-tuple-element.322, bf16[1536,512]{1,0:T(8,128)(2,1)} %multiply_convert_fusion.6, bf16[512,512]{1,0:T(8,128)(2,1)} %get-tuple-element.320, ...), kind=kOutput, calls=%fused_computation.6.clone.1 | convolution fusion | flops 860405760 | bytes 2230276 | tf_op jit(solution)/shard_map/while/body/eval_jaxpr/nh,ht->tn/dot_general | solution.py:54
  98.2 3.9 %fusion.55 = bf16[8,32,1536]{2,1,0:T(8,128)(2,1)} fusion(bf16[8,32,1536]{2,1,0:T(8,128)(2,1)} %get-tuple-element.307, s32[]{:T(128)S(6)} %copy.92, bf16[512,32]{0,1:T(8,128)(2,1)S(1)} %get-tuple-element.322, bf16[1536,512]{1,0:T(8,128)(2,1)} %multiply_convert_fusion.6, bf16[512,512]{1,0:T(8,128)(2,1)} %get-tuple-element.320, ...), kind=kOutput, calls=%fused_computation.6.clone.1 | convolution fusion | flops 860405760 | bytes 2230276 | tf_op jit(solution)/shard_map/while/body/eval_jaxpr/nh,ht->tn/dot_general | solution.py:54
  109.5 7.6 %all-to-all-start.1 = ((bf16[32,24,2,256]{3,1,2,0:T(8,128)(2,1)}), bf16[32,24,2,256]{3,1,2,0:T(8,128)(2,1)}, u32[]{:S(2)}, u32[]{:S(2)}) async-start(bf16[32,24,2,256]{3,1,2,0:T(8,128)(2,1)} %copy.70), calls=%async_computation.1 | async-start | bytes 1572864 | tf_op jit(solution)/shard_map/all_to_all | solution.py:98
  121.3 18.6 %all-to-all-done.1 = bf16[32,24,2,256]{3,1,2,0:T(8,128)(2,1)} async-done(((bf16[32,24,2,256]{3,1,2,0:T(8,128)(2,1)}), bf16[32,24,2,256]{3,1,2,0:T(8,128)(2,1)}, u32[]{:S(2)}, u32[]{:S(2)}) %all-to-all-start.1) | async-done | bytes 786464 | tf_op jit(solution)/shard_map/all_to_all | solution.py:98
  144.7 28.8 %all_to_all.48 = bf16[2,24,32,256]{3,1,0,2:T(8,128)(2,1)S(1)} all-to-all(bf16[2,24,32,256]{3,1,0,2:T(8,128)(2,1)S(1)} %copy.73), channel_id=1, replica_groups=mesh['tile'=16,'tracer'=16] {'tracer'}, dimensions={2} | all-to-all | bytes 1572864 | tf_op jit(solution)/shard_map/all_to_all | solution.py:91
  175.0 43.2 %while.21 = (s32[]{:T(128)}, bf16[8,32,1536]{2,1,0:T(8,128)(2,1)S(1)}, bf16[8,32,1536]{2,1,0:T(8,128)(2,1)S(1)}, bf16[32,512]{1,0:T(8,128)(2,1)S(1)}, f32[512]{0...) while((s32[]{:T(128)}, ...), condition=%wide.region_3.4_spmd, body=%wide.region_2.3_spmd.sunk | while | flops 915456000 | bytes 3936365 | solution.py:58
  177.2 3.2 %fusion.61 = bf16[8,32,1536]{2,1,0:T(8,128)(2,1)S(1)} fusion(bf16[8,32,1536]{2,1,0:T(8,128)(2,1)S(1)} %get-tuple-element.334, s32[]{:T(128)S(6)} %copy.98, bf16[512,32]{0,1:T(8,128)(2,1)S(1)} %get-tuple-element.349, bf16[1536,512]{1,0:T(8,128)(2,1)} %multiply_convert_fusion.7, bf16[512,512]{1,0:T(8,128)(2,1)} %get-tuple-element.347, ...), kind=kOutput, calls=%fused_computation.17.clone.1 | convolution fusion | flops 860405760 | bytes 2230276 | tf_op jit(solution)/shard_map/while/body/eval_jaxpr/nh,ht->tn/dot_general | solution.py:54
  182.6 3.2 %fusion.61 = bf16[8,32,1536]{2,1,0:T(8,128)(2,1)S(1)} fusion(bf16[8,32,1536]{2,1,0:T(8,128)(2,1)S(1)} %get-tuple-element.334, s32[]{:T(128)S(6)} %copy.98, bf16[512,32]{0,1:T(8,128)(2,1)S(1)} %get-tuple-element.349, bf16[1536,512]{1,0:T(8,128)(2,1)} %multiply_convert_fusion.7, bf16[512,512]{1,0:T(8,128)(2,1)} %get-tuple-element.347, ...), kind=kOutput, calls=%fused_computation.17.clone.1 | convolution fusion | flops 860405760 | bytes 2230276 | tf_op jit(solution)/shard_map/while/body/eval_jaxpr/nh,ht->tn/dot_general | solution.py:54
  188.0 3.2 %fusion.61 = bf16[8,32,1536]{2,1,0:T(8,128)(2,1)S(1)} fusion(bf16[8,32,1536]{2,1,0:T(8,128)(2,1)S(1)} %get-tuple-element.334, s32[]{:T(128)S(6)} %copy.98, bf16[512,32]{0,1:T(8,128)(2,1)S(1)} %get-tuple-element.349, bf16[1536,512]{1,0:T(8,128)(2,1)} %multiply_convert_fusion.7, bf16[512,512]{1,0:T(8,128)(2,1)} %get-tuple-element.347, ...), kind=kOutput, calls=%fused_computation.17.clone.1 | convolution fusion | flops 860405760 | bytes 2230276 | tf_op jit(solution)/shard_map/while/body/eval_jaxpr/nh,ht->tn/dot_general | solution.py:54
  193.4 3.2 %fusion.61 = bf16[8,32,1536]{2,1,0:T(8,128)(2,1)S(1)} fusion(bf16[8,32,1536]{2,1,0:T(8,128)(2,1)S(1)} %get-tuple-element.334, s32[]{:T(128)S(6)} %copy.98, bf16[512,32]{0,1:T(8,128)(2,1)S(1)} %get-tuple-element.349, bf16[1536,512]{1,0:T(8,128)(2,1)} %multiply_convert_fusion.7, bf16[512,512]{1,0:T(8,128)(2,1)} %get-tuple-element.347, ...), kind=kOutput, calls=%fused_computation.17.clone.1 | convolution fusion | flops 860405760 | bytes 2230276 | tf_op jit(solution)/shard_map/while/body/eval_jaxpr/nh,ht->tn/dot_general | solution.py:54
  198.8 3.2 %fusion.61 = bf16[8,32,1536]{2,1,0:T(8,128)(2,1)S(1)} fusion(bf16[8,32,1536]{2,1,0:T(8,128)(2,1)S(1)} %get-tuple-element.334, s32[]{:T(128)S(6)} %copy.98, bf16[512,32]{0,1:T(8,128)(2,1)S(1)} %get-tuple-element.349, bf16[1536,512]{1,0:T(8,128)(2,1)} %multiply_convert_fusion.7, bf16[512,512]{1,0:T(8,128)(2,1)} %get-tuple-element.347, ...), kind=kOutput, calls=%fused_computation.17.clone.1 | convolution fusion | flops 860405760 | bytes 2230276 | tf_op jit(solution)/shard_map/while/body/eval_jaxpr/nh,ht->tn/dot_general | solution.py:54
  204.2 3.2 %fusion.61 = bf16[8,32,1536]{2,1,0:T(8,128)(2,1)S(1)} fusion(bf16[8,32,1536]{2,1,0:T(8,128)(2,1)S(1)} %get-tuple-element.334, s32[]{:T(128)S(6)} %copy.98, bf16[512,32]{0,1:T(8,128)(2,1)S(1)} %get-tuple-element.349, bf16[1536,512]{1,0:T(8,128)(2,1)} %multiply_convert_fusion.7, bf16[512,512]{1,0:T(8,128)(2,1)} %get-tuple-element.347, ...), kind=kOutput, calls=%fused_computation.17.clone.1 | convolution fusion | flops 860405760 | bytes 2230276 | tf_op jit(solution)/shard_map/while/body/eval_jaxpr/nh,ht->tn/dot_general | solution.py:54
  209.6 3.2 %fusion.61 = bf16[8,32,1536]{2,1,0:T(8,128)(2,1)S(1)} fusion(bf16[8,32,1536]{2,1,0:T(8,128)(2,1)S(1)} %get-tuple-element.334, s32[]{:T(128)S(6)} %copy.98, bf16[512,32]{0,1:T(8,128)(2,1)S(1)} %get-tuple-element.349, bf16[1536,512]{1,0:T(8,128)(2,1)} %multiply_convert_fusion.7, bf16[512,512]{1,0:T(8,128)(2,1)} %get-tuple-element.347, ...), kind=kOutput, calls=%fused_computation.17.clone.1 | convolution fusion | flops 860405760 | bytes 2230276 | tf_op jit(solution)/shard_map/while/body/eval_jaxpr/nh,ht->tn/dot_general | solution.py:54
  215.0 3.2 %fusion.61 = bf16[8,32,1536]{2,1,0:T(8,128)(2,1)S(1)} fusion(bf16[8,32,1536]{2,1,0:T(8,128)(2,1)S(1)} %get-tuple-element.334, s32[]{:T(128)S(6)} %copy.98, bf16[512,32]{0,1:T(8,128)(2,1)S(1)} %get-tuple-element.349, bf16[1536,512]{1,0:T(8,128)(2,1)} %multiply_convert_fusion.7, bf16[512,512]{1,0:T(8,128)(2,1)} %get-tuple-element.347, ...), kind=kOutput, calls=%fused_computation.17.clone.1 | convolution fusion | flops 860405760 | bytes 2230276 | tf_op jit(solution)/shard_map/while/body/eval_jaxpr/nh,ht->tn/dot_general | solution.py:54
  222.0 4.9 %all-to-all-start.3 = ((bf16[32,24,2,256]{3,1,2,0:T(8,128)(2,1)}), bf16[32,24,2,256]{3,1,2,0:T(8,128)(2,1)}, u32[]{:S(2)}, u32[]{:S(2)}) async-start(bf16[32,24,2,256]{3,1,2,0:T(8,128)(2,1)} %copy.77), calls=%async_computation.3 | async-start | bytes 1572864 | tf_op jit(solution)/shard_map/all_to_all | solution.py:98
  232.0 3.8 %subtract_multiply_fusion = f32[2,24,32,257]{3,1,2,0:T(8,128)} fusion(f32[2,24,32,256]{3,1,2,0:T(8,128)S(1)} %get-tuple-element.188, f32[24,32,257]{2,0,1:T(8,128)S(1)} %copy-done.9, f32[24,32,257]{2,0,1:T(8,128)} %copy-done.10, f32[24,32,257]{2,0,1:T(8,128)} %copy-done.11), kind=kLoop, calls=%fused_computation.26 | loop fusion | flops 2763264 | bytes 5520384 | tf_op jit(solution)/shard_map/mul | solution.py:34
  239.1 10.1 %all-to-all-done.3 = bf16[32,24,2,256]{3,1,2,0:T(8,128)(2,1)} async-done(((bf16[32,24,2,256]{3,1,2,0:T(8,128)(2,1)}), bf16[32,24,2,256]{3,1,2,0:T(8,128)(2,1)}, u32[]{:S(2)}, u32[]{:S(2)}) %all-to-all-start.3) | async-done | bytes 786464 | tf_op jit(solution)/shard_map/all_to_all | solution.py:98
  (124 shorter events, 90.9 us)
Async XLA Ops:
  2.2 16.8 %copy-start.22 = (s32[32,256]{1,0:T(8,128)S(1)}, s32[32,256]{1,0:T(8,128)}, u32[]{:S(2)}) copy-start(s32[32,256]{1,0:T(8,128)} %param.17) | copy-start | bytes 98308
  2.3 16.8 %copy-start.21 = (s32[32,256]{1,0:T(8,128)S(1)}, s32[32,256]{1,0:T(8,128)}, u32[]{:S(2)}) copy-start(s32[32,256]{1,0:T(8,128)} %param.18) | copy-start | bytes 98308
  3.3 34.0 %all-to-all-start = ((bf16[2,24,32,256]{3,1,0,2:T(8,128)(2,1)}), bf16[2,24,32,256]{3,1,0,2:T(8,128)(2,1)}, u32[]{:S(2)}, u32[]{:S(2)}) async-start(bf16[2,24,32,256]{3,1,0,2:T(8,128)(2,1)} %copy.66), calls=%async_computation | async-start | bytes 1572864 | tf_op jit(solution)/shard_map/all_to_all | solution.py:91
  14.5 11.0 %copy-start = (f32[2,24,32,256]{3,2,1,0:T(8,128)S(1)}, f32[2,24,32,256]{3,2,1,0:T(8,128)}, u32[]{:S(2)}) copy-start(f32[2,24,32,256]{3,2,1,0:T(8,128)} %param.14) | copy-start | bytes 4718596
  14.6 104.2 %collective-permute-start.3 = (bf16[2,24,1,256]{3,1,2,0:T(8,128)(2,1)S(1)}, bf16[2,24,1,256]{3,1,2,0:T(8,128)(2,1)S(1)}, u32[]{:S(2)}, u32[]{:S(2)}) collective-permute-start(bf16[2,24,1,256]{3,1,2,0:T(8,128)(2,1)S(1)} %get-tuple-element.196), channel_id=1, source_target_pairs={{16,0},{32,16},{48,32},{64,48},{80,64},{96,80},{112,96},{128,112},... | collective-permute-start | bytes 73736 | tf_op jit(solution)/shard_map/ppermute | solution.py:23
  16.6 102.1 %collective-permute-start.2 = (bf16[2,24,1,256]{3,1,2,0:T(8,128)(2,1)S(1)}, bf16[2,24,1,256]{3,1,2,0:T(8,128)(2,1)S(1)}, u32[]{:S(2)}, u32[]{:S(2)}) collective-permute-start(bf16[2,24,1,256]{3,1,2,0:T(8,128)(2,1)S(1)} %get-tuple-element.195), channel_id=1, source_target_pairs={{0,16},{16,32},{32,48},{48,64},{64,80},{80,96},{96,112},{112,128},... | collective-permute-start | bytes 73736 | tf_op jit(solution)/shard_map/ppermute | solution.py:22
  20.5 96.7 %collective-permute-start.1 = (bf16[2,24,1,256]{3,2,1,0:T(2,128)(2,1)S(1)}, bf16[2,24,1,256]{3,2,1,0:T(2,128)(2,1)S(1)}, u32[]{:S(2)}, u32[]{:S(2)}) collective-permute-start(bf16[2,24,1,256]{3,2,1,0:T(2,128)(2,1)S(1)} %get-tuple-element.194), channel_id=1, source_target_pairs={{16,0},{32,16},{48,32},{64,48},{80,64},{96,80},{112,96},{128,112},... | collective-permute-start | bytes 73736 | tf_op jit(solution)/shard_map/ppermute | solution.py:23
  23.6 93.5 %collective-permute-start = (bf16[2,24,1,256]{3,2,1,0:T(2,128)(2,1)S(1)}, bf16[2,24,1,256]{3,2,1,0:T(2,128)(2,1)S(1)}, u32[]{:S(2)}, u32[]{:S(2)}) collective-permute-start(bf16[2,24,1,256]{3,2,1,0:T(2,128)(2,1)S(1)} %get-tuple-element.193), channel_id=1, source_target_pairs={{0,16},{16,32},{32,48},{48,64},{64,80},{80,96},{96,112},{112,128},... | collective-permute-start | bytes 73736 | tf_op jit(solution)/shard_map/ppermute | solution.py:22
  29.9 2.2 copy-start.8
  30.6 1.5 copy-start.10
  30.6 2.5 copy-start.20
  32.1 1.0 copy-start.11
  40.0 6.5 %copy-start.23 = (bf16[32,512]{1,0:T(8,128)(2,1)S(1)}, bf16[32,512]{1,0:T(8,128)(2,1)}, u32[]{:S(2)}) copy-start(bf16[32,512]{1,0:T(8,128)(2,1)} %param.19) | copy-start | bytes 98308
  40.0 6.5 %copy-start.24 = (bf16[512,32]{0,1:T(8,128)(2,1)S(1)}, bf16[512,32]{0,1:T(8,128)(2,1)}, u32[]{:S(2)}) copy-start(bf16[512,32]{0,1:T(8,128)(2,1)} %param.23) | copy-start | bytes 98308
  40.0 6.5 %copy-start.25 = (f32[512]{0:T(512)S(1)}, f32[512]{0:T(512)}, u32[]{:S(2)}) copy-start(f32[512]{0:T(512)} %param.20) | copy-start | bytes 6148
  40.0 6.5 %copy-start.26 = (f32[512]{0:T(512)S(1)}, f32[512]{0:T(512)}, u32[]{:S(2)}) copy-start(f32[512]{0:T(512)} %param.22) | copy-start | bytes 6148
  109.5 30.3 %all-to-all-start.1 = ((bf16[32,24,2,256]{3,1,2,0:T(8,128)(2,1)}), bf16[32,24,2,256]{3,1,2,0:T(8,128)(2,1)}, u32[]{:S(2)}, u32[]{:S(2)}) async-start(bf16[32,24,2,256]{3,1,2,0:T(8,128)(2,1)} %copy.70), calls=%async_computation.1 | async-start | bytes 1572864 | tf_op jit(solution)/shard_map/all_to_all | solution.py:98
  139.9 1.9 copy-start.3
  141.4 1.5 copy-start.2
  141.4 1.7 copy-start.6
  144.6 29.6 %copy-start.12 = (bf16[2,24,32,256]{3,1,2,0:T(8,128)(2,1)}, bf16[2,24,32,256]{3,1,2,0:T(8,128)(2,1)S(1)}, u32[]{:S(2)}) copy-start(bf16[2,24,32,256]{3,1,2,0:T(8,128)(2,1)S(1)} %get-tuple-element.187) | copy-start | bytes 2359300
  219.7 12.2 %copy-start.9 = (f32[24,32,257]{2,0,1:T(8,128)S(1)}, f32[24,32,257]{2,0,1:T(8,128)}, u32[]{:S(2)}) copy-start(f32[24,32,257]{2,0,1:T(8,128)} %copy-done.8) | copy-start | bytes 2368516
  222.0 27.3 %all-to-all-start.3 = ((bf16[32,24,2,256]{3,1,2,0:T(8,128)(2,1)}), bf16[32,24,2,256]{3,1,2,0:T(8,128)(2,1)}, u32[]{:S(2)}, u32[]{:S(2)}) async-start(bf16[32,24,2,256]{3,1,2,0:T(8,128)(2,1)} %copy.77), calls=%async_computation.3 | async-start | bytes 1572864 | tf_op jit(solution)/shard_map/all_to_all | solution.py:98
  227.6 8.1 %collective-permute-start.5 = (bf16[2,24,1,256]{3,1,2,0:T(8,128)(2,1)S(1)}, bf16[2,24,1,256]{3,1,2,0:T(8,128)(2,1)S(1)}, u32[]{:S(2)}, u32[]{:S(2)}) collective-permute-start(bf16[2,24,1,256]{3,1,2,0:T(8,128)(2,1)S(1)} %get-tuple-element.192), channel_id=1, source_target_pairs={{16,0},{32,16},{48,32},{64,48},{80,64},{96,80},{112,96},{128,112},... | collective-permute-start | bytes 73736 | tf_op jit(solution)/shard_map/ppermute | solution.py:23
  229.5 6.2 %collective-permute-start.4 = (bf16[2,24,1,256]{3,1,2,0:T(8,128)(2,1)S(1)}, bf16[2,24,1,256]{3,1,2,0:T(8,128)(2,1)S(1)}, u32[]{:S(2)}, u32[]{:S(2)}) collective-permute-start(bf16[2,24,1,256]{3,1,2,0:T(8,128)(2,1)S(1)} %get-tuple-element.191), channel_id=1, source_target_pairs={{0,16},{16,32},{32,48},{48,64},{64,80},{80,96},{96,112},{112,128},... | collective-permute-start | bytes 73736 | tf_op jit(solution)/shard_map/ppermute | solution.py:22
  232.0 3.8 %copy-start.13 = (bf16[2,24,32,256]{3,1,2,0:T(8,128)(2,1)S(1)}, bf16[2,24,32,256]{3,1,2,0:T(8,128)(2,1)}, u32[]{:S(2)}) copy-start(bf16[2,24,32,256]{3,1,2,0:T(8,128)(2,1)} %copy-done.12) | copy-start | bytes 2359300
  235.8 1.1 copy-start.15
  235.8 1.4 copy-start.17
  235.8 1.6 copy-start.19
  249.2 1.9 copy-start.4
  250.7 1.5 copy-start.1
  250.7 1.7 copy-start.7
  (4 other events, 3.7 us)
where the time goes:
time: 258 us; the launch traced here: 255 us
  matrix products  98.7 us (38%)
  local copies, waits for them, and re-layouts  39.6 us (15%)
  starting transfers between devices  37.6 us (15%)
  waiting for transfers between devices  30.7 us (12%)
  blocking collectives  28.8 us (11%)
  other arithmetic  18.7 us (7%)
    dot_general x16, matrix products, one_block(): jnp.einsum('nh,ht->tn', second_hidden, out_weight, preferred_element_type...  56.4 us
    dot_general x16, matrix products, one_block(): jnp.einsum('tn,th->nh', cell_block, in_weight, preferred_element_type=jnp...  42.3 us
    all_to_all x1, blocking collectives, body(): lax.all_to_all(inputs, 'tracer', split_axis=2, concat_axis=0, tiled=True)  28.8 us
    all_to_all x2, waiting for transfers between devices, body(): lax.all_to_all(local_sources, 'tracer', split_axis=0, concat_axis=2, tile...  28.7 us
    all_to_all x2, starting transfers between devices, body(): lax.all_to_all(local_sources, 'tracer', split_axis=0, concat_axis=2, tile...  12.5 us
    unnamed x56, local copies, waits for them, and re-layouts  11.7 us
    all_to_all x1, starting transfers between devices, body(): lax.all_to_all(inputs, 'tracer', split_axis=2, concat_axis=0, tiled=True)  11.2 us
    mul x4, other arithmetic, face_flux(): return opened * (moved - diffusion * (ahead_cells - behind_cells))  9.23 us
  transfers between devices with their start and end apart: 9, of which 3 were waited for; matrix products, arithmetic and copies ran while one was open for 36% of the time, Pallas kernels for 0%

commit v1 on v0

v1 whole, which is shorter than its diff:
```python
import functools

import jax
import jax.numpy as jnp
from jax import lax
from jax.experimental import pallas as pl
from jax.experimental.pallas import tpu as pltpu
from jax.sharding import PartitionSpec as P

STEPS = 2
diffusion = 0.2
time_step = 0.2
GROUP = 4

BF16 = jnp.bfloat16
F32 = jnp.float32


def silu_of_half(half):
    return (half + half * jnp.tanh(half)).astype(BF16)


def network(cells, in_weight, mid_weight, mid_bias, out_weight):
    lanes = cells.shape[1]
    cells = jnp.concatenate([cells, jnp.ones((16, lanes), BF16)], axis=0)
    hidden = silu_of_half(jnp.dot(in_weight, cells, preferred_element_type=F32))
    hidden = jnp.dot(mid_weight, hidden, preferred_element_type=F32)
    hidden = silu_of_half(hidden + jnp.concatenate([mid_bias] * (lanes // 128), axis=1))
    return jnp.dot(out_weight, hidden, preferred_element_type=F32)


def turn_kernel(rows, x_ref, turned_ref, first_ref, last_ref, scratch):
    kinds, levels = x_ref.shape[:2]
    for level in range(levels):
        for part in range(scratch.shape[0]):
            block = x_ref[:, level, :, part * 128 : (part + 1) * 128]
            scratch[part] = block.astype(F32).reshape(kinds * rows, 128)
        for row in range(rows):
            picked = [scratch[part, pl.ds(row, kinds, stride=rows), :] for part in range(scratch.shape[0])]
            piece = jnp.concatenate(picked, axis=1).astype(BF16)
            turned_ref[level * rows + row] = piece
            if row < 2:
                first_ref[level * 2 + row] = piece
            if row >= rows - 2:
                last_ref[level * 2 + row - rows + 2] = piece


def source_kernel(cells_ref, in_ref, mid_ref, bias_ref, out_ref, sources_ref):
    def body(i, _):
        cells = jnp.concatenate([cells_ref[i * GROUP + k] for k in range(GROUP)], axis=1)
        result = network(cells, in_ref[...], mid_ref[...], bias_ref[...], out_ref[...])
        width = cells_ref.shape[2]
        for k in range(GROUP):
            sources_ref[i * GROUP + k] = result[:, k * width : (k + 1) * width].astype(BF16)
        return 0

    lax.fori_loop(0, cells_ref.shape[0] // GROUP, body, 0)


def advance(here, above, below, sources, factors):
    width = here.shape[1]
    west = pltpu.roll(here, 1, 1)
    east = pltpu.roll(here, width - 1, 1)
    result = factors[0:1] * here + factors[1:2] * above + factors[2:3] * below
    return result + factors[3:4] * west + factors[4:5] * east + factors[5:6] * sources


def step_kernel(
    rows,
    cells_ref,
    sources_ref,
    top_ref,
    bottom_ref,
    factors_ref,
    in_ref,
    mid_ref,
    bias_ref,
    out_ref,
    change_ref,
    wide,
    wide_sources,
    middle,
    scratch,
):
    levels = cells_ref.shape[0] // rows
    width = cells_ref.shape[2]
    ahead, wider = rows + 2, rows + 4
    edge = []
    for level in range(levels):
        edge += [top_ref[level * 2 + 1], bottom_ref[level * 2]]
    result = network(
        jnp.concatenate(edge, axis=1), in_ref[...], mid_ref[...], bias_ref[...], out_ref[...]
    ).astype(BF16).astype(F32)
    for level in range(levels):
        at = 2 * level * width
        wide_sources[level * ahead] = result[:, at : at + width]
        wide_sources[level * ahead + ahead - 1] = result[:, at + width : at + 2 * width]
        for k in range(2):
            wide[level * wider + k] = top_ref[level * 2 + k].astype(F32)
            wide[level * wider + rows + 2 + k] = bottom_ref[level * 2 + k].astype(F32)

        def widen(row, _):
            wide[level * wider + 2 + row] = cells_ref[level * rows + row].astype(F32)
            wide_sources[level * ahead + 1 + row] = sources_ref[level * rows + row].astype(F32)
            return 0

        lax.fori_loop(0, rows, widen, 0, unroll=4)

        def first_step(row, _):
            at = level * wider + row
            middle[level * ahead + row] = advance(
                wide[at + 1],
                wide[at],
                wide[at + 2],
                wide_sources[level * ahead + row],
                factors_ref[level * ahead + row],
            )
            return 0

        lax.fori_loop(0, ahead, first_step, 0, unroll=3)

    turns = rows // GROUP

    def second_step(i, _):
        level = i // turns
        row = (i - level * turns) * GROUP
        at = level * ahead + row + 1
        held = [middle[at - 1 + k] for k in range(GROUP + 2)]
        cells = jnp.concatenate([held[k + 1].astype(BF16) for k in range(GROUP)], axis=1)
        result = network(cells, in_ref[...], mid_ref[...], bias_ref[...], out_ref[...])
        for k in range(GROUP):
            factors = factors_ref[at + k]
            value = advance(
                held[k + 1],
                held[k],
                held[k + 2],
                result[:, k * width : (k + 1) * width].astype(BF16).astype(F32),
                factors,
            )
            value = value - factors[6:7] * wide[level * wider + row + k + 2]
            kinds = value.shape[0]
            for part in range(scratch.shape[0]):
                scratch[part, pl.ds(level * rows * kinds + row + k, kinds, stride=rows), :] = value[
                    :, part * 128 : (part + 1) * 128
                ]
        return 0

    lax.fori_loop(0, levels * turns, second_step, 0)
    kinds = change_ref.shape[0]
    for level in range(levels):
        for part in range(scratch.shape[0]):
            block = scratch[part, level * rows * kinds : (level + 1) * rows * kinds, :]
            change_ref[:, level, :, part * 128 : (part + 1) * 128] = block.reshape(kinds, rows, 128).astype(BF16)


def kernel_call(kernel, outs, scratch, flops, name):
    return pl.pallas_call(
        kernel,
        out_shape=outs,
        scratch_shapes=scratch,
        cost_estimate=pl.CostEstimate(flops=flops, bytes_accessed=4_000_000, transcendentals=0),
        compiler_params=pltpu.CompilerParams(vmem_limit_bytes=48 * 2**20),
        name=name,
    )


def factors_of(east, north, depth, first_level, levels):
    level = first_level + jnp.arange(levels, dtype=jnp.int32)[:, None, None]
    wet = (level.astype(F32) < depth[None]).astype(F32)
    opened = time_step * wet[:, :-1] * wet[:, 1:]
    plus = opened * (jnp.maximum(east[:, :-1], 0.0) + diffusion)
    minus = opened * (jnp.minimum(east[:, :-1], 0.0) - diffusion)
    inner = wet[:, 1:-1]
    flow = jnp.pad(north[:, 1:-1], ((0, 0), (0, 0), (1, 0)))
    sides = jnp.pad(inner, ((0, 0), (0, 0), (1, 1)))
    opened = time_step * sides[..., :-1] * sides[..., 1:]
    right = opened * (jnp.maximum(flow, 0.0) + diffusion)
    left = opened * (jnp.minimum(flow, 0.0) - diffusion)
    own = inner + (minus[:, :-1] - plus[:, 1:]) + (left[..., :-1] - right[..., 1:])
    return jnp.stack(
        [
            own,
            plus[:, :-1],
            -minus[:, 1:],
            right[..., :-1],
            -left[..., 1:],
            time_step * inner,
            inner,
            jnp.zeros_like(inner),
        ],
        axis=2,
    )


def body(
    tracers,
    east_speed,
    north_speed,
    land_mask,
    bottom_level,
    in_weight,
    in_bias,
    mid_weight,
    mid_bias,
    out_weight,
):
    kinds, levels, length, columns = tracers.shape
    tiles, group = lax.axis_size("tile"), lax.axis_size("tracer")
    halves = 2
    stacks = group // halves
    depth_each, rows = levels // stacks, length // halves
    own = lax.axis_index("tracer")
    half, stack = own // stacks, own % stacks
    all_kinds = kinds * group
    pieces = depth_each * rows

    sent = tracers.astype(BF16).reshape(kinds, stacks, depth_each, halves, rows, columns)
    sent = sent.transpose(3, 1, 0, 2, 4, 5).reshape(group, kinds, depth_each, rows, columns)
    cells = lax.all_to_all(sent, "tracer", split_axis=0, concat_axis=0, tiled=True)
    cells = cells.reshape(all_kinds, depth_each, rows, columns)

    depth = jnp.where(land_mask == 1, bottom_level, 0).astype(F32)
    first_level = stack * depth_each
    east = lax.dynamic_slice_in_dim(east_speed, first_level, depth_each, 0)
    north = lax.dynamic_slice_in_dim(north_speed, first_level, depth_each, 0)
    geometry = jnp.concatenate([east, north, depth[None]], axis=0)

    def at(tile, part, place):
        return tile * group + part * stacks + place

    across, back, within = [], [], []
    for place in range(stacks):
        for tile in range(tiles):
            within.append((at(tile, 0, place), at(tile, 1, place)))
            if tile + 1 < tiles:
                across.append((at(tile, 1, place), at(tile + 1, 0, place)))
    back = [(j, i) for i, j in across]
    axes = ("tile", "tracer")
    edge = lax.dynamic_slice_in_dim(geometry, half * (length - 2), 2, 1)
    arrived = lax.ppermute(edge, axes, across + back)
    geometry = jnp.where(
        half == 0,
        jnp.concatenate([arrived, geometry[:, : rows + 2]], axis=1),
        jnp.concatenate([geometry[:, rows - 2 :], arrived], axis=1),
    )
    factors = factors_of(
        geometry[:depth_each],
        geometry[depth_each : 2 * depth_each],
        geometry[2 * depth_each],
        first_level,
        depth_each,
    ).reshape(depth_each * (rows + 2), 8, columns)

    def parts(value):
        high = value.astype(BF16)
        low = (value - high.astype(F32)).astype(BF16)
        return [high, low, (value - high.astype(F32) - low.astype(F32)).astype(BF16)]

    in_parts = jnp.stack(parts(0.5 * in_bias) + [jnp.zeros(in_bias.shape, BF16)] * 13, axis=1)
    weights = (
        jnp.concatenate([(0.5 * in_weight.astype(F32)).astype(BF16).T, in_parts], axis=1),
        (0.5 * mid_weight.astype(F32)).astype(BF16).T,
        jnp.broadcast_to(0.5 * mid_bias[:, None], mid_bias.shape + (128,)),
        out_weight.T,
    )

    hidden = in_weight.shape[1]
    per_piece = 2 * columns * hidden * (hidden + 2 * all_kinds)
    turned, first, last = kernel_call(
        functools.partial(turn_kernel, rows),
        [
            jax.ShapeDtypeStruct((pieces, all_kinds, columns), BF16),
            jax.ShapeDtypeStruct((depth_each * 2, all_kinds, columns), BF16),
            jax.ShapeDtypeStruct((depth_each * 2, all_kinds, columns), BF16),
        ],
        [pltpu.VMEM((columns // 128, all_kinds * rows, 128), F32)],
        1_000_000,
        "turn",
    )(cells)
    top = lax.ppermute(last, axes, within + across)
    bottom = lax.ppermute(first, axes, [(j, i) for i, j in within] + back)
    sources = kernel_call(
        source_kernel,
        jax.ShapeDtypeStruct(turned.shape, BF16),
        [],
        pieces * per_piece,
        "sources",
    )(turned, *weights)
    change = kernel_call(
        functools.partial(step_kernel, rows),
        jax.ShapeDtypeStruct(cells.shape, BF16),
        [
            pltpu.VMEM((depth_each * (rows + 4), all_kinds, columns), F32),
            pltpu.VMEM((depth_each * (rows + 2), all_kinds, columns), F32),
            pltpu.VMEM((depth_each * (rows + 2), all_kinds, columns), F32),
            pltpu.VMEM((columns // 128, depth_each * rows * all_kinds, 128), F32),
        ],
        pieces * per_piece,
        "steps",
    )(turned, sources, top, bottom, factors, *weights)

    change = change.reshape(group, kinds, depth_each, rows, columns)
    change = lax.all_to_all(change, "tracer", split_axis=0, concat_axis=0, tiled=True)
    change = change.reshape(halves, stacks, kinds, depth_each, rows, columns)
    change = change.transpose(2, 1, 3, 0, 4, 5).reshape(kinds, levels, length, columns)
    level = jnp.arange(levels, dtype=jnp.int32)[:, None, None]
    wet = (level.astype(F32) < depth[None]).astype(F32)
    return wet[None] * (tracers + change.astype(F32))


def solution(mesh):
    return jax.shard_map(
        body,
        mesh=mesh,
        in_specs=(
            P("tracer", None, "tile", None),
            P(None, "tile", None),
            P(None, "tile", None),
            P("tile", None),
            P("tile", None),
            P(),
            P(),
            P(),
            P(),
            P(),
        ),
        out_specs=P("tracer", None, "tile", None),
        check_vma=False,
    )
```

time: 258 us -> 112 us (0.43); the launches traced: 255 us -> 111 us
  matrix products: 98.7 us -> 0 us
  local copies, waits for them, and re-layouts: 39.6 us -> 4.17 us
  Pallas kernels: 0 us -> 33.5 us
  blocking collectives: 28.8 us -> 0 us
  other arithmetic: 18.7 us -> 4.58 us
  waiting for transfers between devices: 30.7 us -> 42.2 us
  starting transfers between devices: 37.6 us -> 26.4 us
    dot_general x32 -> x0, matrix products: 98.7 us -> none  [the longest x16 56.4 us: one_block(): jnp.einsum('nh,ht->tn', second_hidden, out_weight, preferred_element_type...]
    pallas_call x0 -> x3, Pallas kernels: none -> 33.5 us  [the longest x1 19.3 us: body(): kernel_call(functools.partial(step_kernel, rows), jax.ShapeDtypeStruct(ce...]
    all_to_all x1 -> x0, blocking collectives: 28.8 us -> none  [body(): lax.all_to_all(inputs, 'tracer', split_axis=2, concat_axis=0, tiled=True)]
    reshape x6 -> x0, local copies, waits for them, and re-layouts: 12 us -> none  [the longest x4 8.32 us: network(): return result.reshape(result.shape[0], depth, rows, cols)]
    all_to_all x3 -> x2, waiting for transfers between devices: 30.7 us -> 42.2 us  [the longest x1 22 us: body(): lax.all_to_all(change, 'tracer', split_axis=0, concat_axis=0, tiled=True)]
    unnamed x56 -> x13, local copies, waits for them, and re-layouts: 11.7 us -> 0.51 us
    all_to_all x3 -> x2, starting transfers between devices: 23.7 us -> 14 us  [the longest x1 8.61 us: body(): lax.all_to_all(sent, 'tracer', split_axis=0, concat_axis=0, tiled=True)]
    mul x8 -> x4, other arithmetic: 10.5 us -> 1.79 us  [the longest x1 1.6 us: body(): return wet[None] * (tracers + change.astype(F32))]
  transfers between devices with their start and end apart: 9 -> 5, of which waited for: 3 -> 2; matrix products, arithmetic and copies ran while one was open for 36% -> 4% of each run, Pallas kernels for 0% -> 12%
where the time goes in v1:
time: 112 us; the launch traced here: 111 us
  waiting for transfers between devices  42.2 us (38%)
  Pallas kernels  33.5 us (30%)
  starting transfers between devices  26.4 us (24%)
  other arithmetic  4.58 us (4%)
  local copies, waits for them, and re-layouts  4.17 us (4%)
    all_to_all x1, waiting for transfers between devices, body(): lax.all_to_all(change, 'tracer', split_axis=0, concat_axis=0, tiled=True)  22 us
    all_to_all x1, waiting for transfers between devices, body(): lax.all_to_all(sent, 'tracer', split_axis=0, concat_axis=0, tiled=True)  20.2 us
    pallas_call x1, Pallas kernels, body(): kernel_call(functools.partial(step_kernel, rows), jax.ShapeDtypeStruct(ce...  19.3 us
    pallas_call x1, Pallas kernels, body(): kernel_call(source_kernel, jax.ShapeDtypeStruct(turned.shape, BF16), [],...  13.7 us
    all_to_all x1, starting transfers between devices, body(): lax.all_to_all(sent, 'tracer', split_axis=0, concat_axis=0, tiled=True)  8.61 us
    all_to_all x1, starting transfers between devices, body(): lax.all_to_all(change, 'tracer', split_axis=0, concat_axis=0, tiled=True)  5.35 us
    ppermute x1, starting transfers between devices, body(): bottom = lax.ppermute(first, axes, [(j, i) for i, j in within] + back)  5.3 us
    ppermute x1, starting transfers between devices, body(): arrived = lax.ppermute(edge, axes, across + back)  4.51 us
  transfers between devices with their start and end apart: 5, of which 2 were waited for; matrix products, arithmetic and copies ran while one was open for 4% of the time, Pallas kernels for 12%

profile of v1, /device:TPU:2, one launch (start us, length us, event | category | flops | bytes accessed | tf_op | source)
XLA Modules:
  0.0 111.3 jit_solution(1110200075419437344)
XLA Ops:
  0.0 0.8 select_convert_fusion
  0.8 1.0 constant_dynamic-slice_fusion.1
  1.8 4.5 %collective-permute-start.2 = (f32[7,2,256]{2,1,0:T(2,128)S(1)}, f32[7,2,256]{2,1,0:T(2,128)S(1)}, u32[]{:S(2)}, u32[]{:S(2)}) collective-permute-start(f32[7,2,256]{2,1,0:T(2,128)S(1)} %constant_dynamic-slice_fusion), channel_id=1, source_target_pairs={{8,16},{24,32},{40,48},{56,64},{72,80},{88,96},{104,112},{120,128}... | collective-permute-start | bytes 43016 | tf_op jit(solution)/shard_map/ppermute | solution.py:240
  6.3 1.5 %convert_element_type.79 = bf16[2,24,32,256]{3,2,1,0:T(8,128)(2,1)S(1)} convert(f32[2,24,32,256]{3,2,1,0:T(8,128)} %param.10) | non-fusion elementwise | flops 393216 | bytes 2359296 | tf_op jit(solution)/shard_map/convert_element_type | solution.py:217
  7.9 1.0 copy.22
  8.8 8.6 %all-to-all-start = ((bf16[16,2,3,16,256]{4,3,2,1,0:T(8,128)(2,1)}), bf16[16,2,3,16,256]{4,3,2,1,0:T(8,128)(2,1)S(1)}, u32[]{:S(2)}, u32[]{:S(2)}) async-start(bf16[16,2,3,16,256]{4,3,2,1,0:T(8,128)(2,1)} %bitcast.2), calls=%async_computation | async-start | bytes 1572864 | tf_op jit(solution)/shard_map/all_to_all | solution.py:219
  17.6 0.2 copy.23
  17.8 0.1 fusion.mid_ref
  17.9 0.3 copy-done.5
  18.3 0.1 copy.24.in_ref
  18.5 0.1 compare_convert_fusion.1
  18.6 0.1 stack.42
  18.6 0.2 fusion.4
  18.8 0.1 slice_negate_fusion
  19.0 0.1 stack.36
  19.0 0.1 stack.37
  19.1 0.1 stack.38
  19.2 0.1 stack.39
  19.2 0.1 stack.40
  19.4 0.7 stack.43.factors_ref
  20.1 20.2 %all-to-all-done = bf16[16,2,3,16,256]{4,3,2,1,0:T(8,128)(2,1)S(1)} async-done(((bf16[16,2,3,16,256]{4,3,2,1,0:T(8,128)(2,1)}), bf16[16,2,3,16,256]{4,3,2,1,0:T(8,128)(2,1)S(1)}, u32[]{:S(2)}, u32[]{:S(2)}) %all-to-all-start) | async-done | bytes 786464 | tf_op jit(solution)/shard_map/all_to_all | solution.py:219
  40.3 0.6 turn.1
  40.8 2.7 %collective-permute-start = (bf16[6,32,256]{2,1,0:T(8,128)(2,1)S(1)}, bf16[6,32,256]{2,1,0:T(8,128)(2,1)S(1)}, u32[]{:S(2)}, u32[]{:S(2)}) collective-permute-start(bf16[6,32,256]{2,1,0:T(8,128)(2,1)S(1)} %get-tuple-element.9), channel_id=1, source_target_pairs={{0,8},{16,24},{32,40},{48,56},{64,72},{80,88},{96,104},{112,120},{... | collective-permute-start | bytes 294920 | tf_op jit(solution)/shard_map/ppermute | solution.py:280
  43.5 5.3 %collective-permute-start.1 = (bf16[6,32,256]{2,1,0:T(8,128)(2,1)S(1)}, bf16[6,32,256]{2,1,0:T(8,128)(2,1)S(1)}, u32[]{:S(2)}, u32[]{:S(2)}) collective-permute-start(bf16[6,32,256]{2,1,0:T(8,128)(2,1)S(1)} %get-tuple-element.10), channel_id=1, source_target_pairs={{8,0},{24,16},{40,32},{56,48},{72,64},{88,80},{104,96},{120,112},{... | collective-permute-start | bytes 294920 | tf_op jit(solution)/shard_map/ppermute | solution.py:281
  48.8 0.1 broadcast_in_dim.9.bias_ref
  49.0 13.7 %sources.1.sources_ref = bf16[48,32,256]{2,1,0:T(8,128)(2,1)S(1)} custom-call(bf16[48,32,256]{2,1,0:T(8,128)(2,1)S(1)} %get-tuple-element.8.cells_ref, bf16[512,48]{1,0:T(8,128)(2,1)S(1)} %copy.24.in_ref, bf16[512,512]{1,0:T(8,128)(2,1)S(1)} %fusion.mid_ref, f32[512,128]{1,0:T(8,128)S(1)} %broadcast_in_dim.9.bias_ref, bf16[32,512]{1,0:T(8,128)(2,1)S(1)} %bitcast.20), custom_call_target="tpu_custom_call" | custom-call | flops 7247757312 | bytes 4000000 | tf_op jit(solution)/shard_map/sources/pallas_call | solution.py:282
  62.7 19.3 %steps.1 = bf16[32,3,16,256]{3,2,1,0:T(8,128)(2,1)} custom-call(bf16[48,32,256]{2,1,0:T(8,128)(2,1)S(1)} %get-tuple-element.8.cells_ref, bf16[48,32,256]{2,1,0:T(8,128)(2,1)S(1)} %sources.1.sources_ref, bf16[6,32,256]{2,1,0:T(8,128)(2,1)S(1)} %collective-permute-done.top_ref, bf16[6,32,256]{2,1,0:T(8,128)(2,1)S(1)} %collective-permute-done.1.bottom_ref, ...), custom_call_target="tpu_custom_call" | custom-call | flops 7247757312 | bytes 4000000 | tf_op jit(solution)/shard_map/steps/pallas_call | solution.py:289
  81.9 5.3 %all-to-all-start.1 = ((bf16[16,2,3,16,256]{4,3,2,1,0:T(8,128)(2,1)}), bf16[16,2,3,16,256]{4,3,2,1,0:T(8,128)(2,1)S(1)}, u32[]{:S(2)}, u32[]{:S(2)}) async-start(bf16[16,2,3,16,256]{4,3,2,1,0:T(8,128)(2,1)} %bitcast.9), calls=%async_computation.1 | async-start | bytes 1572864 | tf_op jit(solution)/shard_map/all_to_all | solution.py:303
  87.3 0.1 compare_convert_fusion
  87.4 22.0 %all-to-all-done.1 = bf16[16,2,3,16,256]{4,3,2,1,0:T(8,128)(2,1)S(1)} async-done(((bf16[16,2,3,16,256]{4,3,2,1,0:T(8,128)(2,1)}), bf16[16,2,3,16,256]{4,3,2,1,0:T(8,128)(2,1)S(1)}, u32[]{:S(2)}, u32[]{:S(2)}) %all-to-all-start.1) | async-done | bytes 786464 | tf_op jit(solution)/shard_map/all_to_all | solution.py:303
  109.5 0.2 copy.26
  109.7 1.6 %add_multiply_fusion = f32[2,24,32,256]{3,2,1,0:T(8,128)} fusion(f32[2,24,32,256]{3,2,1,0:T(8,128)S(1)} %copy-done.1, f32[2,24,32,256]{3,2,1,0:T(8,128)S(1)} %bitcast.22, f32[24,32,256]{2,1,0:T(8,128)S(1)} %compare_convert_fusion), kind=kLoop, calls=%fused_computation | loop fusion | flops 786432 | bytes 5505024 | tf_op jit(solution)/shard_map/mul | solution.py:308
  (36 shorter events, 0.4 us)
Async XLA Ops:
  1.8 16.6 %collective-permute-start.2 = (f32[7,2,256]{2,1,0:T(2,128)S(1)}, f32[7,2,256]{2,1,0:T(2,128)S(1)}, u32[]{:S(2)}, u32[]{:S(2)}) collective-permute-start(f32[7,2,256]{2,1,0:T(2,128)S(1)} %constant_dynamic-slice_fusion), channel_id=1, source_target_pairs={{8,16},{24,32},{40,48},{56,64},{72,80},{88,96},{104,112},{120,128}... | collective-permute-start | bytes 43016 | tf_op jit(solution)/shard_map/ppermute | solution.py:240
  7.8 9.7 %copy-start.4 = (f32[512]{0:T(512)S(1)}, f32[512]{0:T(512)}, u32[]{:S(2)}) copy-start(f32[512]{0:T(512)} %param.16) | copy-start | bytes 6148
  7.8 9.7 %copy-start.3 = (bf16[32,512]{1,0:T(8,128)(2,1)S(1)}, bf16[32,512]{1,0:T(8,128)(2,1)}, u32[]{:S(2)}) copy-start(bf16[32,512]{1,0:T(8,128)(2,1)} %param.15) | copy-start | bytes 98308
  7.9 9.7 %copy-start.2 = (bf16[512,512]{1,0:T(8,128)(2,1)S(1)}, bf16[512,512]{1,0:T(8,128)(2,1)}, u32[]{:S(2)}) copy-start(bf16[512,512]{1,0:T(8,128)(2,1)} %param.17) | copy-start | bytes 1572868
  8.8 31.4 %all-to-all-start = ((bf16[16,2,3,16,256]{4,3,2,1,0:T(8,128)(2,1)}), bf16[16,2,3,16,256]{4,3,2,1,0:T(8,128)(2,1)S(1)}, u32[]{:S(2)}, u32[]{:S(2)}) async-start(bf16[16,2,3,16,256]{4,3,2,1,0:T(8,128)(2,1)} %bitcast.2), calls=%async_computation | async-start | bytes 1572864 | tf_op jit(solution)/shard_map/all_to_all | solution.py:219
  17.5 0.7 copy-start.5
  18.9 30.0 %copy-start = (bf16[512,32]{0,1:T(8,128)(2,1)S(1)}, bf16[512,32]{0,1:T(8,128)(2,1)}, u32[]{:S(2)}) copy-start(bf16[512,32]{0,1:T(8,128)(2,1)} %param.19) | copy-start | bytes 98308
  40.8 21.8 %collective-permute-start = (bf16[6,32,256]{2,1,0:T(8,128)(2,1)S(1)}, bf16[6,32,256]{2,1,0:T(8,128)(2,1)S(1)}, u32[]{:S(2)}, u32[]{:S(2)}) collective-permute-start(bf16[6,32,256]{2,1,0:T(8,128)(2,1)S(1)} %get-tuple-element.9), channel_id=1, source_target_pairs={{0,8},{16,24},{32,40},{48,56},{64,72},{80,88},{96,104},{112,120},{... | collective-permute-start | bytes 294920 | tf_op jit(solution)/shard_map/ppermute | solution.py:280
  43.5 19.2 %collective-permute-start.1 = (bf16[6,32,256]{2,1,0:T(8,128)(2,1)S(1)}, bf16[6,32,256]{2,1,0:T(8,128)(2,1)S(1)}, u32[]{:S(2)}, u32[]{:S(2)}) collective-permute-start(bf16[6,32,256]{2,1,0:T(8,128)(2,1)S(1)} %get-tuple-element.10), channel_id=1, source_target_pairs={{8,0},{24,16},{40,32},{56,48},{72,64},{88,80},{104,96},{120,112},{... | collective-permute-start | bytes 294920 | tf_op jit(solution)/shard_map/ppermute | solution.py:281
  81.9 27.5 %all-to-all-start.1 = ((bf16[16,2,3,16,256]{4,3,2,1,0:T(8,128)(2,1)}), bf16[16,2,3,16,256]{4,3,2,1,0:T(8,128)(2,1)S(1)}, u32[]{:S(2)}, u32[]{:S(2)}) async-start(bf16[16,2,3,16,256]{4,3,2,1,0:T(8,128)(2,1)} %bitcast.9), calls=%async_computation.1 | async-start | bytes 1572864 | tf_op jit(solution)/shard_map/all_to_all | solution.py:303
  87.3 22.4 %copy-start.1 = (f32[2,24,32,256]{3,2,1,0:T(8,128)S(1)}, f32[2,24,32,256]{3,2,1,0:T(8,128)}, u32[]{:S(2)}) copy-start(f32[2,24,32,256]{3,2,1,0:T(8,128)} %param.10) | copy-start | bytes 4718596

commit v2 on v1

--- a/solution.py
+++ b/solution.py
@@ -11,6 +11,7 @@
 diffusion = 0.2
 time_step = 0.2
 GROUP = 4
+UNROLL = 1
 
 BF16 = jnp.bfloat16
 F32 = jnp.float32
@@ -45,30 +46,47 @@
                 last_ref[level * 2 + row - rows + 2] = piece
 
 
-def source_kernel(cells_ref, in_ref, mid_ref, bias_ref, out_ref, sources_ref):
+def source_kernel(rows, cells_ref, factors_ref, in_ref, mid_ref, bias_ref, out_ref, middle_ref):
+    pieces, _, width = cells_ref.shape
+    ahead, turns = rows + 2, rows // GROUP
+
     def body(i, _):
-        cells = jnp.concatenate([cells_ref[i * GROUP + k] for k in range(GROUP)], axis=1)
+        level = i // turns
+        row = (i - level * turns) * GROUP
+        at = level * rows + row
+        held = [cells_ref[jnp.maximum(at - 1, 0)]] + [cells_ref[at + k] for k in range(GROUP)]
+        held.append(cells_ref[jnp.minimum(at + GROUP, pieces - 1)])
+        cells = jnp.concatenate(held[1:-1], axis=1)
         result = network(cells, in_ref[...], mid_ref[...], bias_ref[...], out_ref[...])
-        width = cells_ref.shape[2]
+        held = [value.astype(F32) for value in held]
         for k in range(GROUP):
-            sources_ref[i * GROUP + k] = result[:, k * width : (k + 1) * width].astype(BF16)
+            factors = factors_ref[level * ahead + row + 1 + k]
+            above, below = factors[1:2], factors[2:3]
+            if k == 0:
+                above = jnp.where(row > 0, above, 0.0)
+            if k == GROUP - 1:
+                below = jnp.where(row + GROUP < rows, below, 0.0)
+            sources = result[:, k * width : (k + 1) * width].astype(BF16).astype(F32)
+            middle_ref[at + k] = advance(
+                held[k + 1], held[k], held[k + 2], sources, factors, above, below
+            )
         return 0
 
-    lax.fori_loop(0, cells_ref.shape[0] // GROUP, body, 0)
-
-
-def advance(here, above, below, sources, factors):
+    lax.fori_loop(0, pieces // GROUP, body, 0, unroll=UNROLL)
+
+
+def advance(here, above, below, sources, factors, from_above, from_below):
     width = here.shape[1]
     west = pltpu.roll(here, 1, 1)
     east = pltpu.roll(here, width - 1, 1)
-    result = factors[0:1] * here + factors[1:2] * above + factors[2:3] * below
+    result = factors[0:1] * here + from_above * above + from_below * below
     return result + factors[3:4] * west + factors[4:5] * east + factors[5:6] * sources
 
 
 def step_kernel(
     rows,
     cells_ref,
-    sources_ref,
+    partial_ref,
     top_ref,
     bottom_ref,
     factors_ref,
@@ -77,14 +95,12 @@
     bias_ref,
     out_ref,
     change_ref,
-    wide,
-    wide_sources,
     middle,
     scratch,
 ):
     levels = cells_ref.shape[0] // rows
-    width = cells_ref.shape[2]
-    ahead, wider = rows + 2, rows + 4
+    kinds, width = cells_ref.shape[1:]
+    ahead = rows + 2
     edge = []
     for level in range(levels):
         edge += [top_ref[level * 2 + 1], bottom_ref[level * 2]]
@@ -92,32 +108,27 @@
         jnp.concatenate(edge, axis=1), in_ref[...], mid_ref[...], bias_ref[...], out_ref[...]
     ).astype(BF16).astype(F32)
     for level in range(levels):
-        at = 2 * level * width
-        wide_sources[level * ahead] = result[:, at : at + width]
-        wide_sources[level * ahead + ahead - 1] = result[:, at + width : at + 2 * width]
+        base, inside = level * ahead, level * rows
         for k in range(2):
-            wide[level * wider + k] = top_ref[level * 2 + k].astype(F32)
-            wide[level * wider + rows + 2 + k] = bottom_ref[level * 2 + k].astype(F32)
-
-        def widen(row, _):
-            wide[level * wider + 2 + row] = cells_ref[level * rows + row].astype(F32)
-            wide_sources[level * ahead + 1 + row] = sources_ref[level * rows + row].astype(F32)
-            return 0
-
-        lax.fori_loop(0, rows, widen, 0, unroll=4)
-
-        def first_step(row, _):
-            at = level * wider + row
-            middle[level * ahead + row] = advance(
-                wide[at + 1],
-                wide[at],
-                wide[at + 2],
-                wide_sources[level * ahead + row],
-                factors_ref[level * ahead + row],
+            piece = [top_ref, bottom_ref][k][level * 2 : level * 2 + 2].astype(F32)
+            near = cells_ref[inside + k * (rows - 1)].astype(F32)
+            at = base + k * (ahead - 1)
+            factors = factors_ref[at]
+            column = (2 * level + k) * width
+            middle[at] = advance(
+                piece[1 - k],
+                piece[0] if k == 0 else near,
+                near if k == 0 else piece[1],
+                result[:, column : column + width],
+                factors,
+                factors[1:2],
+                factors[2:3],
             )
-            return 0
-
-        lax.fori_loop(0, ahead, first_step, 0, unroll=3)
+            row = base + 1 + k * (rows - 1)
+            term = factors_ref[row][1 + k : 2 + k] * piece[1 - k]
+            middle[row] = partial_ref[inside + k * (rows - 1)] + term
+        for row in range(1, rows - 1):
+            middle[base + 1 + row] = partial_ref[inside + row]
 
     turns = rows // GROUP
 
@@ -136,17 +147,17 @@
                 held[k + 2],
                 result[:, k * width : (k + 1) * width].astype(BF16).astype(F32),
                 factors,
+                factors[1:2],
+                factors[2:3],
             )
-            value = value - factors[6:7] * wide[level * wider + row + k + 2]
-            kinds = value.shape[0]
+            value = value - factors[6:7] * cells_ref[level * rows + row + k].astype(F32)
             for part in range(scratch.shape[0]):
                 scratch[part, pl.ds(level * rows * kinds + row + k, kinds, stride=rows), :] = value[
                     :, part * 128 : (part + 1) * 128
                 ]
         return 0
 
-    lax.fori_loop(0, levels * turns, second_step, 0)
-    kinds = change_ref.shape[0]
+    lax.fori_loop(0, levels * turns, second_step, 0, unroll=UNROLL)
     for level in range(levels):
         for part in range(scratch.shape[0]):
             block = scratch[part, level * rows * kinds : (level + 1) * rows * kinds, :]
@@ -219,6 +230,9 @@
     cells = lax.all_to_all(sent, "tracer", split_axis=0, concat_axis=0, tiled=True)
     cells = cells.reshape(all_kinds, depth_each, rows, columns)
 
+    east_speed, north_speed, land_mask, sent = lax.optimization_barrier(
+        (east_speed, north_speed, land_mask, sent)
+    )
     depth = jnp.where(land_mask == 1, bottom_level, 0).astype(F32)
     first_level = stack * depth_each
     east = lax.dynamic_slice_in_dim(east_speed, first_level, depth_each, 0)
@@ -279,25 +293,23 @@
     )(cells)
     top = lax.ppermute(last, axes, within + across)
     bottom = lax.ppermute(first, axes, [(j, i) for i, j in within] + back)
-    sources = kernel_call(
-        source_kernel,
-        jax.ShapeDtypeStruct(turned.shape, BF16),
+    partial = kernel_call(
+        functools.partial(source_kernel, rows),
+        jax.ShapeDtypeStruct(turned.shape, F32),
         [],
         pieces * per_piece,
         "sources",
-    )(turned, *weights)
+    )(turned, factors, *weights)
     change = kernel_call(
         functools.partial(step_kernel, rows),
         jax.ShapeDtypeStruct(cells.shape, BF16),
         [
-            pltpu.VMEM((depth_each * (rows + 4), all_kinds, columns), F32),
-            pltpu.VMEM((depth_each * (rows + 2), all_kinds, columns), F32),
             pltpu.VMEM((depth_each * (rows + 2), all_kinds, columns), F32),
             pltpu.VMEM((columns // 128, depth_each * rows * all_kinds, 128), F32),
         ],
         pieces * per_piece,
         "steps",
-    )(turned, sources, top, bottom, factors, *weights)
+    )(turned, partial, top, bottom, factors, *weights)
 
     change = change.reshape(group, kinds, depth_each, rows, columns)
     change = lax.all_to_all(change, "tracer", split_axis=0, concat_axis=0, tiled=True)

time: 112 us -> 104 us (0.929)
  waiting for transfers between devices: 42.2 us -> 36.9 us
  Pallas kernels: 33.5 us -> 31.4 us
  starting transfers between devices: 26.4 us -> 27.6 us
    all_to_all x1, waiting for transfers between devices: 20.2 us -> 12.4 us  [body(): lax.all_to_all(sent, 'tracer', split_axis=0, concat_axis=0, tiled=True)]
    all_to_all x1, starting transfers between devices: 8.61 us -> 11.3 us  [body(): lax.all_to_all(sent, 'tracer', split_axis=0, concat_axis=0, tiled=True)]
    ppermute x1, waiting for transfers between devices: 0.01 us -> 2.6 us  [body(): arrived = lax.ppermute(edge, axes, across + back)]
    pallas_call x1, Pallas kernels: 19.3 us -> 16.8 us  [body(): kernel_call(functools.partial(step_kernel, rows), jax.ShapeDtypeStruct(ce...]
    all_to_all x1, starting transfers between devices: 5.35 us -> 4.11 us  [body(): lax.all_to_all(change, 'tracer', split_axis=0, concat_axis=0, tiled=True)]
  transfers between devices with their start and end apart: 5 -> 5, of which waited for: 2 -> 3; matrix products, arithmetic and copies ran while one was open for 4% -> 3% of each run, Pallas kernels for 12% -> 13%
where the time goes in v2:
time: 104 us
  waiting for transfers between devices  36.9 us (35%)
  Pallas kernels  31.4 us (30%)
  starting transfers between devices  27.6 us (27%)
  local copies, waits for them, and re-layouts  3.92 us (4%)
  other arithmetic  3.81 us (4%)
    all_to_all x1, waiting for transfers between devices, body(): lax.all_to_all(change, 'tracer', split_axis=0, concat_axis=0, tiled=True)  21.9 us
    pallas_call x1, Pallas kernels, body(): kernel_call(functools.partial(step_kernel, rows), jax.ShapeDtypeStruct(ce...  16.8 us
    pallas_call x1, Pallas kernels, body(): kernel_call(functools.partial(source_kernel, rows), jax.ShapeDtypeStruct(...  13.9 us
    all_to_all x1, waiting for transfers between devices, body(): lax.all_to_all(sent, 'tracer', split_axis=0, concat_axis=0, tiled=True)  12.4 us
    all_to_all x1, starting transfers between devices, body(): lax.all_to_all(sent, 'tracer', split_axis=0, concat_axis=0, tiled=True)  11.3 us
    ppermute x1, starting transfers between devices, body(): bottom = lax.ppermute(first, axes, [(j, i) for i, j in within] + back)  5.59 us
    ppermute x1, starting transfers between devices, body(): arrived = lax.ppermute(edge, axes, across + back)  4.16 us
    all_to_all x1, starting transfers between devices, body(): lax.all_to_all(change, 'tracer', split_axis=0, concat_axis=0, tiled=True)  4.11 us
  transfers between devices with their start and end apart: 5, of which 3 were waited for; matrix products, arithmetic and copies ran while one was open for 3% of the time, Pallas kernels for 13%

profile of v2, /device:TPU:2, one launch (start us, length us, event | category | flops | bytes accessed | tf_op | source)
XLA Modules:
  0.0 104.0 jit_solution(18130287635531297262)
XLA Ops:
  0.0 1.5 %convert_element_type.77 = bf16[2,24,32,256]{3,2,1,0:T(8,128)(2,1)S(1)} convert(f32[2,24,32,256]{3,2,1,0:T(8,128)} %param.10) | non-fusion elementwise | flops 393216 | bytes 2359296 | tf_op jit(solution)/shard_map/convert_element_type | solution.py:228
  1.5 1.0 copy.22
  2.5 11.3 %all-to-all-start = ((bf16[16,2,3,16,256]{4,3,2,1,0:T(8,128)(2,1)}), bf16[16,2,3,16,256]{4,3,2,1,0:T(8,128)(2,1)S(1)}, u32[]{:S(2)}, u32[]{:S(2)}) async-start(bf16[16,2,3,16,256]{4,3,2,1,0:T(8,128)(2,1)} %bitcast.2), calls=%async_computation | async-start | bytes 1572864 | tf_op jit(solution)/shard_map/all_to_all | solution.py:230
  13.9 1.0 constant_dynamic-slice_fusion.1
  15.0 4.2 %collective-permute-start = (f32[7,2,256]{2,1,0:T(2,128)S(1)}, f32[7,2,256]{2,1,0:T(2,128)S(1)}, u32[]{:S(2)}, u32[]{:S(2)}) collective-permute-start(f32[7,2,256]{2,1,0:T(2,128)S(1)} %constant_dynamic-slice_fusion), channel_id=1, source_target_pairs={{8,16},{24,32},{40,48},{56,64},{72,80},{88,96},{104,112},{120,128}... | collective-permute-start | bytes 43016 | tf_op jit(solution)/shard_map/ppermute | solution.py:254
  19.2 0.2 copy.23
  19.4 0.1 fusion.mid_ref
  19.7 0.1 copy.24.in_ref
  19.8 2.6 %collective-permute-done = f32[7,2,256]{2,1,0:T(2,128)S(1)} collective-permute-done((f32[7,2,256]{2,1,0:T(2,128)S(1)}, f32[7,2,256]{2,1,0:T(2,128)S(1)}, u32[]{:S(2)}, u32[]{:S(2)}) %collective-permute-start) | collective-permute-done | bytes 14368 | tf_op jit(solution)/shard_map/ppermute | solution.py:254
  22.5 0.1 compare_convert_fusion.1
  22.6 0.1 stack.39
  22.6 0.2 fusion.4
  22.8 0.1 slice_negate_fusion
  23.0 0.1 stack.33
  23.0 0.1 stack.34
  23.1 0.1 stack.35
  23.2 0.1 stack.36
  23.2 0.1 stack.37
  23.3 0.1 stack.38
  23.4 0.7 stack.40.factors_ref
  24.1 12.4 %all-to-all-done = bf16[16,2,3,16,256]{4,3,2,1,0:T(8,128)(2,1)S(1)} async-done(((bf16[16,2,3,16,256]{4,3,2,1,0:T(8,128)(2,1)}), bf16[16,2,3,16,256]{4,3,2,1,0:T(8,128)(2,1)S(1)}, u32[]{:S(2)}, u32[]{:S(2)}) %all-to-all-start) | async-done | bytes 786464 | tf_op jit(solution)/shard_map/all_to_all | solution.py:230
  36.5 0.6 turn.1
  37.1 2.4 %collective-permute-start.1 = (bf16[6,32,256]{2,1,0:T(8,128)(2,1)S(1)}, bf16[6,32,256]{2,1,0:T(8,128)(2,1)S(1)}, u32[]{:S(2)}, u32[]{:S(2)}) collective-permute-start(bf16[6,32,256]{2,1,0:T(8,128)(2,1)S(1)} %get-tuple-element.15), channel_id=1, source_target_pairs={{0,8},{16,24},{32,40},{48,56},{64,72},{80,88},{96,104},{112,120},{... | collective-permute-start | bytes 294920 | tf_op jit(solution)/shard_map/ppermute | solution.py:294
  39.5 5.6 %collective-permute-start.2 = (bf16[6,32,256]{2,1,0:T(8,128)(2,1)S(1)}, bf16[6,32,256]{2,1,0:T(8,128)(2,1)S(1)}, u32[]{:S(2)}, u32[]{:S(2)}) collective-permute-start(bf16[6,32,256]{2,1,0:T(8,128)(2,1)S(1)} %get-tuple-element.16), channel_id=1, source_target_pairs={{8,0},{24,16},{40,32},{56,48},{72,64},{88,80},{104,96},{120,112},{... | collective-permute-start | bytes 294920 | tf_op jit(solution)/shard_map/ppermute | solution.py:295
  45.1 0.1 broadcast_in_dim.10.bias_ref
  45.2 13.9 %sources.1.partial_ref = f32[48,32,256]{2,1,0:T(8,128)S(1)} custom-call(bf16[48,32,256]{2,1,0:T(8,128)(2,1)S(1)} %get-tuple-element.12.cells_ref, f32[54,8,256]{2,1,0:T(8,128)S(1)} %stack.40.factors_ref, bf16[512,48]{1,0:T(8,128)(2,1)S(1)} %copy.24.in_ref, bf16[512,512]{1,0:T(8,128)(2,1)S(1)} %fusion.mid_ref, f32[512,128]{1,0:T(8,128)S(1)} %broadcast_in_dim.10.bias_ref, ...), custom_call_target="tpu_custom_call" | custom-call | flops 7247757312 | bytes 4000000 | tf_op jit(solution)/shard_map/sources/pallas_call | solution.py:296
  59.2 16.8 %steps.1 = bf16[32,3,16,256]{3,2,1,0:T(8,128)(2,1)} custom-call(bf16[48,32,256]{2,1,0:T(8,128)(2,1)S(1)} %get-tuple-element.12.cells_ref, f32[48,32,256]{2,1,0:T(8,128)S(1)} %sources.1.partial_ref, bf16[6,32,256]{2,1,0:T(8,128)(2,1)S(1)} %collective-permute-done.1.top_ref, bf16[6,32,256]{2,1,0:T(8,128)(2,1)S(1)} %collective-permute-done.2.bottom_ref, ...), custom_call_target="tpu_custom_call" | custom-call | flops 7247757312 | bytes 4000000 | tf_op jit(solution)/shard_map/steps/pallas_call | solution.py:303
  76.0 4.1 %all-to-all-start.1 = ((bf16[16,2,3,16,256]{4,3,2,1,0:T(8,128)(2,1)}), bf16[16,2,3,16,256]{4,3,2,1,0:T(8,128)(2,1)S(1)}, u32[]{:S(2)}, u32[]{:S(2)}) async-start(bf16[16,2,3,16,256]{4,3,2,1,0:T(8,128)(2,1)} %bitcast.9), calls=%async_computation.1 | async-start | bytes 1572864 | tf_op jit(solution)/shard_map/all_to_all | solution.py:315
  80.2 0.1 compare_convert_fusion
  80.3 21.9 %all-to-all-done.1 = bf16[16,2,3,16,256]{4,3,2,1,0:T(8,128)(2,1)S(1)} async-done(((bf16[16,2,3,16,256]{4,3,2,1,0:T(8,128)(2,1)}), bf16[16,2,3,16,256]{4,3,2,1,0:T(8,128)(2,1)S(1)}, u32[]{:S(2)}, u32[]{:S(2)}) %all-to-all-start.1) | async-done | bytes 786464 | tf_op jit(solution)/shard_map/all_to_all | solution.py:315
  102.2 0.2 copy.26
  102.4 1.6 %add_multiply_fusion = f32[2,24,32,256]{3,2,1,0:T(8,128)} fusion(f32[2,24,32,256]{3,2,1,0:T(8,128)S(1)} %copy-done.1, f32[2,24,32,256]{3,2,1,0:T(8,128)S(1)} %bitcast.22, f32[24,32,256]{2,1,0:T(8,128)S(1)} %compare_convert_fusion), kind=kLoop, calls=%fused_computation | loop fusion | flops 786432 | bytes 5505024 | tf_op jit(solution)/shard_map/mul | solution.py:320
  (40 shorter events, 0.3 us)
Async XLA Ops:
  1.5 12.4 %copy-start.3 = (s32[32,256]{1,0:T(8,128)S(1)}, s32[32,256]{1,0:T(8,128)}, u32[]{:S(2)}) copy-start(s32[32,256]{1,0:T(8,128)} %param.14) | copy-start | bytes 98308
  1.5 12.4 %copy-start.4 = (s32[32,256]{1,0:T(8,128)S(1)}, s32[32,256]{1,0:T(8,128)}, u32[]{:S(2)}) copy-start(s32[32,256]{1,0:T(8,128)} %param.13) | copy-start | bytes 98308
  2.5 16.6 %copy-start.6 = (f32[512]{0:T(512)S(1)}, f32[512]{0:T(512)}, u32[]{:S(2)}) copy-start(f32[512]{0:T(512)} %param.16) | copy-start | bytes 6148
  2.5 16.7 %copy-start.5 = (bf16[32,512]{1,0:T(8,128)(2,1)S(1)}, bf16[32,512]{1,0:T(8,128)(2,1)}, u32[]{:S(2)}) copy-start(bf16[32,512]{1,0:T(8,128)(2,1)} %param.15) | copy-start | bytes 98308
  2.5 16.7 %copy-start.2 = (bf16[512,512]{1,0:T(8,128)(2,1)S(1)}, bf16[512,512]{1,0:T(8,128)(2,1)}, u32[]{:S(2)}) copy-start(bf16[512,512]{1,0:T(8,128)(2,1)} %param.17) | copy-start | bytes 1572868
  2.5 34.0 %all-to-all-start = ((bf16[16,2,3,16,256]{4,3,2,1,0:T(8,128)(2,1)}), bf16[16,2,3,16,256]{4,3,2,1,0:T(8,128)(2,1)S(1)}, u32[]{:S(2)}, u32[]{:S(2)}) async-start(bf16[16,2,3,16,256]{4,3,2,1,0:T(8,128)(2,1)} %bitcast.2), calls=%async_computation | async-start | bytes 1572864 | tf_op jit(solution)/shard_map/all_to_all | solution.py:230
  14.9 4.6 %copy-start.7 = (f32[512]{0:T(512)S(1)}, f32[512]{0:T(512)}, u32[]{:S(2)}) copy-start(f32[512]{0:T(512)} %param.18) | copy-start | bytes 6148
  15.0 7.4 %collective-permute-start = (f32[7,2,256]{2,1,0:T(2,128)S(1)}, f32[7,2,256]{2,1,0:T(2,128)S(1)}, u32[]{:S(2)}, u32[]{:S(2)}) collective-permute-start(f32[7,2,256]{2,1,0:T(2,128)S(1)} %constant_dynamic-slice_fusion), channel_id=1, source_target_pairs={{8,16},{24,32},{40,48},{56,64},{72,80},{88,96},{104,112},{120,128}... | collective-permute-start | bytes 43016 | tf_op jit(solution)/shard_map/ppermute | solution.py:254
  23.0 22.2 %copy-start = (bf16[512,32]{0,1:T(8,128)(2,1)S(1)}, bf16[512,32]{0,1:T(8,128)(2,1)}, u32[]{:S(2)}) copy-start(bf16[512,32]{0,1:T(8,128)(2,1)} %param.19) | copy-start | bytes 98308
  37.1 22.1 %collective-permute-start.1 = (bf16[6,32,256]{2,1,0:T(8,128)(2,1)S(1)}, bf16[6,32,256]{2,1,0:T(8,128)(2,1)S(1)}, u32[]{:S(2)}, u32[]{:S(2)}) collective-permute-start(bf16[6,32,256]{2,1,0:T(8,128)(2,1)S(1)} %get-tuple-element.15), channel_id=1, source_target_pairs={{0,8},{16,24},{32,40},{48,56},{64,72},{80,88},{96,104},{112,120},{... | collective-permute-start | bytes 294920 | tf_op jit(solution)/shard_map/ppermute | solution.py:294
  39.5 19.7 %collective-permute-start.2 = (bf16[6,32,256]{2,1,0:T(8,128)(2,1)S(1)}, bf16[6,32,256]{2,1,0:T(8,128)(2,1)S(1)}, u32[]{:S(2)}, u32[]{:S(2)}) collective-permute-start(bf16[6,32,256]{2,1,0:T(8,128)(2,1)S(1)} %get-tuple-element.16), channel_id=1, source_target_pairs={{8,0},{24,16},{40,32},{56,48},{72,64},{88,80},{104,96},{120,112},{... | collective-permute-start | bytes 294920 | tf_op jit(solution)/shard_map/ppermute | solution.py:295
  76.0 26.1 %all-to-all-start.1 = ((bf16[16,2,3,16,256]{4,3,2,1,0:T(8,128)(2,1)}), bf16[16,2,3,16,256]{4,3,2,1,0:T(8,128)(2,1)S(1)}, u32[]{:S(2)}, u32[]{:S(2)}) async-start(bf16[16,2,3,16,256]{4,3,2,1,0:T(8,128)(2,1)} %bitcast.9), calls=%async_computation.1 | async-start | bytes 1572864 | tf_op jit(solution)/shard_map/all_to_all | solution.py:315
  80.1 22.2 %copy-start.1 = (f32[2,24,32,256]{3,2,1,0:T(8,128)S(1)}, f32[2,24,32,256]{3,2,1,0:T(8,128)}, u32[]{:S(2)}) copy-start(f32[2,24,32,256]{3,2,1,0:T(8,128)} %param.10) | copy-start | bytes 4718596

commit v3 on v0

--- a/solution.py
+++ b/solution.py
@@ -1,15 +1,440 @@
+import functools
 import math
 
 import jax
 import jax.numpy as jnp
 from jax import lax
+from jax.experimental import pallas as pl
+from jax.experimental.pallas import tpu as pltpu
 from jax.sharding import PartitionSpec as P
 
 STEPS = 2
-
-
 diffusion = 0.2
 time_step = 0.2
+GROUP = 4
+
+BF16 = jnp.bfloat16
+F32 = jnp.float32
+
+
+def silu_of_half(half):
+    return (half + half * jnp.tanh(half)).astype(BF16)
+
+
+def network(cells, in_weight, mid_weight, mid_bias, out_weight):
+    lanes = cells.shape[1]
+    cells = jnp.concatenate([cells, jnp.ones((16, lanes), BF16)], axis=0)
+    hidden = silu_of_half(jnp.dot(in_weight, cells, preferred_element_type=F32))
+    hidden = jnp.dot(mid_weight, hidden, preferred_element_type=F32)
+    hidden = silu_of_half(hidden + jnp.concatenate([mid_bias] * (lanes // 128), axis=1))
+    return jnp.dot(out_weight, hidden, preferred_element_type=F32)
+
+
+def turn_kernel(rows, x_ref, turned_ref, first_ref, last_ref, scratch):
+    kinds, levels = x_ref.shape[:2]
+    for level in range(levels):
+        for part in range(scratch.shape[0]):
+            block = x_ref[:, level, :, part * 128 : (part + 1) * 128]
+            scratch[part] = block.astype(F32).reshape(kinds * rows, 128)
+        for row in range(rows):
+            picked = [scratch[part, pl.ds(row, kinds, stride=rows), :] for part in range(scratch.shape[0])]
+            piece = jnp.concatenate(picked, axis=1).astype(BF16)
+            turned_ref[level * rows + row] = piece
+            if row < 2:
+                first_ref[level * 2 + row] = piece
+            if row >= rows - 2:
+                last_ref[level * 2 + row - rows + 2] = piece
+
+
+def advance(here, above, below, sources, factors, from_above, from_below):
+    width = here.shape[1]
+    west = pltpu.roll(here, 1, 1)
+    east = pltpu.roll(here, width - 1, 1)
+    result = factors[0:1] * here + from_above * above + from_below * below
+    return result + factors[3:4] * west + factors[4:5] * east + factors[5:6] * sources
+
+
+def nt(rows, table):
+    return lax.dot_general(rows, table, (((1,), (1,)), ((), ())), preferred_element_type=F32)
+
+
+def nn(rows, table):
+    return jnp.dot(rows, table, preferred_element_type=F32)
+
+
+def one_hot(place):
+    width = place.shape[1]
+    slots = lax.broadcasted_iota(jnp.int32, (width, width), 0).astype(F32)
+    return jnp.where(slots == place, 1.0, 0.0).astype(BF16)
+
+
+def halves_of(ref, start, size, stride):
+    return jnp.concatenate(
+        [ref[part, pl.ds(start, size, stride=stride), :] for part in range(ref.shape[0])], axis=1
+    )
+
+
+def put_halves(ref, start, size, stride, value):
+    for part in range(ref.shape[0]):
+        ref[part, pl.ds(start, size, stride=stride), :] = value[:, part * 128 : (part + 1) * 128]
+
+
+def pack_kernel(x_ref, land_ref, bottom_ref, sent_ref, place_ref, depth_ref, counts, table, held, packed):
+    kinds, levels, length, width = x_ref.shape
+    halves, stacks, _, _, rows, _ = sent_ref.shape
+    depth_ref[...] = jnp.where(land_ref[...] == 1, bottom_ref[...], 0).astype(F32)
+    bins = 32
+    value = lax.broadcasted_iota(jnp.int32, (bins, width), 0).astype(F32)
+    for row in range(length):
+        depth = depth_ref[row : row + 1]
+        counts[row * bins : (row + 1) * bins, :width] = jnp.where(depth == value, 1.0, 0.0).astype(BF16)
+        counts[row * bins : (row + 1) * bins, width:] = jnp.where(depth > value, 1.0, 0.0).astype(BF16)
+    before = lax.broadcasted_iota(jnp.int32, (width, width), 0)
+    after = lax.broadcasted_iota(jnp.int32, (width, width), 1)
+    table[:width] = jnp.where(before < after, 1.0, 0.0).astype(BF16)
+    table[width:] = jnp.ones((width, width), BF16)
+    ranks = nn(counts[...], table[...])
+    for row in range(length):
+        here = jnp.where(depth_ref[row : row + 1] == value, ranks[row * bins : (row + 1) * bins], 0.0)
+        place = jnp.sum(here, axis=0, keepdims=True)
+        place_ref[row : row + 1] = place if row % 2 == 0 else (width - 1.0) - place
+
+    thin = levels - stacks
+    for kind in range(kinds):
+        for part in range(held.shape[0]):
+            block = x_ref[kind, stacks:, :, part * 128 : (part + 1) * 128]
+            held[part, kind * thin * length : (kind + 1) * thin * length] = block.reshape(thin * length, 128)
+    level = stacks + lax.broadcasted_iota(jnp.int32, (thin, width), 0).astype(F32)
+
+    def body(i, _):
+        sorted_rows = []
+        for k in range(2):
+            row = 2 * i + k
+            wet = level < depth_ref[pl.ds(row, 1)]
+            cells = [
+                jnp.where(wet, halves_of(held, kind * thin * length + row, thin, length), 0.0).astype(BF16)
+                for kind in range(kinds)
+            ]
+            sorted_rows.append(nt(jnp.concatenate(cells, axis=0), one_hot(place_ref[pl.ds(row, 1)])))
+        for k in range(2):
+            for kind in range(kinds):
+                at = kind * thin
+                deep = sorted_rows[1 - k][at + stacks : at + 2 * stacks]
+                value = sorted_rows[k][at : at + stacks] + pltpu.roll(deep, stacks // 2, 0)
+                put_halves(packed, kind * stacks * length + 2 * i + k, stacks, length, value)
+        return 0
+
+    lax.fori_loop(0, length // 2, body, 0, unroll=2)
+    for half in range(halves):
+        inside = slice(half * rows, (half + 1) * rows)
+        for kind in range(kinds):
+            sent_ref[half, :, kind, 0] = x_ref[kind, :stacks, inside].astype(BF16)
+            for part in range(packed.shape[0]):
+                at = kind * stacks * length
+                block = packed[part, at : at + stacks * length].reshape(stacks, length, 128)
+                sent_ref[half, :, kind, 1, :, part * 128 : (part + 1) * 128] = block[:, inside].astype(BF16)
+
+
+def finish_kernel(x_ref, arrived_ref, place_ref, land_ref, bottom_ref, result_ref, held, spread):
+    kinds, levels, length, width = x_ref.shape
+    halves, stacks, _, _, rows, _ = arrived_ref.shape
+    thin = levels - stacks
+    each = stacks * kinds * rows
+    for half in range(halves):
+        for part in range(held.shape[0]):
+            block = arrived_ref[half, :, :, 1, :, part * 128 : (part + 1) * 128]
+            held[part, half * each : (half + 1) * each] = block.astype(F32).reshape(each, 128)
+
+    def body(i, _):
+        half = i // (rows // 2)
+        row = 2 * i - half * rows
+        cells = []
+        for k in range(2):
+            for kind in range(kinds):
+                cells.append(halves_of(held, half * each + kind * rows + row + k, stacks, kinds * rows))
+        cells = jnp.concatenate(cells, axis=0).astype(BF16)
+        for k in range(2):
+            value = nn(cells, one_hot(place_ref[pl.ds(2 * i + k, 1)]))
+            for kind in range(kinds):
+                near = (k * kinds + kind) * stacks
+                other = ((1 - k) * kinds + kind) * stacks
+                at = kind * thin * length + 2 * i + k
+                put_halves(spread, at, stacks, length, value[near : near + stacks])
+                deep = pltpu.roll(value[other : other + stacks], stacks // 2, 0)
+                put_halves(spread, at + stacks * length, stacks, length, deep)
+        return 0
+
+    lax.fori_loop(0, length // 2, body, 0, unroll=2)
+    depth = jnp.where(land_ref[...] == 1, bottom_ref[...], 0)
+    for kind in range(kinds):
+        for level in range(levels):
+            if level < stacks:
+                change = jnp.concatenate(
+                    [arrived_ref[half, level, kind, 0] for half in range(halves)], axis=0
+                ).astype(F32)
+            else:
+                at = (kind * thin + level - stacks) * length
+                change = jnp.concatenate(
+                    [spread[part, at : at + length] for part in range(spread.shape[0])], axis=1
+                )
+            result_ref[kind, level] = jnp.where(level < depth, x_ref[kind, level] + change, 0.0)
+
+
+def source_kernel(
+    rows, cells_ref, table_ref, factors_ref, in_ref, mid_ref, bias_ref, out_ref, middle_ref, spread_ref, held
+):
+    _, kinds, width = cells_ref.shape
+    ahead = rows + 2
+    weights = (in_ref, mid_ref, bias_ref, out_ref)
+
+    def cell(level, row):
+        if level == 0:
+            return cells_ref[row]
+        return spread_ref[(level - 1) * rows + row]
+
+    def spread_out(i, _):
+        row = 2 * i
+        cells = jnp.concatenate([cells_ref[rows + row], cells_ref[rows + row + 1]], axis=0)
+        for k in range(2):
+            value = nn(cells, table_ref[row + 2 + k]).astype(BF16)
+            spread_ref[row + k] = value[k * kinds : (k + 1) * kinds]
+            spread_ref[rows + row + k] = value[(1 - k) * kinds : (2 - k) * kinds]
+        return 0
+
+    lax.fori_loop(0, rows // 2, spread_out, 0, unroll=2)
+
+    def sources(i):
+        row = 2 * i
+        cells = [cells_ref[row], cells_ref[row + 1], cells_ref[rows + row], cells_ref[rows + row + 1]]
+        result = network(jnp.concatenate(cells, axis=1), *[ref[...] for ref in weights])
+        held[i] = result.astype(BF16)
+
+    def move(i):
+        row = 2 * i
+        result = held[i]
+        packed = jnp.concatenate(
+            [result[:, 2 * width : 3 * width], result[:, 3 * width :]], axis=0
+        )
+        for k in range(2):
+            value = nn(packed, table_ref[row + 2 + k])
+            pieces = [
+                result[:, k * width : (k + 1) * width].astype(F32),
+                value[k * kinds : (k + 1) * kinds],
+                value[(1 - k) * kinds : (2 - k) * kinds],
+            ]
+            for level in range(3):
+                factors = factors_ref[level * ahead + row + 1 + k]
+                above, below = factors[1:2], factors[2:3]
+                if k == 0:
+                    above = jnp.where(row > 0, above, 0.0)
+                else:
+                    below = jnp.where(row + 2 < rows, below, 0.0)
+                middle_ref[level * rows + row + k] = advance(
+                    cell(level, row + k).astype(F32),
+                    cell(level, jnp.maximum(row + k - 1, 0)).astype(F32),
+                    cell(level, jnp.minimum(row + k + 1, rows - 1)).astype(F32),
+                    pieces[level],
+                    factors,
+                    above,
+                    below,
+                )
+
+    def body(i, _):
+        move(i - 1)
+        sources(i)
+        return 0
+
+    sources(0)
+    lax.fori_loop(1, rows // 2, body, 0)
+    move(rows // 2 - 1)
+
+
+def step_kernel(
+    rows,
+    cells_ref,
+    spread_ref,
+    partial_ref,
+    top_ref,
+    bottom_ref,
+    table_ref,
+    factors_ref,
+    in_ref,
+    mid_ref,
+    bias_ref,
+    out_ref,
+    change_ref,
+    middle,
+    packed,
+    held,
+    scratch,
+):
+    _, kinds, width = cells_ref.shape
+    ahead = rows + 2
+    weights = (in_ref, mid_ref, bias_ref, out_ref)
+
+    def run(cells):
+        return network(jnp.concatenate(cells, axis=1), *[ref[...] for ref in weights]).astype(BF16)
+
+    edges = [
+        [top_ref[1], top_ref[2], top_ref[3]],
+        [bottom_ref[0], bottom_ref[2], bottom_ref[3]],
+    ]
+    result = run(edges[0] + edges[1])
+    for k in range(2):
+        packed_cells = jnp.concatenate(edges[k][1:], axis=0)
+        at = 3 * k * width
+        packed_sources = jnp.concatenate(
+            [result[:, at + width : at + 2 * width], result[:, at + 2 * width : at + 3 * width]], axis=0
+        )
+        near = nn(jnp.concatenate([packed_cells, packed_sources], axis=0), table_ref[[1, rows + 2][k]])
+        far = nn(packed_cells, table_ref[[0, rows + 3][k]])
+        near_at = [[1, 0], [0, 1]][k]
+        far_at = [[0, 1], [1, 0]][k]
+        for level in range(3):
+            inside = level * rows + k * (rows - 1)
+            if level == 0:
+                own = edges[k][0].astype(F32)
+                other = (top_ref[0] if k == 0 else bottom_ref[1]).astype(F32)
+                sources = result[:, at : at + width].astype(F32)
+                inner = cells_ref[k * (rows - 1)].astype(F32)
+            else:
+                place = near_at[level - 1] * kinds
+                own = near[place : place + kinds]
+                sources = near[2 * kinds + place : 3 * kinds + place]
+                place = far_at[level - 1] * kinds
+                other = far[place : place + kinds]
+                inner = spread_ref[(level - 1) * rows + k * (rows - 1)].astype(F32)
+            row = level * ahead + k * (ahead - 1)
+            factors = factors_ref[row]
+            middle[row] = advance(
+                own,
+                other if k == 0 else inner,
+                inner if k == 0 else other,
+                sources,
+                factors,
+                factors[1:2],
+                factors[2:3],
+            )
+            row = level * ahead + 1 + k * (rows - 1)
+            middle[row] = partial_ref[inside] + factors_ref[row][1 + k : 2 + k] * own
+    for level in range(3):
+        for row in range(1, rows - 1):
+            middle[level * ahead + 1 + row] = partial_ref[level * rows + row]
+
+    def put_together(row, thin):
+        values = [nt(thin[k], table_ref[row + 2 + k]) for k in range(2)]
+        return [values[k][:kinds] + values[1 - k][kinds:] for k in range(2)]
+
+    def pack(i, _):
+        row = 2 * i
+        thin = [
+            jnp.concatenate(
+                [middle[level * ahead + 1 + row + k].astype(BF16) for level in (1, 2)], axis=0
+            )
+            for k in range(2)
+        ]
+        values = put_together(row, thin)
+        for k in range(2):
+            packed[row + k] = values[k].astype(BF16)
+        return 0
+
+    lax.fori_loop(0, rows // 2, pack, 0, unroll=2)
+
+    def sources_of(i):
+        row = 2 * i
+        cells = [middle[1 + row + k].astype(BF16) for k in range(2)]
+        held[i] = run(cells + [packed[row], packed[row + 1]])
+
+    def move(i):
+        row = 2 * i
+        result = held[i]
+        thin_sources = jnp.concatenate(
+            [result[:, 2 * width : 3 * width], result[:, 3 * width :]], axis=0
+        )
+        changes = []
+        for k in range(2):
+            value = nn(thin_sources, table_ref[row + 2 + k])
+            pieces = [
+                result[:, k * width : (k + 1) * width].astype(F32),
+                value[k * kinds : (k + 1) * kinds],
+                value[(1 - k) * kinds : (2 - k) * kinds],
+            ]
+            for level in range(3):
+                at = level * ahead + 1 + row + k
+                factors = factors_ref[at]
+                value = advance(
+                    middle[at],
+                    middle[at - 1],
+                    middle[at + 1],
+                    pieces[level],
+                    factors,
+                    factors[1:2],
+                    factors[2:3],
+                )
+                if level == 0:
+                    first = cells_ref[row + k]
+                else:
+                    first = spread_ref[(level - 1) * rows + row + k]
+                changes.append(value - factors[6:7] * first.astype(F32))
+        thin = [
+            jnp.concatenate([changes[3 * k + 1].astype(BF16), changes[3 * k + 2].astype(BF16)], axis=0)
+            for k in range(2)
+        ]
+        values = put_together(row, thin)
+        for k in range(2):
+            put_halves(scratch, row + k, kinds, rows, changes[3 * k])
+            put_halves(scratch, rows * kinds + row + k, kinds, rows, values[k])
+
+    def body(i, _):
+        move(i - 1)
+        sources_of(i)
+        return 0
+
+    sources_of(0)
+    lax.fori_loop(1, rows // 2, body, 0)
+    move(rows // 2 - 1)
+    for level in range(2):
+        for part in range(scratch.shape[0]):
+            block = scratch[part, level * rows * kinds : (level + 1) * rows * kinds, :]
+            change_ref[:, level, :, part * 128 : (part + 1) * 128] = block.reshape(kinds, rows, 128).astype(BF16)
+
+
+def kernel_call(kernel, outs, scratch, flops, name):
+    return pl.pallas_call(
+        kernel,
+        out_shape=outs,
+        scratch_shapes=scratch,
+        cost_estimate=pl.CostEstimate(flops=flops, bytes_accessed=4_000_000, transcendentals=0),
+        compiler_params=pltpu.CompilerParams(vmem_limit_bytes=24 * 2**20),
+        name=name,
+    )
+
+
+def factors_of(east, north, depth, level):
+    wet = (level[:, None, None] < depth[None]).astype(F32)
+    opened = time_step * wet[:, :-1] * wet[:, 1:]
+    plus = opened * (jnp.maximum(east[:, :-1], 0.0) + diffusion)
+    minus = opened * (jnp.minimum(east[:, :-1], 0.0) - diffusion)
+    inner = wet[:, 1:-1]
+    flow = jnp.pad(north[:, 1:-1], ((0, 0), (0, 0), (1, 0)))
+    sides = jnp.pad(inner, ((0, 0), (0, 0), (1, 1)))
+    opened = time_step * sides[..., :-1] * sides[..., 1:]
+    right = opened * (jnp.maximum(flow, 0.0) + diffusion)
+    left = opened * (jnp.minimum(flow, 0.0) - diffusion)
+    own = inner + (minus[:, :-1] - plus[:, 1:]) + (left[..., :-1] - right[..., 1:])
+    return jnp.stack(
+        [
+            own,
+            plus[:, :-1],
+            -minus[:, 1:],
+            right[..., :-1],
+            -left[..., 1:],
+            time_step * inner,
+            inner,
+            jnp.zeros_like(inner),
+        ],
+        axis=2,
+    )
 
 
 def with_halo(value, sides, width):
@@ -34,7 +459,7 @@
     return opened * (moved - diffusion * (ahead_cells - behind_cells))
 
 
-def network(inputs, in_weight, in_bias, mid_weight, mid_bias, out_weight):
+def plain_network(inputs, in_weight, in_bias, mid_weight, mid_bias, out_weight):
     kinds, depth, rows, cols = inputs.shape
     cells = depth * rows * cols
     turns = math.gcd(cells, 8)
@@ -59,7 +484,7 @@
     return result.reshape(result.shape[0], depth, rows, cols)
 
 
-def body(
+def plain_body(
     tracers,
     east_speed,
     north_speed,
@@ -87,7 +512,7 @@
     for step in range(STEPS):
         padded = with_halo(as_sent(field), (("tile", 2),), 1).astype(field.dtype)
         inputs = field.astype(jnp.bfloat16)
-        local_sources = network(
+        local_sources = plain_network(
             lax.all_to_all(inputs, "tracer", split_axis=2, concat_axis=0, tiled=True),
             in_weight,
             in_bias,
@@ -102,6 +527,201 @@
         tendency = x_flux[:, :, :-1] - x_flux[:, :, 1:] + (y_flux[..., :-1] - y_flux[..., 1:])
         field = wet_cells[None] * (field + time_step * (tendency + sources.astype(jnp.float32)))
     return field
+
+
+def split_parts(value, count):
+    parts = []
+    for _ in range(count):
+        parts.append(value.astype(BF16))
+        value = value - parts[-1].astype(F32)
+    return parts
+
+
+def body(
+    tracers,
+    east_speed,
+    north_speed,
+    land_mask,
+    bottom_level,
+    in_weight,
+    in_bias,
+    mid_weight,
+    mid_bias,
+    out_weight,
+):
+    arguments = (
+        tracers,
+        east_speed,
+        north_speed,
+        land_mask,
+        bottom_level,
+        in_weight,
+        in_bias,
+        mid_weight,
+        mid_bias,
+        out_weight,
+    )
+    kinds, levels, length, columns = tracers.shape
+    tiles, group = lax.axis_size("tile"), lax.axis_size("tracer")
+    halves = 2
+    stacks = group // halves
+    rows = length // halves
+    own = lax.axis_index("tracer")
+    half, stack = own // stacks, own % stacks
+    all_kinds = kinds * group
+    thin = levels - stacks
+    parts = columns // 128
+
+    sent, place = kernel_call(
+        pack_kernel,
+        [
+            jax.ShapeDtypeStruct((halves, stacks, kinds, 2, rows, columns), BF16),
+            jax.ShapeDtypeStruct((length, columns), F32),
+        ],
+        [
+            pltpu.VMEM((length, columns), F32),
+            pltpu.VMEM((length * 32, 2 * columns), BF16),
+            pltpu.VMEM((2 * columns, columns), BF16),
+            pltpu.VMEM((parts, kinds * thin * length, 128), F32),
+            pltpu.VMEM((parts, kinds * stacks * length, 128), F32),
+        ],
+        2 * length * columns * columns * (32 + 64),
+        "pack",
+    )(tracers, land_mask, bottom_level)
+    sent = sent.reshape(group, kinds, 2, rows, columns)
+    cells = lax.all_to_all(sent, "tracer", split_axis=0, concat_axis=0, tiled=True)
+    cells = cells.reshape(all_kinds, 2, rows, columns)
+
+    east_speed, north_speed, land_mask, sent = lax.optimization_barrier(
+        (east_speed, north_speed, land_mask, sent)
+    )
+    depth = jnp.where(land_mask == 1, bottom_level, 0).astype(F32)
+    level_list = [stack, stacks + stack, 2 * stacks + (stack + stacks // 2) % stacks]
+
+    side, position = stack // (stacks // 2), stack % (stacks // 2)
+
+    def own_levels(value):
+        value = value.reshape(2 * levels // stacks, stacks // 2, length, columns)
+        value = lax.dynamic_slice_in_dim(value, position, 1, 1)[:, 0]
+        return jnp.where(
+            side == 0,
+            jnp.stack([value[0], value[2], value[5]]),
+            jnp.stack([value[1], value[3], value[4]]),
+        )
+
+    geometry = [own_levels(east_speed), own_levels(north_speed), depth[None], place[None]]
+
+    def at(tile, part, position):
+        return tile * group + part * stacks + position
+
+    across, within = [], []
+    for position in range(stacks):
+        for tile in range(tiles):
+            within.append((at(tile, 0, position), at(tile, 1, position)))
+            if tile + 1 < tiles:
+                across.append((at(tile, 1, position), at(tile + 1, 0, position)))
+    back = [(j, i) for i, j in across]
+    axes = ("tile", "tracer")
+    edge = jnp.concatenate(
+        [lax.dynamic_slice_in_dim(value, half * (length - 2), 2, 1) for value in geometry], axis=0
+    )
+    arrived = lax.ppermute(edge, axes, across + back)
+    arrived = [arrived[:3], arrived[3:6], arrived[6:7], arrived[7:8]]
+
+    def widened(value, outside):
+        return jnp.where(
+            half == 0,
+            jnp.concatenate([outside, value[:, : rows + 2]], axis=1),
+            jnp.concatenate([value[:, rows - 2 :], outside], axis=1),
+        )
+
+    east, north, wide_depth, wide_place = [widened(*pair) for pair in zip(geometry, arrived)]
+    factors = factors_of(east, north, wide_depth[0], jnp.stack(level_list).astype(F32)).reshape(
+        3 * (rows + 2), 8, columns
+    )
+    slots = jnp.arange(columns, dtype=jnp.int32).astype(F32)
+    table = (slots[None, :, None] == wide_place[0][:, None, :]).astype(BF16)
+
+    in_parts = jnp.stack(split_parts(0.5 * in_bias, 3) + [jnp.zeros(in_bias.shape, BF16)] * 13, axis=1)
+    weights = (
+        jnp.concatenate([(0.5 * in_weight.astype(F32)).astype(BF16).T, in_parts], axis=1),
+        (0.5 * mid_weight.astype(F32)).astype(BF16).T,
+        jnp.broadcast_to(0.5 * mid_bias[:, None], mid_bias.shape + (128,)),
+        out_weight.T,
+    )
+
+    hidden = in_weight.shape[1]
+    pieces = 2 * rows
+    per_piece = 2 * columns * hidden * (hidden + 2 * all_kinds)
+    turned, first, last = kernel_call(
+        functools.partial(turn_kernel, rows),
+        [
+            jax.ShapeDtypeStruct((pieces, all_kinds, columns), BF16),
+            jax.ShapeDtypeStruct((4, all_kinds, columns), BF16),
+            jax.ShapeDtypeStruct((4, all_kinds, columns), BF16),
+        ],
+        [pltpu.VMEM((parts, all_kinds * rows, 128), F32)],
+        1_000_000,
+        "turn",
+    )(cells)
+    top = lax.ppermute(last, axes, within + across)
+    bottom = lax.ppermute(first, axes, [(j, i) for i, j in within] + back)
+    partial, spread = kernel_call(
+        functools.partial(source_kernel, rows),
+        [
+            jax.ShapeDtypeStruct((3 * rows, all_kinds, columns), F32),
+            jax.ShapeDtypeStruct((2 * rows, all_kinds, columns), BF16),
+        ],
+        [pltpu.VMEM((rows // 2, all_kinds, 4 * columns), BF16)],
+        pieces * per_piece,
+        "sources",
+    )(turned, table, factors, *weights)
+    change = kernel_call(
+        functools.partial(step_kernel, rows),
+        jax.ShapeDtypeStruct(cells.shape, BF16),
+        [
+            pltpu.VMEM((3 * (rows + 2), all_kinds, columns), F32),
+            pltpu.VMEM((rows, all_kinds, columns), BF16),
+            pltpu.VMEM((rows // 2, all_kinds, 4 * columns), BF16),
+            pltpu.VMEM((parts, 2 * rows * all_kinds, 128), F32),
+        ],
+        pieces * per_piece,
+        "steps",
+    )(turned, spread, partial, top, bottom, table, factors, *weights)
+
+    depth, change = lax.optimization_barrier((depth, change))
+    level = jnp.arange(levels, dtype=jnp.int32).astype(F32)
+    count = jnp.sum((level[:, None, None] < depth[None]).astype(F32), axis=2)
+    deep = jnp.roll(count[2 * stacks :], -(stacks // 2), axis=0)
+    deep = jnp.flip(deep.reshape(stacks, length // 2, 2), axis=2).reshape(stacks, length)
+    fullest = jnp.full((8, 128), jnp.max(count[stacks : 2 * stacks] + deep))
+    step = 1
+    while step < tiles:
+        pairs = [(tile, tile ^ step) for tile in range(tiles)]
+        fullest = jnp.maximum(fullest, lax.ppermute(fullest, "tile", pairs))
+        step *= 2
+    excess = fullest[0, 0] > columns
+
+    change = change.reshape(group, kinds, 2, rows, columns)
+    change = lax.all_to_all(change, "tracer", split_axis=0, concat_axis=0, tiled=True)
+    change = change.reshape(halves, stacks, kinds, 2, rows, columns)
+
+    def finish(change, place, arguments):
+        return kernel_call(
+            finish_kernel,
+            jax.ShapeDtypeStruct(tracers.shape, F32),
+            [
+                pltpu.VMEM((parts, group * kinds * rows, 128), F32),
+                pltpu.VMEM((parts, kinds * thin * length, 128), F32),
+            ],
+            2 * length * columns * columns * 32,
+            "finish",
+        )(arguments[0], change, place, arguments[3], arguments[4])
+
+    def in_full(change, place, arguments):
+        return plain_body(*arguments)
+
+    return lax.cond(excess, in_full, finish, change, place, arguments)
 
 
 def solution(mesh):

time: 258 us -> 97.9 us (0.38)
  matrix products: 98.7 us -> 0 us
  Pallas kernels: 0 us -> 34.4 us
  local copies, waits for them, and re-layouts: 39.6 us -> 8.7 us
  blocking collectives: 28.8 us -> 0 us
  other arithmetic: 18.7 us -> 4.34 us
  waiting for transfers between devices: 30.7 us -> 16.8 us
  starting transfers between devices: 37.6 us -> 31.2 us
    dot_general x32 -> x0, matrix products: 98.7 us -> none  [the longest x16 56.4 us: one_block(): jnp.einsum('nh,ht->tn', second_hidden, out_weight, preferred_element_type...]
    pallas_call x0 -> x5, Pallas kernels: none -> 34.4 us  [the longest x1 14.6 us: body(): kernel_call(functools.partial(step_kernel, rows), jax.ShapeDtypeStruct(ce...]
    all_to_all x1 -> x0, blocking collectives: 28.8 us -> none  [body(): lax.all_to_all(inputs, 'tracer', split_axis=2, concat_axis=0, tiled=True)]
    all_to_all x3 -> x2, waiting for transfers between devices: 30.7 us -> 4.37 us  [the longest x1 4.37 us: body(): lax.all_to_all(sent, 'tracer', split_axis=0, concat_axis=0, tiled=True)]
    ppermute x6 -> x7, waiting for transfers between devices: 0.02 us -> 12.4 us  [the longest x4 10.4 us: body(): fullest = jnp.maximum(fullest, lax.ppermute(fullest, 'tile', pairs))]
    reshape x6 -> x1, local copies, waits for them, and re-layouts: 12 us -> 0.07 us  [body(): jnp.flip(deep.reshape(stacks, length // 2, 2), axis=2)]
    mul x8 -> x3, other arithmetic: 10.5 us -> 0.21 us  [the longest x1 0.16 us: factors_of(): left = opened * (jnp.minimum(flow, 0.0) - diffusion)]
    unnamed x56 -> x21, local copies, waits for them, and re-layouts: 11.7 us -> 3.43 us
  transfers between devices with their start and end apart: 9 -> 9, of which waited for: 3 -> 6; matrix products, arithmetic and copies ran while one was open for 36% -> 10% of each run, Pallas kernels for 0% -> 11%
where the time goes in v3:
time: 97.9 us; the launch traced here: 97 us
  Pallas kernels  34.4 us (35%)
  starting transfers between devices  31.2 us (32%)
  waiting for transfers between devices  16.8 us (17%)
  local copies, waits for them, and re-layouts  8.7 us (9%)
  other arithmetic  4.34 us (4%)
  between operations  1.25 us (1%)
    pallas_call x1, Pallas kernels, body(): kernel_call(functools.partial(step_kernel, rows), jax.ShapeDtypeStruct(ce...  14.6 us
    all_to_all x1, starting transfers between devices, body(): lax.all_to_all(sent, 'tracer', split_axis=0, concat_axis=0, tiled=True)  11.3 us
    pallas_call x1, Pallas kernels, body(): kernel_call(functools.partial(source_kernel, rows), [jax.ShapeDtypeStruct...  10.5 us
    ppermute x4, waiting for transfers between devices, body(): fullest = jnp.maximum(fullest, lax.ppermute(fullest, 'tile', pairs))  10.4 us
    ppermute x1, starting transfers between devices, body(): bottom = lax.ppermute(first, axes, [(j, i) for i, j in within] + back)  5.33 us
    pallas_call x1, Pallas kernels, body(): kernel_call(pack_kernel, [jax.ShapeDtypeStruct((halves, stacks, kinds, 2,...  5.21 us
    all_to_all x1, waiting for transfers between devices, body(): lax.all_to_all(sent, 'tracer', split_axis=0, concat_axis=0, tiled=True)  4.37 us
    all_to_all x1, starting transfers between devices, body(): lax.all_to_all(change, 'tracer', split_axis=0, concat_axis=0, tiled=True)  4.21 us
  transfers between devices with their start and end apart: 9, of which 6 were waited for; matrix products, arithmetic and copies ran while one was open for 10% of the time, Pallas kernels for 11%

profile of v3, /device:TPU:2, one launch (start us, length us, event | category | flops | bytes accessed | tf_op | source)
XLA Modules:
  0.0 97.0 jit_solution(10580453349741736740)
XLA Ops:
  0.0 5.2 %pack.1 = (bf16[2,8,2,2,16,256]{5,4,3,2,1,0:T(8,128)(2,1)}, f32[32,256]{1,0:T(8,128)S(1)}) custom-call(f32[2,24,32,256]{3,2,1,0:T(8,128)} %x_ref.1, s32[32,256]{1,0:T(8,128)} %land_ref.1, s32[32,256]{1,0:T(8,128)} %bottom_ref.1), custom_call_target="tpu_custom_call" | custom-call | flops 402653184 | bytes 4000000 | tf_op jit(solution)/shard_map/pack/pallas_call | solution.py:575
  5.2 11.3 %all-to-all-start.4 = ((bf16[16,2,2,16,256]{4,3,2,1,0:T(8,128)(2,1)}), bf16[16,2,2,16,256]{4,3,2,1,0:T(8,128)(2,1)S(1)}, u32[]{:S(2)}, u32[]{:S(2)}) async-start(bf16[16,2,2,16,256]{4,3,2,1,0:T(8,128)(2,1)} %bitcast.25), calls=%async_computation.4 | async-start | bytes 1048576 | tf_op jit(solution)/shard_map/all_to_all | solution.py:592
  16.7 0.9 dynamic-slice_bitcast_fusion.2
  17.6 0.9 dynamic-slice_bitcast_fusion.8
  18.6 4.2 %collective-permute-start.6 = (f32[8,2,256]{2,1,0:T(2,128)S(1)}, f32[8,2,256]{2,1,0:T(2,128)S(1)}, u32[]{:S(2)}, u32[]{:S(2)}) collective-permute-start(f32[8,2,256]{2,1,0:T(2,128)S(1)} %pad_maximum_fusion.9), channel_id=1, source_target_pairs={{8,16},{24,32},{40,48},{56,64},{72,80},{88,96},{104,112},{120,128}... | collective-permute-start | bytes 49160 | tf_op jit(solution)/shard_map/ppermute | solution.py:628
  23.1 0.9 fusion.29.mid_ref
  24.3 2.0 %collective-permute-done.6 = f32[8,2,256]{2,1,0:T(2,128)S(1)} collective-permute-done((f32[8,2,256]{2,1,0:T(2,128)S(1)}, f32[8,2,256]{2,1,0:T(2,128)S(1)}, u32[]{:S(2)}, u32[]{:S(2)}) %collective-permute-start.6) | collective-permute-done | bytes 16416 | tf_op jit(solution)/shard_map/ppermute | solution.py:628
  27.3 1.4 %stack.81.factors_ref = f32[54,8,256]{2,1,0:T(8,128)} concatenate(f32[54,1,256]{2,1,0:T(1,128)S(1)} %stack.74, f32[54,1,256]{2,1,0:T(1,128)S(1)} %stack.75, f32[54,1,256]{2,1,0:T(1,128)S(1)} %stack.76, f32[54,1,256]{2,1,0:T(1,128)S(1)} %stack.77, f32[54,1,256]{2,1,0:T(1,128)S(1)} %stack.78, f32[54,1,256]{2,1,0:T(1,128)S(1)} %stack.79, f32[54,1,256]{2,1,0:T(1,128)S(1)} %stack.80, ...), dimensions={1} | concatenate | bytes 884736 | tf_op jit(solution)/shard_map/stack | solution.py:425
  28.7 0.7 compare_convert_fusion.table_ref
  29.4 4.4 %all-to-all-done.4 = bf16[16,2,2,16,256]{4,3,2,1,0:T(8,128)(2,1)S(1)} async-done(((bf16[16,2,2,16,256]{4,3,2,1,0:T(8,128)(2,1)}), bf16[16,2,2,16,256]{4,3,2,1,0:T(8,128)(2,1)S(1)}, u32[]{:S(2)}, u32[]{:S(2)}) %all-to-all-start.4) | async-done | bytes 524320 | tf_op jit(solution)/shard_map/all_to_all | solution.py:592
  34.1 2.6 %collective-permute-start.7 = (bf16[4,32,256]{2,1,0:T(8,128)(2,1)S(1)}, bf16[4,32,256]{2,1,0:T(8,128)(2,1)S(1)}, u32[]{:S(2)}, u32[]{:S(2)}) collective-permute-start(bf16[4,32,256]{2,1,0:T(8,128)(2,1)S(1)} %get-tuple-element.157), channel_id=1, source_target_pairs={{0,8},{16,24},{32,40},{48,56},{64,72},{80,88},{96,104},{112,120},{... | collective-permute-start | bytes 196616 | tf_op jit(solution)/shard_map/ppermute | solution.py:667
  36.8 5.3 %collective-permute-start.8 = (bf16[4,32,256]{2,1,0:T(8,128)(2,1)S(1)}, bf16[4,32,256]{2,1,0:T(8,128)(2,1)S(1)}, u32[]{:S(2)}, u32[]{:S(2)}) collective-permute-start(bf16[4,32,256]{2,1,0:T(8,128)(2,1)S(1)} %get-tuple-element.158), channel_id=1, source_target_pairs={{8,0},{24,16},{40,32},{56,48},{72,64},{88,80},{104,96},{120,112},{... | collective-permute-start | bytes 196616 | tf_op jit(solution)/shard_map/ppermute | solution.py:668
  42.3 1.0 %copy-done = bf16[512,512]{1,0:T(8,128)(2,1)S(1)} copy-done((bf16[512,512]{1,0:T(8,128)(2,1)S(1)}, bf16[512,512]{1,0:T(8,128)(2,1)}, u32[]{:S(2)}) %copy-start) | copy-done | bytes 524312
  43.3 1.0 %copy-done.1 = f32[54,8,256]{2,1,0:T(8,128)S(1)} copy-done((f32[54,8,256]{2,1,0:T(8,128)S(1)}, f32[54,8,256]{2,1,0:T(8,128)}, u32[]{:S(2)}) %copy-start.1) | copy-done | bytes 442392
  44.3 10.5 %sources.1 = (f32[48,32,256]{2,1,0:T(8,128)S(1)}, bf16[32,32,256]{2,1,0:T(8,128)(2,1)S(1)}) custom-call(bf16[32,32,256]{2,1,0:T(8,128)(2,1)S(1)} %get-tuple-element.151.cells_ref, bf16[20,256,256]{2,1,0:T(8,128)(2,1)S(1)} %compare_convert_fusion.table_ref, f32[54,8,256]{2,1,0:T(8,128)S(1)} %copy-done.1, bf16[512,48]{1,0:T(8,128)(2,1)S(1)} %copy.112.in_ref, ...), custom_call_target="tpu_custom_call" | custom-call | flops 4831838208 | bytes 4000000 | tf_op jit(solution)/shard_map/sources/pallas_call | solution.py:669
  54.9 14.6 %steps.1 = bf16[32,2,16,256]{3,2,1,0:T(8,128)(2,1)} custom-call(bf16[32,32,256]{2,1,0:T(8,128)(2,1)S(1)} %get-tuple-element.151.cells_ref, bf16[32,32,256]{2,1,0:T(8,128)(2,1)S(1)} %get-tuple-element.155.spread_ref, f32[48,32,256]{2,1,0:T(8,128)S(1)} %get-tuple-element.156.partial_ref, bf16[4,32,256]{2,1,0:T(8,128)(2,1)S(1)} %collective-permute-done.7.top_ref, ...), custom_call_target="tpu_custom_call" | custom-call | flops 4831838208 | bytes 4000000 | tf_op jit(solution)/shard_map/steps/pallas_call | solution.py:679
  69.5 4.2 %all-to-all-start.5 = ((bf16[16,2,2,16,256]{4,3,2,1,0:T(8,128)(2,1)}), bf16[16,2,2,16,256]{4,3,2,1,0:T(8,128)(2,1)S(1)}, u32[]{:S(2)}, u32[]{:S(2)}) async-start(bf16[16,2,2,16,256]{4,3,2,1,0:T(8,128)(2,1)} %bitcast.60), calls=%async_computation.5 | async-start | bytes 1048576 | tf_op jit(solution)/shard_map/all_to_all | solution.py:706
  74.2 0.6 fusion.41
  74.8 0.6 broadcast_in_dim.25
  75.5 1.2 %collective-permute-done.9 = f32[8,128]{1,0:T(8,128)S(1)} collective-permute-done((f32[8,128]{1,0:T(8,128)S(1)}, f32[8,128]{1,0:T(8,128)S(1)}, u32[]{:S(2)}, u32[]{:S(2)}) %collective-permute-start.9) | collective-permute-done | bytes 4128 | tf_op jit(solution)/shard_map/ppermute | solution.py:701
  76.7 0.6 broadcast_maximum_fusion
  77.3 0.5 collective-permute-start.10
  77.9 3.3 %collective-permute-done.10 = f32[8,128]{1,0:T(8,128)S(1)} collective-permute-done((f32[8,128]{1,0:T(8,128)S(1)}, f32[8,128]{1,0:T(8,128)S(1)}, u32[]{:S(2)}, u32[]{:S(2)}) %collective-permute-start.10) | collective-permute-done | bytes 4128 | tf_op jit(solution)/shard_map/ppermute | solution.py:701
  81.2 0.6 fusion.61
  81.9 2.2 %collective-permute-start.11 = (f32[8,128]{1,0:T(8,128)S(1)}, f32[8,128]{1,0:T(8,128)S(1)}, u32[]{:S(2)}, u32[]{:S(2)}) collective-permute-start(f32[8,128]{1,0:T(8,128)S(1)} %fusion.61), channel_id=1, source_target_pairs={{0,64},{16,80},{32,96},{48,112},{64,0},{80,16},{96,32},{112,48},{1... | collective-permute-start | bytes 12296 | tf_op jit(solution)/shard_map/ppermute | solution.py:701
  84.1 3.0 %collective-permute-done.11 = f32[8,128]{1,0:T(8,128)S(1)} collective-permute-done((f32[8,128]{1,0:T(8,128)S(1)}, f32[8,128]{1,0:T(8,128)S(1)}, u32[]{:S(2)}, u32[]{:S(2)}) %collective-permute-start.11) | collective-permute-done | bytes 4128 | tf_op jit(solution)/shard_map/ppermute | solution.py:701
  87.1 0.7 collective-permute-start.12
  87.7 2.9 %collective-permute-done.12 = f32[8,128]{1,0:T(8,128)S(1)} collective-permute-done((f32[8,128]{1,0:T(8,128)S(1)}, f32[8,128]{1,0:T(8,128)S(1)}, u32[]{:S(2)}, u32[]{:S(2)}) %collective-permute-start.12) | collective-permute-done | bytes 4128 | tf_op jit(solution)/shard_map/ppermute | solution.py:701
  90.7 0.5 slice.309
  91.9 4.0 %conditional.1 = (f32[2,24,32,256]{3,2,1,0:T(8,128)S(1)}) conditional(s32[]{:T(128)} %bitcast.59, (f32[2,24,32,256]{3,2,1,0:T(8,128)}, bf16[16,2,2,16,256]{4,3,2,1,0:T(8,128)(2,1)S(1)}, f32[32,256]{1,0:T(8,128)S(1)}, s32[32,256]{1,0:T(8,128)S(1)}, s32[32,256]{1,0:T(8,128)S(1)}) %tuple.110, (s32[32,256]{1,0:T(8,128)S(1)}, s32[32,256]{1,0:T(8,128)S(1)}, ...), branch_computations={%region_2.3_spmd, %region_3.8_spmd} | conditional | flops 1856398592 | bytes 219619936 | solution.py:724
  91.9 3.7 %finish.1 = f32[2,24,32,256]{3,2,1,0:T(8,128)S(1)} custom-call(f32[2,24,32,256]{3,2,1,0:T(8,128)} %get-tuple-element.102.x_ref, bf16[2,8,2,2,16,256]{5,4,3,2,1,0:T(8,128)(2,1)S(1)} %bitcast.153, f32[32,256]{1,0:T(8,128)S(1)} %get-tuple-element.104.place_ref, s32[32,256]{1,0:T(8,128)S(1)} %get-tuple-element.105.land_ref, ...), custom_call_target="tpu_custom_call" | custom-call | flops 134217728 | bytes 4000000 | tf_op jit(solution)/shard_map/cond/branch_0_fun/finish/pallas_call | solution.py:710
  95.9 1.1 %copy-done.24 = f32[2,24,32,256]{3,2,1,0:T(8,128)} copy-done((f32[2,24,32,256]{3,2,1,0:T(8,128)}, f32[2,24,32,256]{3,2,1,0:T(8,128)S(1)}, u32[]{:S(2)}) %copy-start.24) | copy-done | bytes 1572888
  (74 shorter events, 2.6 us)
Async XLA Ops:
  0.0 16.6 %copy-start.26 = (s32[32,256]{1,0:T(8,128)S(1)}, s32[32,256]{1,0:T(8,128)}, u32[]{:S(2)}) copy-start(s32[32,256]{1,0:T(8,128)} %bottom_ref.1) | copy-start | bytes 98308
  0.0 16.6 %copy-start.29 = (s32[32,256]{1,0:T(8,128)S(1)}, s32[32,256]{1,0:T(8,128)}, u32[]{:S(2)}) copy-start(s32[32,256]{1,0:T(8,128)} %land_ref.1) | copy-start | bytes 98308
  5.2 17.6 %copy-start.37 = (bf16[32,512]{1,0:T(8,128)(2,1)S(1)}, bf16[32,512]{1,0:T(8,128)(2,1)}, u32[]{:S(2)}) copy-start(bf16[32,512]{1,0:T(8,128)(2,1)} %param.21) | copy-start | bytes 98308
  5.2 17.6 %copy-start.39 = (f32[512]{0:T(512)S(1)}, f32[512]{0:T(512)}, u32[]{:S(2)}) copy-start(f32[512]{0:T(512)} %param.22) | copy-start | bytes 6148
  5.2 17.7 %copy-start.31 = (bf16[512,512]{1,0:T(8,128)(2,1)S(1)}, bf16[512,512]{1,0:T(8,128)(2,1)}, u32[]{:S(2)}) copy-start(bf16[512,512]{1,0:T(8,128)(2,1)} %param.23) | copy-start | bytes 1572868
  5.2 28.5 %all-to-all-start.4 = ((bf16[16,2,2,16,256]{4,3,2,1,0:T(8,128)(2,1)}), bf16[16,2,2,16,256]{4,3,2,1,0:T(8,128)(2,1)S(1)}, u32[]{:S(2)}, u32[]{:S(2)}) async-start(bf16[16,2,2,16,256]{4,3,2,1,0:T(8,128)(2,1)} %bitcast.25), calls=%async_computation.4 | async-start | bytes 1048576 | tf_op jit(solution)/shard_map/all_to_all | solution.py:592
  18.5 5.5 %copy-start.40 = (f32[512]{0:T(512)S(1)}, f32[512]{0:T(512)}, u32[]{:S(2)}) copy-start(f32[512]{0:T(512)} %param.24) | copy-start | bytes 6148
  18.6 7.8 %collective-permute-start.6 = (f32[8,2,256]{2,1,0:T(2,128)S(1)}, f32[8,2,256]{2,1,0:T(2,128)S(1)}, u32[]{:S(2)}, u32[]{:S(2)}) collective-permute-start(f32[8,2,256]{2,1,0:T(2,128)S(1)} %pad_maximum_fusion.9), channel_id=1, source_target_pairs={{8,16},{24,32},{40,48},{56,64},{72,80},{88,96},{104,112},{120,128}... | collective-permute-start | bytes 49160 | tf_op jit(solution)/shard_map/ppermute | solution.py:628
  28.7 13.6 %copy-start.34 = (bf16[512,32]{0,1:T(8,128)(2,1)S(1)}, bf16[512,32]{0,1:T(8,128)(2,1)}, u32[]{:S(2)}) copy-start(bf16[512,32]{0,1:T(8,128)(2,1)} %param.25) | copy-start | bytes 98308
  34.1 20.7 %collective-permute-start.7 = (bf16[4,32,256]{2,1,0:T(8,128)(2,1)S(1)}, bf16[4,32,256]{2,1,0:T(8,128)(2,1)S(1)}, u32[]{:S(2)}, u32[]{:S(2)}) collective-permute-start(bf16[4,32,256]{2,1,0:T(8,128)(2,1)S(1)} %get-tuple-element.157), channel_id=1, source_target_pairs={{0,8},{16,24},{32,40},{48,56},{64,72},{80,88},{96,104},{112,120},{... | collective-permute-start | bytes 196616 | tf_op jit(solution)/shard_map/ppermute | solution.py:667
  36.8 18.1 %collective-permute-start.8 = (bf16[4,32,256]{2,1,0:T(8,128)(2,1)S(1)}, bf16[4,32,256]{2,1,0:T(8,128)(2,1)S(1)}, u32[]{:S(2)}, u32[]{:S(2)}) collective-permute-start(bf16[4,32,256]{2,1,0:T(8,128)(2,1)S(1)} %get-tuple-element.158), channel_id=1, source_target_pairs={{8,0},{24,16},{40,32},{56,48},{72,64},{88,80},{104,96},{120,112},{... | collective-permute-start | bytes 196616 | tf_op jit(solution)/shard_map/ppermute | solution.py:668
  42.2 1.0 %copy-start = (bf16[512,512]{1,0:T(8,128)(2,1)S(1)}, bf16[512,512]{1,0:T(8,128)(2,1)}, u32[]{:S(2)}) copy-start(bf16[512,512]{1,0:T(8,128)(2,1)} %fusion.29.mid_ref) | copy-start | bytes 1572868
  43.3 1.0 %copy-start.1 = (f32[54,8,256]{2,1,0:T(8,128)S(1)}, f32[54,8,256]{2,1,0:T(8,128)}, u32[]{:S(2)}) copy-start(f32[54,8,256]{2,1,0:T(8,128)} %stack.81.factors_ref) | copy-start | bytes 1327108
  69.5 22.4 %all-to-all-start.5 = ((bf16[16,2,2,16,256]{4,3,2,1,0:T(8,128)(2,1)}), bf16[16,2,2,16,256]{4,3,2,1,0:T(8,128)(2,1)S(1)}, u32[]{:S(2)}, u32[]{:S(2)}) async-start(bf16[16,2,2,16,256]{4,3,2,1,0:T(8,128)(2,1)} %bitcast.60), calls=%async_computation.5 | async-start | bytes 1048576 | tf_op jit(solution)/shard_map/all_to_all | solution.py:706
  75.4 1.3 %collective-permute-start.9 = (f32[8,128]{1,0:T(8,128)S(1)}, f32[8,128]{1,0:T(8,128)S(1)}, u32[]{:S(2)}, u32[]{:S(2)}) collective-permute-start(f32[8,128]{1,0:T(8,128)S(1)} %broadcast_in_dim.25), channel_id=1, source_target_pairs={{0,16},{16,0},{32,48},{48,32},{64,80},{80,64},{96,112},{112,96},{1... | collective-permute-start | bytes 12296 | tf_op jit(solution)/shard_map/ppermute | solution.py:701
  77.3 3.9 %collective-permute-start.10 = (f32[8,128]{1,0:T(8,128)S(1)}, f32[8,128]{1,0:T(8,128)S(1)}, u32[]{:S(2)}, u32[]{:S(2)}) collective-permute-start(f32[8,128]{1,0:T(8,128)S(1)} %broadcast_maximum_fusion), channel_id=1, source_target_pairs={{0,32},{16,48},{32,0},{48,16},{64,96},{80,112},{96,64},{112,80},{1... | collective-permute-start | bytes 12296 | tf_op jit(solution)/shard_map/ppermute | solution.py:701
  81.9 5.2 %collective-permute-start.11 = (f32[8,128]{1,0:T(8,128)S(1)}, f32[8,128]{1,0:T(8,128)S(1)}, u32[]{:S(2)}, u32[]{:S(2)}) collective-permute-start(f32[8,128]{1,0:T(8,128)S(1)} %fusion.61), channel_id=1, source_target_pairs={{0,64},{16,80},{32,96},{48,112},{64,0},{80,16},{96,32},{112,48},{1... | collective-permute-start | bytes 12296 | tf_op jit(solution)/shard_map/ppermute | solution.py:701
  87.1 3.6 %collective-permute-start.12 = (f32[8,128]{1,0:T(8,128)S(1)}, f32[8,128]{1,0:T(8,128)S(1)}, u32[]{:S(2)}, u32[]{:S(2)}) collective-permute-start(f32[8,128]{1,0:T(8,128)S(1)} %max.31), channel_id=1, source_target_pairs={{0,128},{16,144},{32,160},{48,176},{64,192},{80,208},{96,224},{112... | collective-permute-start | bytes 12296 | tf_op jit(solution)/shard_map/ppermute | solution.py:701
  95.8 1.1 %copy-start.24 = (f32[2,24,32,256]{3,2,1,0:T(8,128)}, f32[2,24,32,256]{3,2,1,0:T(8,128)S(1)}, u32[]{:S(2)}) copy-start(f32[2,24,32,256]{3,2,1,0:T(8,128)S(1)} %get-tuple-element.559) | copy-start | bytes 4718596

commit v4 on v3

--- a/solution.py
+++ b/solution.py
@@ -79,9 +79,30 @@
         ref[part, pl.ds(start, size, stride=stride), :] = value[:, part * 128 : (part + 1) * 128]
 
 
-def pack_kernel(x_ref, land_ref, bottom_ref, sent_ref, place_ref, depth_ref, counts, table, held, packed):
-    kinds, levels, length, width = x_ref.shape
+def pack_kernel(
+    x_ref, land_ref, bottom_ref, sent_ref, place_ref, depth_ref, counts, table, held, plain, packed, arrivals
+):
+    kinds, _, width = x_ref.shape
+    length = land_ref.shape[0]
     halves, stacks, _, _, rows, _ = sent_ref.shape
+    levels = x_ref.shape[1] // length
+    thin = levels - stacks
+    parts = held.shape[0]
+    copies = []
+    for kind in range(kinds):
+        for part in range(parts):
+            copies.append(
+                pltpu.make_async_copy(
+                    x_ref.at[kind, pl.ds(stacks * length, thin * length), pl.ds(part * 128, 128)],
+                    held.at[part, pl.ds(kind * thin * length, thin * length)],
+                    arrivals.at[len(copies)],
+                )
+            )
+    copies.append(
+        pltpu.make_async_copy(x_ref.at[:, pl.ds(0, stacks * length)], plain, arrivals.at[len(copies)])
+    )
+    for copy in copies:
+        copy.start()
     depth_ref[...] = jnp.where(land_ref[...] == 1, bottom_ref[...], 0).astype(F32)
     bins = 32
     value = lax.broadcasted_iota(jnp.int32, (bins, width), 0).astype(F32)
@@ -99,11 +120,8 @@
         place = jnp.sum(here, axis=0, keepdims=True)
         place_ref[row : row + 1] = place if row % 2 == 0 else (width - 1.0) - place
 
-    thin = levels - stacks
-    for kind in range(kinds):
-        for part in range(held.shape[0]):
-            block = x_ref[kind, stacks:, :, part * 128 : (part + 1) * 128]
-            held[part, kind * thin * length : (kind + 1) * thin * length] = block.reshape(thin * length, 128)
+    for copy in copies[:-1]:
+        copy.wait()
     level = stacks + lax.broadcasted_iota(jnp.int32, (thin, width), 0).astype(F32)
 
     def body(i, _):
@@ -124,19 +142,26 @@
                 put_halves(packed, kind * stacks * length + 2 * i + k, stacks, length, value)
         return 0
 
-    lax.fori_loop(0, length // 2, body, 0, unroll=2)
+    lax.fori_loop(0, length // 2, body, 0, unroll=8)
+    copies[-1].wait()
     for half in range(halves):
         inside = slice(half * rows, (half + 1) * rows)
         for kind in range(kinds):
-            sent_ref[half, :, kind, 0] = x_ref[kind, :stacks, inside].astype(BF16)
+            block = plain[kind].reshape(stacks, length, width)
+            sent_ref[half, :, kind, 0] = block[:, inside].astype(BF16)
             for part in range(packed.shape[0]):
                 at = kind * stacks * length
                 block = packed[part, at : at + stacks * length].reshape(stacks, length, 128)
                 sent_ref[half, :, kind, 1, :, part * 128 : (part + 1) * 128] = block[:, inside].astype(BF16)
 
 
-def finish_kernel(x_ref, arrived_ref, place_ref, land_ref, bottom_ref, result_ref, held, spread):
+def finish_kernel(
+    x_ref, arrived_ref, place_ref, land_ref, bottom_ref, result_ref, held, spread, field, arrivals, leaving
+):
     kinds, levels, length, width = x_ref.shape
+    copies = [pltpu.make_async_copy(x_ref.at[kind], field.at[kind], arrivals.at[kind]) for kind in range(kinds)]
+    for copy in copies:
+        copy.start()
     halves, stacks, _, _, rows, _ = arrived_ref.shape
     thin = levels - stacks
     each = stacks * kinds * rows
@@ -164,9 +189,11 @@
                 put_halves(spread, at + stacks * length, stacks, length, deep)
         return 0
 
-    lax.fori_loop(0, length // 2, body, 0, unroll=2)
+    lax.fori_loop(0, length // 2, body, 0, unroll=8)
     depth = jnp.where(land_ref[...] == 1, bottom_ref[...], 0)
+    sent = []
     for kind in range(kinds):
+        copies[kind].wait()
         for level in range(levels):
             if level < stacks:
                 change = jnp.concatenate(
@@ -177,31 +204,57 @@
                 change = jnp.concatenate(
                     [spread[part, at : at + length] for part in range(spread.shape[0])], axis=1
                 )
-            result_ref[kind, level] = jnp.where(level < depth, x_ref[kind, level] + change, 0.0)
+            field[kind, level] = jnp.where(level < depth, field[kind, level] + change, 0.0)
+            if level % stacks == stacks - 1:
+                block = pl.ds(level + 1 - stacks, stacks)
+                sent.append(
+                    pltpu.make_async_copy(
+                        field.at[kind, block], result_ref.at[kind, block], leaving.at[len(sent)]
+                    )
+                )
+                sent[-1].start()
+    for copy in sent:
+        copy.wait()
 
 
 def source_kernel(
-    rows, cells_ref, table_ref, factors_ref, in_ref, mid_ref, bias_ref, out_ref, middle_ref, spread_ref, held
+    rows,
+    cells_ref,
+    table_ref,
+    factors_hbm,
+    in_ref,
+    mid_hbm,
+    bias_ref,
+    out_ref,
+    middle_ref,
+    spread_ref,
+    held,
+    factors_ref,
+    mid_ref,
+    arrivals,
 ):
     _, kinds, width = cells_ref.shape
     ahead = rows + 2
     weights = (in_ref, mid_ref, bias_ref, out_ref)
+    copies = [
+        pltpu.make_async_copy(mid_hbm, mid_ref, arrivals.at[0]),
+        pltpu.make_async_copy(factors_hbm, factors_ref, arrivals.at[1]),
+    ]
+    for copy in copies:
+        copy.start()
 
     def cell(level, row):
         if level == 0:
             return cells_ref[row]
         return spread_ref[(level - 1) * rows + row]
 
-    def spread_out(i, _):
+    def spread_out(i):
         row = 2 * i
         cells = jnp.concatenate([cells_ref[rows + row], cells_ref[rows + row + 1]], axis=0)
         for k in range(2):
             value = nn(cells, table_ref[row + 2 + k]).astype(BF16)
             spread_ref[row + k] = value[k * kinds : (k + 1) * kinds]
             spread_ref[rows + row + k] = value[(1 - k) * kinds : (2 - k) * kinds]
-        return 0
-
-    lax.fori_loop(0, rows // 2, spread_out, 0, unroll=2)
 
     def sources(i):
         row = 2 * i
@@ -244,7 +297,11 @@
         sources(i)
         return 0
 
+    for i in range(rows // 2):
+        spread_out(i)
+    copies[0].wait()
     sources(0)
+    copies[1].wait()
     lax.fori_loop(1, rows // 2, body, 0)
     move(rows // 2 - 1)
 
@@ -275,6 +332,82 @@
     def run(cells):
         return network(jnp.concatenate(cells, axis=1), *[ref[...] for ref in weights]).astype(BF16)
 
+    for level in range(3):
+        for row in range(1, rows - 1):
+            middle[level * ahead + 1 + row] = partial_ref[level * rows + row]
+
+
+    def put_together(row, thin):
+        values = [nt(thin[k], table_ref[row + 2 + k]) for k in range(2)]
+        return [values[k][:kinds] + values[1 - k][kinds:] for k in range(2)]
+
+    def pack(i):
+        row = 2 * i
+        thin = [
+            jnp.concatenate(
+                [middle[level * ahead + 1 + row + k].astype(BF16) for level in (1, 2)], axis=0
+            )
+            for k in range(2)
+        ]
+        values = put_together(row, thin)
+        for k in range(2):
+            packed[row + k] = values[k].astype(BF16)
+
+    def sources_of(i):
+        row = 2 * i
+        cells = [middle[1 + row + k].astype(BF16) for k in range(2)]
+        held[i] = run(cells + [packed[row], packed[row + 1]])
+
+    def move(i):
+        row = 2 * i
+        result = held[i]
+        thin_sources = jnp.concatenate(
+            [result[:, 2 * width : 3 * width], result[:, 3 * width :]], axis=0
+        )
+        changes = []
+        for k in range(2):
+            value = nn(thin_sources, table_ref[row + 2 + k])
+            pieces = [
+                result[:, k * width : (k + 1) * width].astype(F32),
+                value[k * kinds : (k + 1) * kinds],
+                value[(1 - k) * kinds : (2 - k) * kinds],
+            ]
+            for level in range(3):
+                at = level * ahead + 1 + row + k
+                factors = factors_ref[at]
+                value = advance(
+                    middle[at],
+                    middle[at - 1],
+                    middle[at + 1],
+                    pieces[level],
+                    factors,
+                    factors[1:2],
+                    factors[2:3],
+                )
+                if level == 0:
+                    first = cells_ref[row + k]
+                else:
+                    first = spread_ref[(level - 1) * rows + row + k]
+                changes.append(value - factors[6:7] * first.astype(F32))
+        thin = [
+            jnp.concatenate([changes[3 * k + 1].astype(BF16), changes[3 * k + 2].astype(BF16)], axis=0)
+            for k in range(2)
+        ]
+        values = put_together(row, thin)
+        for k in range(2):
+            put_halves(scratch, row + k, kinds, rows, changes[3 * k])
+            put_halves(scratch, rows * kinds + row + k, kinds, rows, values[k])
+
+    def turn(i):
+        return (i + 1) % (rows // 2)
+
+    def body(i, _):
+        move(turn(i - 1))
+        sources_of(turn(i))
+        return 0
+
+    for i in range(1, rows // 2 - 1):
+        pack(i)
     edges = [
         [top_ref[1], top_ref[2], top_ref[3]],
         [bottom_ref[0], bottom_ref[2], bottom_ref[3]],
@@ -317,92 +450,31 @@
             )
             row = level * ahead + 1 + k * (rows - 1)
             middle[row] = partial_ref[inside] + factors_ref[row][1 + k : 2 + k] * own
-    for level in range(3):
-        for row in range(1, rows - 1):
-            middle[level * ahead + 1 + row] = partial_ref[level * rows + row]
-
-    def put_together(row, thin):
-        values = [nt(thin[k], table_ref[row + 2 + k]) for k in range(2)]
-        return [values[k][:kinds] + values[1 - k][kinds:] for k in range(2)]
-
-    def pack(i, _):
-        row = 2 * i
-        thin = [
-            jnp.concatenate(
-                [middle[level * ahead + 1 + row + k].astype(BF16) for level in (1, 2)], axis=0
-            )
-            for k in range(2)
-        ]
-        values = put_together(row, thin)
-        for k in range(2):
-            packed[row + k] = values[k].astype(BF16)
-        return 0
-
-    lax.fori_loop(0, rows // 2, pack, 0, unroll=2)
-
-    def sources_of(i):
-        row = 2 * i
-        cells = [middle[1 + row + k].astype(BF16) for k in range(2)]
-        held[i] = run(cells + [packed[row], packed[row + 1]])
-
-    def move(i):
-        row = 2 * i
-        result = held[i]
-        thin_sources = jnp.concatenate(
-            [result[:, 2 * width : 3 * width], result[:, 3 * width :]], axis=0
-        )
-        changes = []
-        for k in range(2):
-            value = nn(thin_sources, table_ref[row + 2 + k])
-            pieces = [
-                result[:, k * width : (k + 1) * width].astype(F32),
-                value[k * kinds : (k + 1) * kinds],
-                value[(1 - k) * kinds : (2 - k) * kinds],
-            ]
-            for level in range(3):
-                at = level * ahead + 1 + row + k
-                factors = factors_ref[at]
-                value = advance(
-                    middle[at],
-                    middle[at - 1],
-                    middle[at + 1],
-                    pieces[level],
-                    factors,
-                    factors[1:2],
-                    factors[2:3],
-                )
-                if level == 0:
-                    first = cells_ref[row + k]
-                else:
-                    first = spread_ref[(level - 1) * rows + row + k]
-                changes.append(value - factors[6:7] * first.astype(F32))
-        thin = [
-            jnp.concatenate([changes[3 * k + 1].astype(BF16), changes[3 * k + 2].astype(BF16)], axis=0)
-            for k in range(2)
-        ]
-        values = put_together(row, thin)
-        for k in range(2):
-            put_halves(scratch, row + k, kinds, rows, changes[3 * k])
-            put_halves(scratch, rows * kinds + row + k, kinds, rows, values[k])
-
-    def body(i, _):
-        move(i - 1)
-        sources_of(i)
-        return 0
-
-    sources_of(0)
+    sources_of(1)
+    pack(0)
+    pack(rows // 2 - 1)
     lax.fori_loop(1, rows // 2, body, 0)
-    move(rows // 2 - 1)
+    move(0)
     for level in range(2):
         for part in range(scratch.shape[0]):
             block = scratch[part, level * rows * kinds : (level + 1) * rows * kinds, :]
             change_ref[:, level, :, part * 128 : (part + 1) * 128] = block.reshape(kinds, rows, 128).astype(BF16)
 
 
-def kernel_call(kernel, outs, scratch, flops, name):
+HBM = pltpu.HBM
+
+
+def kernel_call(kernel, outs, scratch, flops, name, places=None, result_places=None):
+    def specs(given):
+        return [pl.BlockSpec(memory_space=place or pltpu.VMEM) for place in given]
+
+    spaces = {} if places is None else {"in_specs": specs(places)}
+    if result_places is not None:
+        spaces["out_specs"] = specs(result_places)[0]
     return pl.pallas_call(
         kernel,
         out_shape=outs,
+        **spaces,
         scratch_shapes=scratch,
         cost_estimate=pl.CostEstimate(flops=flops, bytes_accessed=4_000_000, transcendentals=0),
         compiler_params=pltpu.CompilerParams(vmem_limit_bytes=24 * 2**20),
@@ -583,11 +655,14 @@
             pltpu.VMEM((length * 32, 2 * columns), BF16),
             pltpu.VMEM((2 * columns, columns), BF16),
             pltpu.VMEM((parts, kinds * thin * length, 128), F32),
+            pltpu.VMEM((kinds, stacks * length, columns), F32),
             pltpu.VMEM((parts, kinds * stacks * length, 128), F32),
+            pltpu.SemaphoreType.DMA((kinds * parts + 1,)),
         ],
         2 * length * columns * columns * (32 + 64),
         "pack",
-    )(tracers, land_mask, bottom_level)
+        [HBM, None, None],
+    )(tracers.reshape(kinds, levels * length, columns), land_mask, bottom_level)
     sent = sent.reshape(group, kinds, 2, rows, columns)
     cells = lax.all_to_all(sent, "tracer", split_axis=0, concat_axis=0, tiled=True)
     cells = cells.reshape(all_kinds, 2, rows, columns)
@@ -672,9 +747,15 @@
             jax.ShapeDtypeStruct((3 * rows, all_kinds, columns), F32),
             jax.ShapeDtypeStruct((2 * rows, all_kinds, columns), BF16),
         ],
-        [pltpu.VMEM((rows // 2, all_kinds, 4 * columns), BF16)],
+        [
+            pltpu.VMEM((rows // 2, all_kinds, 4 * columns), BF16),
+            pltpu.VMEM(factors.shape, F32),
+            pltpu.VMEM(mid_weight.shape, BF16),
+            pltpu.SemaphoreType.DMA((2,)),
+        ],
         pieces * per_piece,
         "sources",
+        [None, None, HBM, None, HBM, None, None],
     )(turned, table, factors, *weights)
     change = kernel_call(
         functools.partial(step_kernel, rows),
@@ -695,11 +776,12 @@
     deep = jnp.roll(count[2 * stacks :], -(stacks // 2), axis=0)
     deep = jnp.flip(deep.reshape(stacks, length // 2, 2), axis=2).reshape(stacks, length)
     fullest = jnp.full((8, 128), jnp.max(count[stacks : 2 * stacks] + deep))
-    step = 1
-    while step < tiles:
-        pairs = [(tile, tile ^ step) for tile in range(tiles)]
-        fullest = jnp.maximum(fullest, lax.ppermute(fullest, "tile", pairs))
-        step *= 2
+    for step in (1, tiles // 4):
+        others = []
+        for times in (1, 2, 3):
+            pairs = [(tile, tile ^ (step * times)) for tile in range(tiles)]
+            others.append(lax.ppermute(fullest, "tile", pairs))
+        fullest = functools.reduce(jnp.maximum, others, fullest)
     excess = fullest[0, 0] > columns
 
     change = change.reshape(group, kinds, 2, rows, columns)
@@ -713,9 +795,14 @@
             [
                 pltpu.VMEM((parts, group * kinds * rows, 128), F32),
                 pltpu.VMEM((parts, kinds * thin * length, 128), F32),
+                pltpu.VMEM(tracers.shape, F32),
+                pltpu.SemaphoreType.DMA((kinds,)),
+                pltpu.SemaphoreType.DMA((kinds * levels // stacks,)),
             ],
             2 * length * columns * columns * 32,
             "finish",
+            [HBM, None, None, None, None],
+            [HBM],
         )(arguments[0], change, place, arguments[3], arguments[4])
 
     def in_full(change, place, arguments):

time: 97.9 us -> 93.7 us (0.957)
  waiting for transfers between devices: 16.8 us -> 13 us
  starting transfers between devices: 31.2 us -> 34.7 us
  Pallas kernels: 34.4 us -> 31.3 us
    ppermute x4 -> x6, waiting for transfers between devices: 10.4 us -> 5.52 us  [body(): others.append(lax.ppermute(fullest, 'tile', pairs))]
    ppermute x4 -> x6, starting transfers between devices: 3.54 us -> 7.04 us  [body(): others.append(lax.ppermute(fullest, 'tile', pairs))]
    pallas_call x1, Pallas kernels: 3.7 us -> 1.91 us  [finish(): kernel_call(finish_kernel, jax.ShapeDtypeStruct(tracers.shape, F32), [plt...]
    all_to_all x1, waiting for transfers between devices: 0.01 us -> 1.05 us  [body(): lax.all_to_all(change, 'tracer', split_axis=0, concat_axis=0, tiled=True)]
  transfers between devices with their start and end apart: 9 -> 11, of which waited for: 6 -> 8; matrix products, arithmetic and copies ran while one was open for 10% -> 10% of each run, Pallas kernels for 11% -> 11%
where the time goes in v4:
time: 93.7 us; the launch traced here: 92.8 us
  starting transfers between devices  34.7 us (37%)
  Pallas kernels  31.3 us (33%)
  waiting for transfers between devices  13 us (14%)
  local copies, waits for them, and re-layouts  8.69 us (9%)
  other arithmetic  3.69 us (4%)
  between operations  1.25 us (1%)
    pallas_call x1, Pallas kernels, body(): kernel_call(functools.partial(step_kernel, rows), jax.ShapeDtypeStruct(ce...  13.9 us
    all_to_all x1, starting transfers between devices, body(): lax.all_to_all(sent, 'tracer', split_axis=0, concat_axis=0, tiled=True)  11.3 us
    pallas_call x1, Pallas kernels, body(): kernel_call(functools.partial(source_kernel, rows), [jax.ShapeDtypeStruct...  10.5 us
    ppermute x6, starting transfers between devices, body(): others.append(lax.ppermute(fullest, 'tile', pairs))  7.04 us
    ppermute x6, waiting for transfers between devices, body(): others.append(lax.ppermute(fullest, 'tile', pairs))  5.52 us
    ppermute x1, starting transfers between devices, body(): bottom = lax.ppermute(first, axes, [(j, i) for i, j in within] + back)  5.35 us
    pallas_call x1, Pallas kernels, body(): kernel_call(pack_kernel, [jax.ShapeDtypeStruct((halves, stacks, kinds, 2,...  4.54 us
    all_to_all x1, waiting for transfers between devices, body(): lax.all_to_all(sent, 'tracer', split_axis=0, concat_axis=0, tiled=True)  4.39 us
  transfers between devices with their start and end apart: 11, of which 8 were waited for; matrix products, arithmetic and copies ran while one was open for 10% of the time, Pallas kernels for 11%

profile of v4, /device:TPU:2, one launch (start us, length us, event | category | flops | bytes accessed | tf_op | source)
XLA Modules:
  0.0 92.8 jit_solution(16529311742660532075)
XLA Ops:
  0.0 4.5 %pack.1 = (bf16[2,8,2,2,16,256]{5,4,3,2,1,0:T(8,128)(2,1)}, f32[32,256]{1,0:T(8,128)S(1)}) custom-call(f32[2,768,256]{2,1,0:T(8,128)} %bitcast.142, s32[32,256]{1,0:T(8,128)} %land_ref.1, s32[32,256]{1,0:T(8,128)} %bottom_ref.1), custom_call_target="tpu_custom_call" | custom-call | flops 402653184 | bytes 4000000 | tf_op jit(solution)/shard_map/pack/pallas_call | solution.py:647
  4.6 11.3 %all-to-all-start.4 = ((bf16[16,2,2,16,256]{4,3,2,1,0:T(8,128)(2,1)}), bf16[16,2,2,16,256]{4,3,2,1,0:T(8,128)(2,1)S(1)}, u32[]{:S(2)}, u32[]{:S(2)}) async-start(bf16[16,2,2,16,256]{4,3,2,1,0:T(8,128)(2,1)} %bitcast.26), calls=%async_computation.4 | async-start | bytes 1048576 | tf_op jit(solution)/shard_map/all_to_all | solution.py:667
  16.1 0.9 dynamic-slice_bitcast_fusion.2
  16.9 0.9 dynamic-slice_bitcast_fusion.8
  17.9 4.1 %collective-permute-start.6 = (f32[8,2,256]{2,1,0:T(2,128)S(1)}, f32[8,2,256]{2,1,0:T(2,128)S(1)}, u32[]{:S(2)}, u32[]{:S(2)}) collective-permute-start(f32[8,2,256]{2,1,0:T(2,128)S(1)} %pad_maximum_fusion.9), channel_id=1, source_target_pairs={{8,16},{24,32},{40,48},{56,64},{72,80},{88,96},{104,112},{120,128}... | collective-permute-start | bytes 49160 | tf_op jit(solution)/shard_map/ppermute | solution.py:703
  22.5 0.9 fusion.29.mid_hbm.mid_ref
  23.7 2.0 %collective-permute-done.6 = f32[8,2,256]{2,1,0:T(2,128)S(1)} collective-permute-done((f32[8,2,256]{2,1,0:T(2,128)S(1)}, f32[8,2,256]{2,1,0:T(2,128)S(1)}, u32[]{:S(2)}, u32[]{:S(2)}) %collective-permute-start.6) | collective-permute-done | bytes 16416 | tf_op jit(solution)/shard_map/ppermute | solution.py:703
  26.7 1.4 %stack.81.factors_hbm.factors_ref = f32[54,8,256]{2,1,0:T(8,128)} concatenate(f32[54,1,256]{2,1,0:T(1,128)S(1)} %stack.74, f32[54,1,256]{2,1,0:T(1,128)S(1)} %stack.75, f32[54,1,256]{2,1,0:T(1,128)S(1)} %stack.76, f32[54,1,256]{2,1,0:T(1,128)S(1)} %stack.77, f32[54,1,256]{2,1,0:T(1,128)S(1)} %stack.78, f32[54,1,256]{2,1,0:T(1,128)S(1)} %stack.79, f32[54,1,256]{2,1,0:T(1,128)S(1)} %stack.80, ...), dimensions={1} | concatenate | bytes 884736 | tf_op jit(solution)/shard_map/stack | solution.py:497
  28.1 0.7 compare_convert_fusion.table_ref
  28.8 4.4 %all-to-all-done.4 = bf16[16,2,2,16,256]{4,3,2,1,0:T(8,128)(2,1)S(1)} async-done(((bf16[16,2,2,16,256]{4,3,2,1,0:T(8,128)(2,1)}), bf16[16,2,2,16,256]{4,3,2,1,0:T(8,128)(2,1)S(1)}, u32[]{:S(2)}, u32[]{:S(2)}) %all-to-all-start.4) | async-done | bytes 524320 | tf_op jit(solution)/shard_map/all_to_all | solution.py:667
  33.5 2.6 %collective-permute-start.7 = (bf16[4,32,256]{2,1,0:T(8,128)(2,1)S(1)}, bf16[4,32,256]{2,1,0:T(8,128)(2,1)S(1)}, u32[]{:S(2)}, u32[]{:S(2)}) collective-permute-start(bf16[4,32,256]{2,1,0:T(8,128)(2,1)S(1)} %get-tuple-element.157), channel_id=1, source_target_pairs={{0,8},{16,24},{32,40},{48,56},{64,72},{80,88},{96,104},{112,120},{... | collective-permute-start | bytes 196616 | tf_op jit(solution)/shard_map/ppermute | solution.py:742
  36.1 5.4 %collective-permute-start.8 = (bf16[4,32,256]{2,1,0:T(8,128)(2,1)S(1)}, bf16[4,32,256]{2,1,0:T(8,128)(2,1)S(1)}, u32[]{:S(2)}, u32[]{:S(2)}) collective-permute-start(bf16[4,32,256]{2,1,0:T(8,128)(2,1)S(1)} %get-tuple-element.158), channel_id=1, source_target_pairs={{8,0},{24,16},{40,32},{56,48},{72,64},{88,80},{104,96},{120,112},{... | collective-permute-start | bytes 196616 | tf_op jit(solution)/shard_map/ppermute | solution.py:743
  41.7 1.0 %copy-done = bf16[512,512]{1,0:T(8,128)(2,1)S(1)} copy-done((bf16[512,512]{1,0:T(8,128)(2,1)S(1)}, bf16[512,512]{1,0:T(8,128)(2,1)}, u32[]{:S(2)}) %copy-start) | copy-done | bytes 524312
  42.7 1.0 %copy-done.1 = f32[54,8,256]{2,1,0:T(8,128)S(1)} copy-done((f32[54,8,256]{2,1,0:T(8,128)S(1)}, f32[54,8,256]{2,1,0:T(8,128)}, u32[]{:S(2)}) %copy-start.1) | copy-done | bytes 442392
  43.7 10.5 %sources.1 = (f32[48,32,256]{2,1,0:T(8,128)S(1)}, bf16[32,32,256]{2,1,0:T(8,128)(2,1)S(1)}) custom-call(bf16[32,32,256]{2,1,0:T(8,128)(2,1)S(1)} %get-tuple-element.151.cells_ref, bf16[20,256,256]{2,1,0:T(8,128)(2,1)S(1)} %compare_convert_fusion.table_ref, f32[54,8,256]{2,1,0:T(8,128)S(1)} %copy-done.1, bf16[512,48]{1,0:T(8,128)(2,1)S(1)} %copy.112.in_ref, ...), custom_call_target="tpu_custom_call" | custom-call | flops 4831838208 | bytes 4000000 | tf_op jit(solution)/shard_map/sources/pallas_call | solution.py:744
  54.2 13.9 %steps.1 = bf16[32,2,16,256]{3,2,1,0:T(8,128)(2,1)} custom-call(bf16[32,32,256]{2,1,0:T(8,128)(2,1)S(1)} %get-tuple-element.151.cells_ref, bf16[32,32,256]{2,1,0:T(8,128)(2,1)S(1)} %get-tuple-element.155.spread_ref, f32[48,32,256]{2,1,0:T(8,128)S(1)} %get-tuple-element.156.partial_ref, bf16[4,32,256]{2,1,0:T(8,128)(2,1)S(1)} %collective-permute-done.7.top_ref, ...), custom_call_target="tpu_custom_call" | custom-call | flops 4831838208 | bytes 4000000 | tf_op jit(solution)/shard_map/steps/pallas_call | solution.py:760
  68.2 4.2 %all-to-all-start.5 = ((bf16[16,2,2,16,256]{4,3,2,1,0:T(8,128)(2,1)}), bf16[16,2,2,16,256]{4,3,2,1,0:T(8,128)(2,1)S(1)}, u32[]{:S(2)}, u32[]{:S(2)}) async-start(bf16[16,2,2,16,256]{4,3,2,1,0:T(8,128)(2,1)} %bitcast.61), calls=%async_computation.5 | async-start | bytes 1048576 | tf_op jit(solution)/shard_map/all_to_all | solution.py:788
  72.8 0.6 fusion.41
  74.2 1.2 %collective-permute-start.10 = (f32[8,128]{1,0:T(8,128)S(1)}, f32[8,128]{1,0:T(8,128)S(1)}, u32[]{:S(2)}, u32[]{:S(2)}) collective-permute-start(f32[8,128]{1,0:T(8,128)S(1)} %broadcast_in_dim.25), channel_id=1, source_target_pairs={{0,32},{16,48},{32,0},{48,16},{64,96},{80,112},{96,64},{112,80},{1... | collective-permute-start | bytes 12296 | tf_op jit(solution)/shard_map/ppermute | solution.py:783
  75.4 0.7 collective-permute-start.9
  76.1 1.2 %collective-permute-done.11 = f32[8,128]{1,0:T(8,128)S(1)} collective-permute-done((f32[8,128]{1,0:T(8,128)S(1)}, f32[8,128]{1,0:T(8,128)S(1)}, u32[]{:S(2)}, u32[]{:S(2)}) %collective-permute-start.11) | collective-permute-done | bytes 4128 | tf_op jit(solution)/shard_map/ppermute | solution.py:783
  77.2 0.7 collective-permute-done.10
  77.9 0.6 maximum_maximum_fusion.1
  78.5 2.3 %collective-permute-start.14 = (f32[8,128]{1,0:T(8,128)S(1)}, f32[8,128]{1,0:T(8,128)S(1)}, u32[]{:S(2)}, u32[]{:S(2)}) collective-permute-start(f32[8,128]{1,0:T(8,128)S(1)} %maximum_maximum_fusion.1), channel_id=1, source_target_pairs={{0,192},{16,208},{32,224},{48,240},{64,128},{80,144},{96,160},{112... | collective-permute-start | bytes 12296 | tf_op jit(solution)/shard_map/ppermute | solution.py:783
  80.8 1.3 %collective-permute-start.13 = (f32[8,128]{1,0:T(8,128)S(1)}, f32[8,128]{1,0:T(8,128)S(1)}, u32[]{:S(2)}, u32[]{:S(2)}) collective-permute-start(f32[8,128]{1,0:T(8,128)S(1)} %maximum_maximum_fusion.1), channel_id=1, source_target_pairs={{0,128},{16,144},{32,160},{48,176},{64,192},{80,208},{96,224},{112... | collective-permute-start | bytes 12296 | tf_op jit(solution)/shard_map/ppermute | solution.py:783
  82.2 1.4 %collective-permute-start.12 = (f32[8,128]{1,0:T(8,128)S(1)}, f32[8,128]{1,0:T(8,128)S(1)}, u32[]{:S(2)}, u32[]{:S(2)}) collective-permute-start(f32[8,128]{1,0:T(8,128)S(1)} %maximum_maximum_fusion.1), channel_id=1, source_target_pairs={{0,64},{16,80},{32,96},{48,112},{64,0},{80,16},{96,32},{112,48},{1... | collective-permute-start | bytes 12296 | tf_op jit(solution)/shard_map/ppermute | solution.py:783
  83.6 1.2 %collective-permute-done.14 = f32[8,128]{1,0:T(8,128)S(1)} collective-permute-done((f32[8,128]{1,0:T(8,128)S(1)}, f32[8,128]{1,0:T(8,128)S(1)}, u32[]{:S(2)}, u32[]{:S(2)}) %collective-permute-start.14) | collective-permute-done | bytes 4128 | tf_op jit(solution)/shard_map/ppermute | solution.py:783
  84.9 2.4 %collective-permute-done.12 = f32[8,128]{1,0:T(8,128)S(1)} collective-permute-done((f32[8,128]{1,0:T(8,128)S(1)}, f32[8,128]{1,0:T(8,128)S(1)}, u32[]{:S(2)}, u32[]{:S(2)}) %collective-permute-start.12) | collective-permute-done | bytes 4128 | tf_op jit(solution)/shard_map/ppermute | solution.py:783
  88.5 1.1 %all-to-all-done.5 = bf16[16,2,2,16,256]{4,3,2,1,0:T(8,128)(2,1)S(1)} async-done(((bf16[16,2,2,16,256]{4,3,2,1,0:T(8,128)(2,1)}), bf16[16,2,2,16,256]{4,3,2,1,0:T(8,128)(2,1)S(1)}, u32[]{:S(2)}, u32[]{:S(2)}) %all-to-all-start.5) | async-done | bytes 524320 | tf_op jit(solution)/shard_map/all_to_all | solution.py:788
  89.5 2.2 %conditional.1 = (f32[2,24,32,256]{3,2,1,0:T(8,128)S(1)}) conditional(s32[]{:T(128)} %bitcast.60, (f32[2,24,32,256]{3,2,1,0:T(8,128)}, bf16[16,2,2,16,256]{4,3,2,1,0:T(8,128)(2,1)S(1)}, f32[32,256]{1,0:T(8,128)S(1)}, s32[32,256]{1,0:T(8,128)S(1)}, s32[32,256]{1,0:T(8,128)S(1)}) %tuple.110, (s32[32,256]{1,0:T(8,128)S(1)}, s32[32,256]{1,0:T(8,128)S(1)}, ...), branch_computations={%region_2.3_spmd, %region_3.8_spmd} | conditional | flops 1856398592 | bytes 219619936 | solution.py:811
  89.5 1.9 %finish.1 = f32[2,24,32,256]{3,2,1,0:T(8,128)S(1)} custom-call(f32[2,24,32,256]{3,2,1,0:T(8,128)} %get-tuple-element.102.x_ref, bf16[2,8,2,2,16,256]{5,4,3,2,1,0:T(8,128)(2,1)S(1)} %bitcast.155, f32[32,256]{1,0:T(8,128)S(1)} %get-tuple-element.104.place_ref, s32[32,256]{1,0:T(8,128)S(1)} %get-tuple-element.105.land_ref, ...), custom_call_target="tpu_custom_call" | custom-call | flops 134217728 | bytes 4000000 | tf_op jit(solution)/shard_map/cond/branch_0_fun/finish/pallas_call | solution.py:792
  91.7 1.1 %copy-done.24 = f32[2,24,32,256]{3,2,1,0:T(8,128)} copy-done((f32[2,24,32,256]{3,2,1,0:T(8,128)}, f32[2,24,32,256]{3,2,1,0:T(8,128)S(1)}, u32[]{:S(2)}) %copy-start.24) | copy-done | bytes 1572888
  (76 shorter events, 3.9 us)
Async XLA Ops:
  0.0 16.0 %copy-start.26 = (s32[32,256]{1,0:T(8,128)S(1)}, s32[32,256]{1,0:T(8,128)}, u32[]{:S(2)}) copy-start(s32[32,256]{1,0:T(8,128)} %bottom_ref.1) | copy-start | bytes 98308
  0.0 16.0 %copy-start.29 = (s32[32,256]{1,0:T(8,128)S(1)}, s32[32,256]{1,0:T(8,128)}, u32[]{:S(2)}) copy-start(s32[32,256]{1,0:T(8,128)} %land_ref.1) | copy-start | bytes 98308
  4.6 17.6 %copy-start.37 = (bf16[32,512]{1,0:T(8,128)(2,1)S(1)}, bf16[32,512]{1,0:T(8,128)(2,1)}, u32[]{:S(2)}) copy-start(bf16[32,512]{1,0:T(8,128)(2,1)} %param.21) | copy-start | bytes 98308
  4.6 17.7 %copy-start.39 = (f32[512]{0:T(512)S(1)}, f32[512]{0:T(512)}, u32[]{:S(2)}) copy-start(f32[512]{0:T(512)} %param.22) | copy-start | bytes 6148
  4.6 17.7 %copy-start.31 = (bf16[512,512]{1,0:T(8,128)(2,1)S(1)}, bf16[512,512]{1,0:T(8,128)(2,1)}, u32[]{:S(2)}) copy-start(bf16[512,512]{1,0:T(8,128)(2,1)} %param.23) | copy-start | bytes 1572868
  4.6 28.6 %all-to-all-start.4 = ((bf16[16,2,2,16,256]{4,3,2,1,0:T(8,128)(2,1)}), bf16[16,2,2,16,256]{4,3,2,1,0:T(8,128)(2,1)S(1)}, u32[]{:S(2)}, u32[]{:S(2)}) async-start(bf16[16,2,2,16,256]{4,3,2,1,0:T(8,128)(2,1)} %bitcast.26), calls=%async_computation.4 | async-start | bytes 1048576 | tf_op jit(solution)/shard_map/all_to_all | solution.py:667
  17.9 5.5 %copy-start.40 = (f32[512]{0:T(512)S(1)}, f32[512]{0:T(512)}, u32[]{:S(2)}) copy-start(f32[512]{0:T(512)} %param.24) | copy-start | bytes 6148
  17.9 7.8 %collective-permute-start.6 = (f32[8,2,256]{2,1,0:T(2,128)S(1)}, f32[8,2,256]{2,1,0:T(2,128)S(1)}, u32[]{:S(2)}, u32[]{:S(2)}) collective-permute-start(f32[8,2,256]{2,1,0:T(2,128)S(1)} %pad_maximum_fusion.9), channel_id=1, source_target_pairs={{8,16},{24,32},{40,48},{56,64},{72,80},{88,96},{104,112},{120,128}... | collective-permute-start | bytes 49160 | tf_op jit(solution)/shard_map/ppermute | solution.py:703
  28.0 13.6 %copy-start.34 = (bf16[512,32]{0,1:T(8,128)(2,1)S(1)}, bf16[512,32]{0,1:T(8,128)(2,1)}, u32[]{:S(2)}) copy-start(bf16[512,32]{0,1:T(8,128)(2,1)} %param.25) | copy-start | bytes 98308
  33.5 20.7 %collective-permute-start.7 = (bf16[4,32,256]{2,1,0:T(8,128)(2,1)S(1)}, bf16[4,32,256]{2,1,0:T(8,128)(2,1)S(1)}, u32[]{:S(2)}, u32[]{:S(2)}) collective-permute-start(bf16[4,32,256]{2,1,0:T(8,128)(2,1)S(1)} %get-tuple-element.157), channel_id=1, source_target_pairs={{0,8},{16,24},{32,40},{48,56},{64,72},{80,88},{96,104},{112,120},{... | collective-permute-start | bytes 196616 | tf_op jit(solution)/shard_map/ppermute | solution.py:742
  36.1 18.1 %collective-permute-start.8 = (bf16[4,32,256]{2,1,0:T(8,128)(2,1)S(1)}, bf16[4,32,256]{2,1,0:T(8,128)(2,1)S(1)}, u32[]{:S(2)}, u32[]{:S(2)}) collective-permute-start(bf16[4,32,256]{2,1,0:T(8,128)(2,1)S(1)} %get-tuple-element.158), channel_id=1, source_target_pairs={{8,0},{24,16},{40,32},{56,48},{72,64},{88,80},{104,96},{120,112},{... | collective-permute-start | bytes 196616 | tf_op jit(solution)/shard_map/ppermute | solution.py:743
  41.6 1.0 %copy-start = (bf16[512,512]{1,0:T(8,128)(2,1)S(1)}, bf16[512,512]{1,0:T(8,128)(2,1)}, u32[]{:S(2)}) copy-start(bf16[512,512]{1,0:T(8,128)(2,1)} %fusion.29.mid_hbm.mid_ref) | copy-start | bytes 1572868
  42.7 1.0 %copy-start.1 = (f32[54,8,256]{2,1,0:T(8,128)S(1)}, f32[54,8,256]{2,1,0:T(8,128)}, u32[]{:S(2)}) copy-start(f32[54,8,256]{2,1,0:T(8,128)} %stack.81.factors_hbm.factors_ref) | copy-start | bytes 1327108
  68.2 21.4 %all-to-all-start.5 = ((bf16[16,2,2,16,256]{4,3,2,1,0:T(8,128)(2,1)}), bf16[16,2,2,16,256]{4,3,2,1,0:T(8,128)(2,1)S(1)}, u32[]{:S(2)}, u32[]{:S(2)}) async-start(bf16[16,2,2,16,256]{4,3,2,1,0:T(8,128)(2,1)} %bitcast.61), calls=%async_computation.5 | async-start | bytes 1048576 | tf_op jit(solution)/shard_map/all_to_all | solution.py:788
  74.1 3.1 %collective-permute-start.11 = (f32[8,128]{1,0:T(8,128)S(1)}, f32[8,128]{1,0:T(8,128)S(1)}, u32[]{:S(2)}, u32[]{:S(2)}) collective-permute-start(f32[8,128]{1,0:T(8,128)S(1)} %broadcast_in_dim.25), channel_id=1, source_target_pairs={{0,48},{16,32},{32,16},{48,0},{64,112},{80,96},{96,80},{112,64},{1... | collective-permute-start | bytes 12296 | tf_op jit(solution)/shard_map/ppermute | solution.py:783
  74.2 3.7 %collective-permute-start.10 = (f32[8,128]{1,0:T(8,128)S(1)}, f32[8,128]{1,0:T(8,128)S(1)}, u32[]{:S(2)}, u32[]{:S(2)}) collective-permute-start(f32[8,128]{1,0:T(8,128)S(1)} %broadcast_in_dim.25), channel_id=1, source_target_pairs={{0,32},{16,48},{32,0},{48,16},{64,96},{80,112},{96,64},{112,80},{1... | collective-permute-start | bytes 12296 | tf_op jit(solution)/shard_map/ppermute | solution.py:783
  75.4 2.5 %collective-permute-start.9 = (f32[8,128]{1,0:T(8,128)S(1)}, f32[8,128]{1,0:T(8,128)S(1)}, u32[]{:S(2)}, u32[]{:S(2)}) collective-permute-start(f32[8,128]{1,0:T(8,128)S(1)} %broadcast_in_dim.25), channel_id=1, source_target_pairs={{0,16},{16,0},{32,48},{48,32},{64,80},{80,64},{96,112},{112,96},{1... | collective-permute-start | bytes 12296 | tf_op jit(solution)/shard_map/ppermute | solution.py:783
  78.5 6.2 %collective-permute-start.14 = (f32[8,128]{1,0:T(8,128)S(1)}, f32[8,128]{1,0:T(8,128)S(1)}, u32[]{:S(2)}, u32[]{:S(2)}) collective-permute-start(f32[8,128]{1,0:T(8,128)S(1)} %maximum_maximum_fusion.1), channel_id=1, source_target_pairs={{0,192},{16,208},{32,224},{48,240},{64,128},{80,144},{96,160},{112... | collective-permute-start | bytes 12296 | tf_op jit(solution)/shard_map/ppermute | solution.py:783
  80.8 4.0 %collective-permute-start.13 = (f32[8,128]{1,0:T(8,128)S(1)}, f32[8,128]{1,0:T(8,128)S(1)}, u32[]{:S(2)}, u32[]{:S(2)}) collective-permute-start(f32[8,128]{1,0:T(8,128)S(1)} %maximum_maximum_fusion.1), channel_id=1, source_target_pairs={{0,128},{16,144},{32,160},{48,176},{64,192},{80,208},{96,224},{112... | collective-permute-start | bytes 12296 | tf_op jit(solution)/shard_map/ppermute | solution.py:783
  82.2 5.1 %collective-permute-start.12 = (f32[8,128]{1,0:T(8,128)S(1)}, f32[8,128]{1,0:T(8,128)S(1)}, u32[]{:S(2)}, u32[]{:S(2)}) collective-permute-start(f32[8,128]{1,0:T(8,128)S(1)} %maximum_maximum_fusion.1), channel_id=1, source_target_pairs={{0,64},{16,80},{32,96},{48,112},{64,0},{80,16},{96,32},{112,48},{1... | collective-permute-start | bytes 12296 | tf_op jit(solution)/shard_map/ppermute | solution.py:783
  91.7 1.1 %copy-start.24 = (f32[2,24,32,256]{3,2,1,0:T(8,128)}, f32[2,24,32,256]{3,2,1,0:T(8,128)S(1)}, u32[]{:S(2)}) copy-start(f32[2,24,32,256]{3,2,1,0:T(8,128)S(1)} %get-tuple-element.559) | copy-start | bytes 4718596

commit v5 on v4

--- a/solution.py
+++ b/solution.py
@@ -220,28 +220,20 @@
 def source_kernel(
     rows,
     cells_ref,
-    table_ref,
-    factors_hbm,
+    place_ref,
+    factors_ref,
     in_ref,
-    mid_hbm,
+    mid_ref,
     bias_ref,
     out_ref,
     middle_ref,
     spread_ref,
+    table_ref,
     held,
-    factors_ref,
-    mid_ref,
-    arrivals,
 ):
     _, kinds, width = cells_ref.shape
     ahead = rows + 2
     weights = (in_ref, mid_ref, bias_ref, out_ref)
-    copies = [
-        pltpu.make_async_copy(mid_hbm, mid_ref, arrivals.at[0]),
-        pltpu.make_async_copy(factors_hbm, factors_ref, arrivals.at[1]),
-    ]
-    for copy in copies:
-        copy.start()
 
     def cell(level, row):
         if level == 0:
@@ -252,7 +244,9 @@
         row = 2 * i
         cells = jnp.concatenate([cells_ref[rows + row], cells_ref[rows + row + 1]], axis=0)
         for k in range(2):
-            value = nn(cells, table_ref[row + 2 + k]).astype(BF16)
+            table = one_hot(place_ref[row + 2 + k : row + 3 + k])
+            table_ref[row + 2 + k] = table
+            value = nn(cells, table).astype(BF16)
             spread_ref[row + k] = value[k * kinds : (k + 1) * kinds]
             spread_ref[rows + row + k] = value[(1 - k) * kinds : (2 - k) * kinds]
 
@@ -299,9 +293,9 @@
 
     for i in range(rows // 2):
         spread_out(i)
-    copies[0].wait()
+    for row in (0, 1, rows + 2, rows + 3):
+        table_ref[row] = one_hot(place_ref[row : row + 1])
     sources(0)
-    copies[1].wait()
     lax.fori_loop(1, rows // 2, body, 0)
     move(rows // 2 - 1)
 
@@ -453,7 +447,7 @@
     sources_of(1)
     pack(0)
     pack(rows // 2 - 1)
-    lax.fori_loop(1, rows // 2, body, 0)
+    lax.fori_loop(1, rows // 2, body, 0, unroll=True)
     move(0)
     for level in range(2):
         for part in range(scratch.shape[0]):
@@ -464,7 +458,7 @@
 HBM = pltpu.HBM
 
 
-def kernel_call(kernel, outs, scratch, flops, name, places=None, result_places=None):
+def kernel_call(kernel, outs, scratch, flops, name, places=None, result_places=None, memory=32):
     def specs(given):
         return [pl.BlockSpec(memory_space=place or pltpu.VMEM) for place in given]
 
@@ -477,7 +471,7 @@
         **spaces,
         scratch_shapes=scratch,
         cost_estimate=pl.CostEstimate(flops=flops, bytes_accessed=4_000_000, transcendentals=0),
-        compiler_params=pltpu.CompilerParams(vmem_limit_bytes=24 * 2**20),
+        compiler_params=pltpu.CompilerParams(vmem_limit_bytes=memory * 2**20),
         name=name,
     )
 
@@ -714,8 +708,13 @@
     factors = factors_of(east, north, wide_depth[0], jnp.stack(level_list).astype(F32)).reshape(
         3 * (rows + 2), 8, columns
     )
-    slots = jnp.arange(columns, dtype=jnp.int32).astype(F32)
-    table = (slots[None, :, None] == wide_place[0][:, None, :]).astype(BF16)
+
+    level = jnp.arange(levels, dtype=jnp.int32).astype(F32)
+    count = jnp.sum((level[:, None, None] < depth[None]).astype(F32), axis=2)
+    deep = jnp.roll(count[2 * stacks :], -(stacks // 2), axis=0)
+    deep = jnp.flip(deep.reshape(stacks, length // 2, 2), axis=2).reshape(stacks, length)
+    fullest = count[stacks : 2 * stacks] + deep
+    fullest, cells = lax.optimization_barrier((fullest, cells))
 
     in_parts = jnp.stack(split_parts(0.5 * in_bias, 3) + [jnp.zeros(in_bias.shape, BF16)] * 13, axis=1)
     weights = (
@@ -741,22 +740,17 @@
     )(cells)
     top = lax.ppermute(last, axes, within + across)
     bottom = lax.ppermute(first, axes, [(j, i) for i, j in within] + back)
-    partial, spread = kernel_call(
+    partial, spread, table = kernel_call(
         functools.partial(source_kernel, rows),
         [
             jax.ShapeDtypeStruct((3 * rows, all_kinds, columns), F32),
             jax.ShapeDtypeStruct((2 * rows, all_kinds, columns), BF16),
+            jax.ShapeDtypeStruct((rows + 4, columns, columns), BF16),
         ],
-        [
-            pltpu.VMEM((rows // 2, all_kinds, 4 * columns), BF16),
-            pltpu.VMEM(factors.shape, F32),
-            pltpu.VMEM(mid_weight.shape, BF16),
-            pltpu.SemaphoreType.DMA((2,)),
-        ],
+        [pltpu.VMEM((rows // 2, all_kinds, 4 * columns), BF16)],
         pieces * per_piece,
         "sources",
-        [None, None, HBM, None, HBM, None, None],
-    )(turned, table, factors, *weights)
+    )(turned, wide_place[0], factors, *weights)
     change = kernel_call(
         functools.partial(step_kernel, rows),
         jax.ShapeDtypeStruct(cells.shape, BF16),
@@ -770,19 +764,14 @@
         "steps",
     )(turned, spread, partial, top, bottom, table, factors, *weights)
 
-    depth, change = lax.optimization_barrier((depth, change))
-    level = jnp.arange(levels, dtype=jnp.int32).astype(F32)
-    count = jnp.sum((level[:, None, None] < depth[None]).astype(F32), axis=2)
-    deep = jnp.roll(count[2 * stacks :], -(stacks // 2), axis=0)
-    deep = jnp.flip(deep.reshape(stacks, length // 2, 2), axis=2).reshape(stacks, length)
-    fullest = jnp.full((8, 128), jnp.max(count[stacks : 2 * stacks] + deep))
+    fullest, change = lax.optimization_barrier((fullest, change))
     for step in (1, tiles // 4):
         others = []
         for times in (1, 2, 3):
             pairs = [(tile, tile ^ (step * times)) for tile in range(tiles)]
             others.append(lax.ppermute(fullest, "tile", pairs))
         fullest = functools.reduce(jnp.maximum, others, fullest)
-    excess = fullest[0, 0] > columns
+    excess = jnp.max(fullest) > columns
 
     change = change.reshape(group, kinds, 2, rows, columns)
     change = lax.all_to_all(change, "tracer", split_axis=0, concat_axis=0, tiled=True)
@@ -803,6 +792,7 @@
             "finish",
             [HBM, None, None, None, None],
             [HBM],
+            memory=63,
         )(arguments[0], change, place, arguments[3], arguments[4])
 
     def in_full(change, place, arguments):

time: 93.7 us -> 90.7 us (0.968)
  local copies, waits for them, and re-layouts: 8.69 us -> 3.74 us
  waiting for transfers between devices: 13 us -> 16.5 us
  other arithmetic: 3.69 us -> 1.63 us
    unnamed x21 -> x15, local copies, waits for them, and re-layouts: 3.44 us -> 0.25 us
    all_to_all x1, waiting for transfers between devices: 1.05 us -> 2.99 us  [body(): lax.all_to_all(change, 'tracer', split_axis=0, concat_axis=0, tiled=True)]
    all_to_all x1, waiting for transfers between devices: 4.39 us -> 5.69 us  [body(): lax.all_to_all(sent, 'tracer', split_axis=0, concat_axis=0, tiled=True)]
  transfers between devices with their start and end apart: 11 -> 11, of which waited for: 8 -> 7; matrix products, arithmetic and copies ran while one was open for 10% -> 6% of each run, Pallas kernels for 11% -> 12%
where the time goes in v5:
time: 90.7 us; the launch traced here: 90 us
  starting transfers between devices  34.8 us (38%)
  Pallas kernels  31.6 us (35%)
  waiting for transfers between devices  16.5 us (18%)
  local copies, waits for them, and re-layouts  3.74 us (4%)
  other arithmetic  1.63 us (2%)
  between operations  1.5 us (2%)
    pallas_call x1, Pallas kernels, body(): kernel_call(functools.partial(step_kernel, rows), jax.ShapeDtypeStruct(ce...  13.5 us
    all_to_all x1, starting transfers between devices, body(): lax.all_to_all(sent, 'tracer', split_axis=0, concat_axis=0, tiled=True)  11.2 us
    pallas_call x1, Pallas kernels, body(): kernel_call(functools.partial(source_kernel, rows), [jax.ShapeDtypeStruct...  10.4 us
    ppermute x6, starting transfers between devices, body(): others.append(lax.ppermute(fullest, 'tile', pairs))  7.26 us
    all_to_all x1, waiting for transfers between devices, body(): lax.all_to_all(sent, 'tracer', split_axis=0, concat_axis=0, tiled=True)  5.69 us
    ppermute x6, waiting for transfers between devices, body(): others.append(lax.ppermute(fullest, 'tile', pairs))  5.52 us
    ppermute x1, starting transfers between devices, body(): bottom = lax.ppermute(first, axes, [(j, i) for i, j in within] + back)  5.35 us
    pallas_call x1, Pallas kernels, body(): kernel_call(pack_kernel, [jax.ShapeDtypeStruct((halves, stacks, kinds, 2,...  4.54 us
  transfers between devices with their start and end apart: 11, of which 7 were waited for; matrix products, arithmetic and copies ran while one was open for 6% of the time, Pallas kernels for 12%

profile of v5, /device:TPU:2, one launch (start us, length us, event | category | flops | bytes accessed | tf_op | source)
XLA Modules:
  0.0 90.0 jit_solution(2399456985759144787)
XLA Ops:
  0.0 4.5 %pack.1 = (bf16[2,8,2,2,16,256]{5,4,3,2,1,0:T(8,128)(2,1)}, f32[32,256]{1,0:T(8,128)S(1)}) custom-call(f32[2,768,256]{2,1,0:T(8,128)} %bitcast.141, s32[32,256]{1,0:T(8,128)} %land_ref.1, s32[32,256]{1,0:T(8,128)} %bottom_ref.1), custom_call_target="tpu_custom_call" | custom-call | flops 402653184 | bytes 4000000 | tf_op jit(solution)/shard_map/pack/pallas_call | solution.py:641
  4.6 11.2 %all-to-all-start.4 = ((bf16[16,2,2,16,256]{4,3,2,1,0:T(8,128)(2,1)}), bf16[16,2,2,16,256]{4,3,2,1,0:T(8,128)(2,1)S(1)}, u32[]{:S(2)}, u32[]{:S(2)}) async-start(bf16[16,2,2,16,256]{4,3,2,1,0:T(8,128)(2,1)} %bitcast.26), calls=%async_computation.4 | async-start | bytes 1048576 | tf_op jit(solution)/shard_map/all_to_all | solution.py:661
  15.9 0.9 dynamic-slice_bitcast_fusion.2
  16.8 0.9 dynamic-slice_bitcast_fusion.8
  17.8 4.2 %collective-permute-start.6 = (f32[8,2,256]{2,1,0:T(2,128)S(1)}, f32[8,2,256]{2,1,0:T(2,128)S(1)}, u32[]{:S(2)}, u32[]{:S(2)}) collective-permute-start(f32[8,2,256]{2,1,0:T(2,128)S(1)} %pad_maximum_fusion.9), channel_id=1, source_target_pairs={{8,16},{24,32},{40,48},{56,64},{72,80},{88,96},{104,112},{120,128}... | collective-permute-start | bytes 49160 | tf_op jit(solution)/shard_map/ppermute | solution.py:697
  22.1 0.2 convert_reduce_fusion
  22.7 0.2 copy.113
  23.3 2.3 %collective-permute-done.6 = f32[8,2,256]{2,1,0:T(2,128)S(1)} collective-permute-done((f32[8,2,256]{2,1,0:T(2,128)S(1)}, f32[8,2,256]{2,1,0:T(2,128)S(1)}, u32[]{:S(2)}, u32[]{:S(2)}) %collective-permute-start.6) | collective-permute-done | bytes 16416 | tf_op jit(solution)/shard_map/ppermute | solution.py:697
  25.8 0.2 fusion.33
  26.6 0.7 stack.81.factors_ref
  27.3 5.7 %all-to-all-done.4 = bf16[16,2,2,16,256]{4,3,2,1,0:T(8,128)(2,1)S(1)} async-done(((bf16[16,2,2,16,256]{4,3,2,1,0:T(8,128)(2,1)}), bf16[16,2,2,16,256]{4,3,2,1,0:T(8,128)(2,1)S(1)}, u32[]{:S(2)}, u32[]{:S(2)}) %all-to-all-start.4) | async-done | bytes 524320 | tf_op jit(solution)/shard_map/all_to_all | solution.py:661
  33.0 0.4 turn.1
  33.4 2.6 %collective-permute-start.7 = (bf16[4,32,256]{2,1,0:T(8,128)(2,1)S(1)}, bf16[4,32,256]{2,1,0:T(8,128)(2,1)S(1)}, u32[]{:S(2)}, u32[]{:S(2)}) collective-permute-start(bf16[4,32,256]{2,1,0:T(8,128)(2,1)S(1)} %get-tuple-element.162), channel_id=1, source_target_pairs={{0,8},{16,24},{32,40},{48,56},{64,72},{80,88},{96,104},{112,120},{... | collective-permute-start | bytes 196616 | tf_op jit(solution)/shard_map/ppermute | solution.py:741
  36.0 5.4 %collective-permute-start.8 = (bf16[4,32,256]{2,1,0:T(8,128)(2,1)S(1)}, bf16[4,32,256]{2,1,0:T(8,128)(2,1)S(1)}, u32[]{:S(2)}, u32[]{:S(2)}) collective-permute-start(bf16[4,32,256]{2,1,0:T(8,128)(2,1)S(1)} %get-tuple-element.163), channel_id=1, source_target_pairs={{8,0},{24,16},{40,32},{56,48},{72,64},{88,80},{104,96},{120,112},{... | collective-permute-start | bytes 196616 | tf_op jit(solution)/shard_map/ppermute | solution.py:742
  41.4 0.1 broadcast_in_dim.22.bias_ref
  41.5 10.4 %sources.1 = (f32[48,32,256]{2,1,0:T(8,128)S(1)}, bf16[32,32,256]{2,1,0:T(8,128)(2,1)S(1)}, bf16[20,256,256]{2,1,0:T(8,128)(2,1)S(1)}) custom-call(bf16[32,32,256]{2,1,0:T(8,128)(2,1)S(1)} %get-tuple-element.156.cells_ref, f32[20,256]{1,0:T(8,128)S(1)} %maximum_select_fusion.2.place_ref, f32[54,8,256]{2,1,0:T(8,128)S(1)} %stack.81.factors_ref, ...), custom_call_target="tpu_custom_call" | custom-call | flops 4831838208 | bytes 4000000 | tf_op jit(solution)/shard_map/sources/pallas_call | solution.py:743
  51.9 13.5 %steps.1 = bf16[32,2,16,256]{3,2,1,0:T(8,128)(2,1)} custom-call(bf16[32,32,256]{2,1,0:T(8,128)(2,1)S(1)} %get-tuple-element.156.cells_ref, bf16[32,32,256]{2,1,0:T(8,128)(2,1)S(1)} %get-tuple-element.160.spread_ref, f32[48,32,256]{2,1,0:T(8,128)S(1)} %get-tuple-element.161.partial_ref, bf16[4,32,256]{2,1,0:T(8,128)(2,1)S(1)} %collective-permute-done.7.top_ref, ...), custom_call_target="tpu_custom_call" | custom-call | flops 4831838208 | bytes 4000000 | tf_op jit(solution)/shard_map/steps/pallas_call | solution.py:754
  65.4 4.2 %all-to-all-start.5 = ((bf16[16,2,2,16,256]{4,3,2,1,0:T(8,128)(2,1)}), bf16[16,2,2,16,256]{4,3,2,1,0:T(8,128)(2,1)S(1)}, u32[]{:S(2)}, u32[]{:S(2)}) async-start(bf16[16,2,2,16,256]{4,3,2,1,0:T(8,128)(2,1)} %bitcast.60), calls=%async_computation.5 | async-start | bytes 1048576 | tf_op jit(solution)/shard_map/all_to_all | solution.py:777
  69.6 0.3 collective-permute-start.11
  69.9 1.2 %collective-permute-start.10 = (f32[8,32]{1,0:T(8,128)S(1)}, f32[8,32]{1,0:T(8,128)S(1)}, u32[]{:S(2)}, u32[]{:S(2)}) collective-permute-start(f32[8,32]{1,0:T(8,128)S(1)} %slice_add_fusion), channel_id=1, source_target_pairs={{0,32},{16,48},{32,0},{48,16},{64,96},{80,112},{96,64},{112,80},{1... | collective-permute-start | bytes 3080 | tf_op jit(solution)/shard_map/ppermute | solution.py:772
  71.1 0.7 collective-permute-start.9
  71.8 1.2 %collective-permute-done.11 = f32[8,32]{1,0:T(8,128)S(1)} collective-permute-done((f32[8,32]{1,0:T(8,128)S(1)}, f32[8,32]{1,0:T(8,128)S(1)}, u32[]{:S(2)}, u32[]{:S(2)}) %collective-permute-start.11) | collective-permute-done | bytes 1056 | tf_op jit(solution)/shard_map/ppermute | solution.py:772
  73.0 0.7 collective-permute-done.10
  73.6 2.3 %collective-permute-start.14 = (f32[8,32]{1,0:T(8,128)S(1)}, f32[8,32]{1,0:T(8,128)S(1)}, u32[]{:S(2)}, u32[]{:S(2)}) collective-permute-start(f32[8,32]{1,0:T(8,128)S(1)} %maximum_maximum_fusion), channel_id=1, source_target_pairs={{0,192},{16,208},{32,224},{48,240},{64,128},{80,144},{96,160},{112... | collective-permute-start | bytes 3080 | tf_op jit(solution)/shard_map/ppermute | solution.py:772
  76.0 1.3 %collective-permute-start.13 = (f32[8,32]{1,0:T(8,128)S(1)}, f32[8,32]{1,0:T(8,128)S(1)}, u32[]{:S(2)}, u32[]{:S(2)}) collective-permute-start(f32[8,32]{1,0:T(8,128)S(1)} %maximum_maximum_fusion), channel_id=1, source_target_pairs={{0,128},{16,144},{32,160},{48,176},{64,192},{80,208},{96,224},{112... | collective-permute-start | bytes 3080 | tf_op jit(solution)/shard_map/ppermute | solution.py:772
  77.3 1.4 %collective-permute-start.12 = (f32[8,32]{1,0:T(8,128)S(1)}, f32[8,32]{1,0:T(8,128)S(1)}, u32[]{:S(2)}, u32[]{:S(2)}) collective-permute-start(f32[8,32]{1,0:T(8,128)S(1)} %maximum_maximum_fusion), channel_id=1, source_target_pairs={{0,64},{16,80},{32,96},{48,112},{64,0},{80,16},{96,32},{112,48},{1... | collective-permute-start | bytes 3080 | tf_op jit(solution)/shard_map/ppermute | solution.py:772
  78.7 1.0 %collective-permute-done.14 = f32[8,32]{1,0:T(8,128)S(1)} collective-permute-done((f32[8,32]{1,0:T(8,128)S(1)}, f32[8,32]{1,0:T(8,128)S(1)}, u32[]{:S(2)}, u32[]{:S(2)}) %collective-permute-start.14) | collective-permute-done | bytes 1056 | tf_op jit(solution)/shard_map/ppermute | solution.py:772
  79.8 2.7 %collective-permute-done.12 = f32[8,32]{1,0:T(8,128)S(1)} collective-permute-done((f32[8,32]{1,0:T(8,128)S(1)}, f32[8,32]{1,0:T(8,128)S(1)}, u32[]{:S(2)}, u32[]{:S(2)}) %collective-permute-start.12) | collective-permute-done | bytes 1056 | tf_op jit(solution)/shard_map/ppermute | solution.py:772
  82.4 0.7 maximum_reduce_fusion
  83.8 3.0 %all-to-all-done.5 = bf16[16,2,2,16,256]{4,3,2,1,0:T(8,128)(2,1)S(1)} async-done(((bf16[16,2,2,16,256]{4,3,2,1,0:T(8,128)(2,1)}), bf16[16,2,2,16,256]{4,3,2,1,0:T(8,128)(2,1)S(1)}, u32[]{:S(2)}, u32[]{:S(2)}) %all-to-all-start.5) | async-done | bytes 524320 | tf_op jit(solution)/shard_map/all_to_all | solution.py:777
  86.8 3.1 %conditional.1 = (f32[2,24,32,256]{3,2,1,0:T(8,128)}) conditional(s32[]{:T(128)} %convert_element_type.157, (f32[2,24,32,256]{3,2,1,0:T(8,128)}, bf16[16,2,2,16,256]{4,3,2,1,0:T(8,128)(2,1)S(1)}, f32[32,256]{1,0:T(8,128)S(1)}, s32[32,256]{1,0:T(8,128)S(1)}, s32[32,256]{1,0:T(8,128)S(1)}) %tuple.111, (s32[32,256]{1,0:T(8,128)S(1)}, ...), branch_computations={%region_2.3_spmd, %region_3.8_spmd} | conditional | flops 1856398592 | bytes 219619936 | solution.py:801
  86.8 2.8 %finish.1 = f32[2,24,32,256]{3,2,1,0:T(8,128)} custom-call(f32[2,24,32,256]{3,2,1,0:T(8,128)} %get-tuple-element.102.x_ref, bf16[2,8,2,2,16,256]{5,4,3,2,1,0:T(8,128)(2,1)S(1)} %bitcast.154, f32[32,256]{1,0:T(8,128)S(1)} %get-tuple-element.104.place_ref, s32[32,256]{1,0:T(8,128)S(1)} %get-tuple-element.105.land_ref, s32[32,256]{1,0:T(8,128)S(1)} %get-tuple-element.106.bottom_ref), custom_call_target="tpu_custom_call" | custom-call | flops 134217728 | bytes 4000000 | tf_op jit(solution)/shard_map/cond/branch_0_fun/finish/pallas_call | solution.py:781
  (66 shorter events, 1.5 us)
Async XLA Ops:
  0.0 15.9 %copy-start.23 = (s32[32,256]{1,0:T(8,128)S(1)}, s32[32,256]{1,0:T(8,128)}, u32[]{:S(2)}) copy-start(s32[32,256]{1,0:T(8,128)} %bottom_ref.1) | copy-start | bytes 98308
  0.0 15.9 %copy-start.26 = (s32[32,256]{1,0:T(8,128)S(1)}, s32[32,256]{1,0:T(8,128)}, u32[]{:S(2)}) copy-start(s32[32,256]{1,0:T(8,128)} %land_ref.1) | copy-start | bytes 98308
  4.6 18.0 %copy-start.34 = (bf16[32,512]{1,0:T(8,128)(2,1)S(1)}, bf16[32,512]{1,0:T(8,128)(2,1)}, u32[]{:S(2)}) copy-start(bf16[32,512]{1,0:T(8,128)(2,1)} %param.21) | copy-start | bytes 98308
  4.6 28.4 %all-to-all-start.4 = ((bf16[16,2,2,16,256]{4,3,2,1,0:T(8,128)(2,1)}), bf16[16,2,2,16,256]{4,3,2,1,0:T(8,128)(2,1)S(1)}, u32[]{:S(2)}, u32[]{:S(2)}) async-start(bf16[16,2,2,16,256]{4,3,2,1,0:T(8,128)(2,1)} %bitcast.26), calls=%async_computation.4 | async-start | bytes 1048576 | tf_op jit(solution)/shard_map/all_to_all | solution.py:661
  15.8 6.8 %copy-start.36 = (f32[512]{0:T(512)S(1)}, f32[512]{0:T(512)}, u32[]{:S(2)}) copy-start(f32[512]{0:T(512)} %param.22) | copy-start | bytes 6148
  15.8 6.8 %copy-start.28 = (bf16[512,512]{1,0:T(8,128)(2,1)S(1)}, bf16[512,512]{1,0:T(8,128)(2,1)}, u32[]{:S(2)}) copy-start(bf16[512,512]{1,0:T(8,128)(2,1)} %param.23) | copy-start | bytes 1572868
  17.8 5.2 %copy-start.37 = (f32[512]{0:T(512)S(1)}, f32[512]{0:T(512)}, u32[]{:S(2)}) copy-start(f32[512]{0:T(512)} %param.24) | copy-start | bytes 6148
  17.8 7.7 %collective-permute-start.6 = (f32[8,2,256]{2,1,0:T(2,128)S(1)}, f32[8,2,256]{2,1,0:T(2,128)S(1)}, u32[]{:S(2)}, u32[]{:S(2)}) collective-permute-start(f32[8,2,256]{2,1,0:T(2,128)S(1)} %pad_maximum_fusion.9), channel_id=1, source_target_pairs={{8,16},{24,32},{40,48},{56,64},{72,80},{88,96},{104,112},{120,128}... | collective-permute-start | bytes 49160 | tf_op jit(solution)/shard_map/ppermute | solution.py:697
  26.0 15.5 %copy-start.31 = (bf16[512,32]{0,1:T(8,128)(2,1)S(1)}, bf16[512,32]{0,1:T(8,128)(2,1)}, u32[]{:S(2)}) copy-start(bf16[512,32]{0,1:T(8,128)(2,1)} %param.25) | copy-start | bytes 98308
  33.4 18.5 %collective-permute-start.7 = (bf16[4,32,256]{2,1,0:T(8,128)(2,1)S(1)}, bf16[4,32,256]{2,1,0:T(8,128)(2,1)S(1)}, u32[]{:S(2)}, u32[]{:S(2)}) collective-permute-start(bf16[4,32,256]{2,1,0:T(8,128)(2,1)S(1)} %get-tuple-element.162), channel_id=1, source_target_pairs={{0,8},{16,24},{32,40},{48,56},{64,72},{80,88},{96,104},{112,120},{... | collective-permute-start | bytes 196616 | tf_op jit(solution)/shard_map/ppermute | solution.py:741
  36.0 15.9 %collective-permute-start.8 = (bf16[4,32,256]{2,1,0:T(8,128)(2,1)S(1)}, bf16[4,32,256]{2,1,0:T(8,128)(2,1)S(1)}, u32[]{:S(2)}, u32[]{:S(2)}) collective-permute-start(bf16[4,32,256]{2,1,0:T(8,128)(2,1)S(1)} %get-tuple-element.163), channel_id=1, source_target_pairs={{8,0},{24,16},{40,32},{56,48},{72,64},{88,80},{104,96},{120,112},{... | collective-permute-start | bytes 196616 | tf_op jit(solution)/shard_map/ppermute | solution.py:742
  65.4 21.3 %all-to-all-start.5 = ((bf16[16,2,2,16,256]{4,3,2,1,0:T(8,128)(2,1)}), bf16[16,2,2,16,256]{4,3,2,1,0:T(8,128)(2,1)S(1)}, u32[]{:S(2)}, u32[]{:S(2)}) async-start(bf16[16,2,2,16,256]{4,3,2,1,0:T(8,128)(2,1)} %bitcast.60), calls=%async_computation.5 | async-start | bytes 1048576 | tf_op jit(solution)/shard_map/all_to_all | solution.py:777
  69.6 3.4 %collective-permute-start.11 = (f32[8,32]{1,0:T(8,128)S(1)}, f32[8,32]{1,0:T(8,128)S(1)}, u32[]{:S(2)}, u32[]{:S(2)}) collective-permute-start(f32[8,32]{1,0:T(8,128)S(1)} %slice_add_fusion), channel_id=1, source_target_pairs={{0,48},{16,32},{32,16},{48,0},{64,112},{80,96},{96,80},{112,64},{1... | collective-permute-start | bytes 3080 | tf_op jit(solution)/shard_map/ppermute | solution.py:772
  69.9 3.7 %collective-permute-start.10 = (f32[8,32]{1,0:T(8,128)S(1)}, f32[8,32]{1,0:T(8,128)S(1)}, u32[]{:S(2)}, u32[]{:S(2)}) collective-permute-start(f32[8,32]{1,0:T(8,128)S(1)} %slice_add_fusion), channel_id=1, source_target_pairs={{0,32},{16,48},{32,0},{48,16},{64,96},{80,112},{96,64},{112,80},{1... | collective-permute-start | bytes 3080 | tf_op jit(solution)/shard_map/ppermute | solution.py:772
  71.1 2.5 %collective-permute-start.9 = (f32[8,32]{1,0:T(8,128)S(1)}, f32[8,32]{1,0:T(8,128)S(1)}, u32[]{:S(2)}, u32[]{:S(2)}) collective-permute-start(f32[8,32]{1,0:T(8,128)S(1)} %slice_add_fusion), channel_id=1, source_target_pairs={{0,16},{16,0},{32,48},{48,32},{64,80},{80,64},{96,112},{112,96},{1... | collective-permute-start | bytes 3080 | tf_op jit(solution)/shard_map/ppermute | solution.py:772
  73.6 6.1 %collective-permute-start.14 = (f32[8,32]{1,0:T(8,128)S(1)}, f32[8,32]{1,0:T(8,128)S(1)}, u32[]{:S(2)}, u32[]{:S(2)}) collective-permute-start(f32[8,32]{1,0:T(8,128)S(1)} %maximum_maximum_fusion), channel_id=1, source_target_pairs={{0,192},{16,208},{32,224},{48,240},{64,128},{80,144},{96,160},{112... | collective-permute-start | bytes 3080 | tf_op jit(solution)/shard_map/ppermute | solution.py:772
  76.0 3.8 %collective-permute-start.13 = (f32[8,32]{1,0:T(8,128)S(1)}, f32[8,32]{1,0:T(8,128)S(1)}, u32[]{:S(2)}, u32[]{:S(2)}) collective-permute-start(f32[8,32]{1,0:T(8,128)S(1)} %maximum_maximum_fusion), channel_id=1, source_target_pairs={{0,128},{16,144},{32,160},{48,176},{64,192},{80,208},{96,224},{112... | collective-permute-start | bytes 3080 | tf_op jit(solution)/shard_map/ppermute | solution.py:772
  77.3 5.1 %collective-permute-start.12 = (f32[8,32]{1,0:T(8,128)S(1)}, f32[8,32]{1,0:T(8,128)S(1)}, u32[]{:S(2)}, u32[]{:S(2)}) collective-permute-start(f32[8,32]{1,0:T(8,128)S(1)} %maximum_maximum_fusion), channel_id=1, source_target_pairs={{0,64},{16,80},{32,96},{48,112},{64,0},{80,16},{96,32},{112,48},{1... | collective-permute-start | bytes 3080 | tf_op jit(solution)/shard_map/ppermute | solution.py:772

commit v6 on v5

--- a/solution.py
+++ b/solution.py
@@ -80,7 +80,22 @@
 
 
 def pack_kernel(
-    x_ref, land_ref, bottom_ref, sent_ref, place_ref, depth_ref, counts, table, held, plain, packed, arrivals
+    x_ref,
+    land_hbm,
+    bottom_hbm,
+    sent_hbm,
+    place_ref,
+    depth_ref,
+    counts,
+    table,
+    held,
+    plain,
+    packed,
+    land_ref,
+    bottom_ref,
+    sent_ref,
+    arrivals,
+    leaving,
 ):
     kinds, _, width = x_ref.shape
     length = land_ref.shape[0]
@@ -101,8 +116,14 @@
     copies.append(
         pltpu.make_async_copy(x_ref.at[:, pl.ds(0, stacks * length)], plain, arrivals.at[len(copies)])
     )
-    for copy in copies:
+    masks = [
+        pltpu.make_async_copy(land_hbm, land_ref, arrivals.at[len(copies)]),
+        pltpu.make_async_copy(bottom_hbm, bottom_ref, arrivals.at[len(copies) + 1]),
+    ]
+    for copy in masks + copies:
         copy.start()
+    for copy in masks:
+        copy.wait()
     depth_ref[...] = jnp.where(land_ref[...] == 1, bottom_ref[...], 0).astype(F32)
     bins = 32
     value = lax.broadcasted_iota(jnp.int32, (bins, width), 0).astype(F32)
@@ -120,8 +141,23 @@
         place = jnp.sum(here, axis=0, keepdims=True)
         place_ref[row : row + 1] = place if row % 2 == 0 else (width - 1.0) - place
 
-    for copy in copies[:-1]:
+    for copy in copies:
         copy.wait()
+    sent = []
+
+    def send(half, kind, slot):
+        block = (half, slice(None), kind, slot)
+        sent.append(
+            pltpu.make_async_copy(sent_ref.at[block], sent_hbm.at[block], leaving.at[len(sent)])
+        )
+        sent[-1].start()
+
+    for half in range(halves):
+        inside = slice(half * rows, (half + 1) * rows)
+        for kind in range(kinds):
+            block = plain[kind].reshape(stacks, length, width)
+            sent_ref[half, :, kind, 0] = block[:, inside].astype(BF16)
+            send(half, kind, 0)
     level = stacks + lax.broadcasted_iota(jnp.int32, (thin, width), 0).astype(F32)
 
     def body(i, _):
@@ -143,16 +179,16 @@
         return 0
 
     lax.fori_loop(0, length // 2, body, 0, unroll=8)
-    copies[-1].wait()
     for half in range(halves):
         inside = slice(half * rows, (half + 1) * rows)
         for kind in range(kinds):
-            block = plain[kind].reshape(stacks, length, width)
-            sent_ref[half, :, kind, 0] = block[:, inside].astype(BF16)
             for part in range(packed.shape[0]):
                 at = kind * stacks * length
                 block = packed[part, at : at + stacks * length].reshape(stacks, length, 128)
                 sent_ref[half, :, kind, 1, :, part * 128 : (part + 1) * 128] = block[:, inside].astype(BF16)
+            send(half, kind, 1)
+    for copy in sent:
+        copy.wait()
 
 
 def finish_kernel(
@@ -464,7 +500,8 @@
 
     spaces = {} if places is None else {"in_specs": specs(places)}
     if result_places is not None:
-        spaces["out_specs"] = specs(result_places)[0]
+        given = specs(result_places)
+        spaces["out_specs"] = given if isinstance(outs, list) else given[0]
     return pl.pallas_call(
         kernel,
         out_shape=outs,
@@ -651,11 +688,16 @@
             pltpu.VMEM((parts, kinds * thin * length, 128), F32),
             pltpu.VMEM((kinds, stacks * length, columns), F32),
             pltpu.VMEM((parts, kinds * stacks * length, 128), F32),
-            pltpu.SemaphoreType.DMA((kinds * parts + 1,)),
+            pltpu.VMEM((length, columns), jnp.int32),
+            pltpu.VMEM((length, columns), jnp.int32),
+            pltpu.VMEM((halves, stacks, kinds, 2, rows, columns), BF16),
+            pltpu.SemaphoreType.DMA((kinds * parts + 3,)),
+            pltpu.SemaphoreType.DMA((halves * kinds * 2,)),
         ],
         2 * length * columns * columns * (32 + 64),
         "pack",
-        [HBM, None, None],
+        [HBM, HBM, HBM],
+        [HBM, None],
     )(tracers.reshape(kinds, levels * length, columns), land_mask, bottom_level)
     sent = sent.reshape(group, kinds, 2, rows, columns)
     cells = lax.all_to_all(sent, "tracer", split_axis=0, concat_axis=0, tiled=True)

time: 90.7 us -> 90 us (level)
  no operation moved by 1% of the time
where the time goes in v6:
time: 90 us; the launch traced here: 89.4 us
  starting transfers between devices  34.8 us (39%)
  Pallas kernels  30.9 us (34%)
  waiting for transfers between devices  16.5 us (18%)
  local copies, waits for them, and re-layouts  3.74 us (4%)
  other arithmetic  1.63 us (2%)
  between operations  1.5 us (2%)
    pallas_call x1, Pallas kernels, body(): kernel_call(functools.partial(step_kernel, rows), jax.ShapeDtypeStruct(ce...  13.5 us
    all_to_all x1, starting transfers between devices, body(): lax.all_to_all(sent, 'tracer', split_axis=0, concat_axis=0, tiled=True)  11.2 us
    pallas_call x1, Pallas kernels, body(): kernel_call(functools.partial(source_kernel, rows), [jax.ShapeDtypeStruct...  10.4 us
    ppermute x6, starting transfers between devices, body(): others.append(lax.ppermute(fullest, 'tile', pairs))  7.26 us
    all_to_all x1, waiting for transfers between devices, body(): lax.all_to_all(sent, 'tracer', split_axis=0, concat_axis=0, tiled=True)  5.67 us
    ppermute x6, waiting for transfers between devices, body(): others.append(lax.ppermute(fullest, 'tile', pairs))  5.53 us
    ppermute x1, starting transfers between devices, body(): bottom = lax.ppermute(first, axes, [(j, i) for i, j in within] + back)  5.33 us
    all_to_all x1, starting transfers between devices, body(): lax.all_to_all(change, 'tracer', split_axis=0, concat_axis=0, tiled=True)  4.22 us
  transfers between devices with their start and end apart: 11, of which 7 were waited for; matrix products, arithmetic and copies ran while one was open for 6% of the time, Pallas kernels for 12%

profile of v6, /device:TPU:2, one launch (start us, length us, event | category | flops | bytes accessed | tf_op | source)
XLA Modules:
  0.0 89.4 jit_solution(16108870683860653393)
XLA Ops:
  0.0 3.9 %pack.1 = (bf16[2,8,2,2,16,256]{5,4,3,2,1,0:T(8,128)(2,1)}, f32[32,256]{1,0:T(8,128)S(1)}) custom-call(f32[2,768,256]{2,1,0:T(8,128)} %bitcast.141, s32[32,256]{1,0:T(8,128)} %land_hbm.1, s32[32,256]{1,0:T(8,128)} %bottom_hbm.1), custom_call_target="tpu_custom_call" | custom-call | flops 402653184 | bytes 4000000 | tf_op jit(solution)/shard_map/pack/pallas_call | solution.py:678
  3.9 11.2 %all-to-all-start.4 = ((bf16[16,2,2,16,256]{4,3,2,1,0:T(8,128)(2,1)}), bf16[16,2,2,16,256]{4,3,2,1,0:T(8,128)(2,1)S(1)}, u32[]{:S(2)}, u32[]{:S(2)}) async-start(bf16[16,2,2,16,256]{4,3,2,1,0:T(8,128)(2,1)} %bitcast.26), calls=%async_computation.4 | async-start | bytes 1048576 | tf_op jit(solution)/shard_map/all_to_all | solution.py:703
  15.3 0.9 %dynamic-slice_bitcast_fusion.2 = (f32[1,32,256]{2,1,0:T(8,128)S(1)}, f32[1,32,256]{2,1,0:T(8,128)S(1)}, f32[1,32,256]{2,1,0:T(8,128)S(1)}, f32[1,32,256]{2,1,0:...) fusion(f32[6,4,32,256]{3,2,1,0:T(8,128)} %bitcast.155, s32[]{:T(128)S(6)} %add.154, s32[]{:T(128)S(6)} %select_n.87, ...), kind=kLoop, calls=%fused_computation.112 | loop fusion | bytes 393240 | tf_op jit(solution)/shard_map/slice | solution.py:720
  16.2 0.9 dynamic-slice_bitcast_fusion.8
  17.2 4.2 %collective-permute-start.6 = (f32[8,2,256]{2,1,0:T(2,128)S(1)}, f32[8,2,256]{2,1,0:T(2,128)S(1)}, u32[]{:S(2)}, u32[]{:S(2)}) collective-permute-start(f32[8,2,256]{2,1,0:T(2,128)S(1)} %pad_maximum_fusion.9), channel_id=1, source_target_pairs={{8,16},{24,32},{40,48},{56,64},{72,80},{88,96},{104,112},{120,128}... | collective-permute-start | bytes 49160 | tf_op jit(solution)/shard_map/ppermute | solution.py:739
  21.4 0.2 convert_reduce_fusion
  22.0 0.2 copy.113
  22.6 2.3 %collective-permute-done.6 = f32[8,2,256]{2,1,0:T(2,128)S(1)} collective-permute-done((f32[8,2,256]{2,1,0:T(2,128)S(1)}, f32[8,2,256]{2,1,0:T(2,128)S(1)}, u32[]{:S(2)}, u32[]{:S(2)}) %collective-permute-start.6) | collective-permute-done | bytes 16416 | tf_op jit(solution)/shard_map/ppermute | solution.py:739
  25.1 0.2 fusion.33
  25.9 0.7 stack.81.factors_ref
  26.6 5.7 %all-to-all-done.4 = bf16[16,2,2,16,256]{4,3,2,1,0:T(8,128)(2,1)S(1)} async-done(((bf16[16,2,2,16,256]{4,3,2,1,0:T(8,128)(2,1)}), bf16[16,2,2,16,256]{4,3,2,1,0:T(8,128)(2,1)S(1)}, u32[]{:S(2)}, u32[]{:S(2)}) %all-to-all-start.4) | async-done | bytes 524320 | tf_op jit(solution)/shard_map/all_to_all | solution.py:703
  32.3 0.4 turn.1
  32.7 2.6 %collective-permute-start.7 = (bf16[4,32,256]{2,1,0:T(8,128)(2,1)S(1)}, bf16[4,32,256]{2,1,0:T(8,128)(2,1)S(1)}, u32[]{:S(2)}, u32[]{:S(2)}) collective-permute-start(bf16[4,32,256]{2,1,0:T(8,128)(2,1)S(1)} %get-tuple-element.162), channel_id=1, source_target_pairs={{0,8},{16,24},{32,40},{48,56},{64,72},{80,88},{96,104},{112,120},{... | collective-permute-start | bytes 196616 | tf_op jit(solution)/shard_map/ppermute | solution.py:783
  35.3 5.3 %collective-permute-start.8 = (bf16[4,32,256]{2,1,0:T(8,128)(2,1)S(1)}, bf16[4,32,256]{2,1,0:T(8,128)(2,1)S(1)}, u32[]{:S(2)}, u32[]{:S(2)}) collective-permute-start(bf16[4,32,256]{2,1,0:T(8,128)(2,1)S(1)} %get-tuple-element.163), channel_id=1, source_target_pairs={{8,0},{24,16},{40,32},{56,48},{72,64},{88,80},{104,96},{120,112},{... | collective-permute-start | bytes 196616 | tf_op jit(solution)/shard_map/ppermute | solution.py:784
  40.7 0.1 broadcast_in_dim.22.bias_ref
  40.8 10.4 %sources.1 = (f32[48,32,256]{2,1,0:T(8,128)S(1)}, bf16[32,32,256]{2,1,0:T(8,128)(2,1)S(1)}, bf16[20,256,256]{2,1,0:T(8,128)(2,1)S(1)}) custom-call(bf16[32,32,256]{2,1,0:T(8,128)(2,1)S(1)} %get-tuple-element.156.cells_ref, f32[20,256]{1,0:T(8,128)S(1)} %maximum_select_fusion.2.place_ref, f32[54,8,256]{2,1,0:T(8,128)S(1)} %stack.81.factors_ref, ...), custom_call_target="tpu_custom_call" | custom-call | flops 4831838208 | bytes 4000000 | tf_op jit(solution)/shard_map/sources/pallas_call | solution.py:785
  51.2 13.5 %steps.1 = bf16[32,2,16,256]{3,2,1,0:T(8,128)(2,1)} custom-call(bf16[32,32,256]{2,1,0:T(8,128)(2,1)S(1)} %get-tuple-element.156.cells_ref, bf16[32,32,256]{2,1,0:T(8,128)(2,1)S(1)} %get-tuple-element.160.spread_ref, f32[48,32,256]{2,1,0:T(8,128)S(1)} %get-tuple-element.161.partial_ref, bf16[4,32,256]{2,1,0:T(8,128)(2,1)S(1)} %collective-permute-done.7.top_ref, ...), custom_call_target="tpu_custom_call" | custom-call | flops 4831838208 | bytes 4000000 | tf_op jit(solution)/shard_map/steps/pallas_call | solution.py:796
  64.7 4.2 %all-to-all-start.5 = ((bf16[16,2,2,16,256]{4,3,2,1,0:T(8,128)(2,1)}), bf16[16,2,2,16,256]{4,3,2,1,0:T(8,128)(2,1)S(1)}, u32[]{:S(2)}, u32[]{:S(2)}) async-start(bf16[16,2,2,16,256]{4,3,2,1,0:T(8,128)(2,1)} %bitcast.60), calls=%async_computation.5 | async-start | bytes 1048576 | tf_op jit(solution)/shard_map/all_to_all | solution.py:819
  69.0 0.3 collective-permute-start.11
  69.3 1.2 %collective-permute-start.10 = (f32[8,32]{1,0:T(8,128)S(1)}, f32[8,32]{1,0:T(8,128)S(1)}, u32[]{:S(2)}, u32[]{:S(2)}) collective-permute-start(f32[8,32]{1,0:T(8,128)S(1)} %slice_add_fusion), channel_id=1, source_target_pairs={{0,32},{16,48},{32,0},{48,16},{64,96},{80,112},{96,64},{112,80},{1... | collective-permute-start | bytes 3080 | tf_op jit(solution)/shard_map/ppermute | solution.py:814
  70.5 0.7 collective-permute-start.9
  71.2 1.2 %collective-permute-done.11 = f32[8,32]{1,0:T(8,128)S(1)} collective-permute-done((f32[8,32]{1,0:T(8,128)S(1)}, f32[8,32]{1,0:T(8,128)S(1)}, u32[]{:S(2)}, u32[]{:S(2)}) %collective-permute-start.11) | collective-permute-done | bytes 1056 | tf_op jit(solution)/shard_map/ppermute | solution.py:814
  72.3 0.7 collective-permute-done.10
  73.0 2.3 %collective-permute-start.14 = (f32[8,32]{1,0:T(8,128)S(1)}, f32[8,32]{1,0:T(8,128)S(1)}, u32[]{:S(2)}, u32[]{:S(2)}) collective-permute-start(f32[8,32]{1,0:T(8,128)S(1)} %maximum_maximum_fusion), channel_id=1, source_target_pairs={{0,192},{16,208},{32,224},{48,240},{64,128},{80,144},{96,160},{112... | collective-permute-start | bytes 3080 | tf_op jit(solution)/shard_map/ppermute | solution.py:814
  75.3 1.3 %collective-permute-start.13 = (f32[8,32]{1,0:T(8,128)S(1)}, f32[8,32]{1,0:T(8,128)S(1)}, u32[]{:S(2)}, u32[]{:S(2)}) collective-permute-start(f32[8,32]{1,0:T(8,128)S(1)} %maximum_maximum_fusion), channel_id=1, source_target_pairs={{0,128},{16,144},{32,160},{48,176},{64,192},{80,208},{96,224},{112... | collective-permute-start | bytes 3080 | tf_op jit(solution)/shard_map/ppermute | solution.py:814
  76.7 1.4 %collective-permute-start.12 = (f32[8,32]{1,0:T(8,128)S(1)}, f32[8,32]{1,0:T(8,128)S(1)}, u32[]{:S(2)}, u32[]{:S(2)}) collective-permute-start(f32[8,32]{1,0:T(8,128)S(1)} %maximum_maximum_fusion), channel_id=1, source_target_pairs={{0,64},{16,80},{32,96},{48,112},{64,0},{80,16},{96,32},{112,48},{1... | collective-permute-start | bytes 3080 | tf_op jit(solution)/shard_map/ppermute | solution.py:814
  78.1 1.0 %collective-permute-done.14 = f32[8,32]{1,0:T(8,128)S(1)} collective-permute-done((f32[8,32]{1,0:T(8,128)S(1)}, f32[8,32]{1,0:T(8,128)S(1)}, u32[]{:S(2)}, u32[]{:S(2)}) %collective-permute-start.14) | collective-permute-done | bytes 1056 | tf_op jit(solution)/shard_map/ppermute | solution.py:814
  79.1 2.7 %collective-permute-done.12 = f32[8,32]{1,0:T(8,128)S(1)} collective-permute-done((f32[8,32]{1,0:T(8,128)S(1)}, f32[8,32]{1,0:T(8,128)S(1)}, u32[]{:S(2)}, u32[]{:S(2)}) %collective-permute-start.12) | collective-permute-done | bytes 1056 | tf_op jit(solution)/shard_map/ppermute | solution.py:814
  81.8 0.7 maximum_reduce_fusion
  83.1 3.0 %all-to-all-done.5 = bf16[16,2,2,16,256]{4,3,2,1,0:T(8,128)(2,1)S(1)} async-done(((bf16[16,2,2,16,256]{4,3,2,1,0:T(8,128)(2,1)}), bf16[16,2,2,16,256]{4,3,2,1,0:T(8,128)(2,1)S(1)}, u32[]{:S(2)}, u32[]{:S(2)}) %all-to-all-start.5) | async-done | bytes 524320 | tf_op jit(solution)/shard_map/all_to_all | solution.py:819
  86.1 3.1 %conditional.1 = (f32[2,24,32,256]{3,2,1,0:T(8,128)}) conditional(s32[]{:T(128)} %convert_element_type.157, (f32[2,24,32,256]{3,2,1,0:T(8,128)}, bf16[16,2,2,16,256]{4,3,2,1,0:T(8,128)(2,1)S(1)}, f32[32,256]{1,0:T(8,128)S(1)}, s32[32,256]{1,0:T(8,128)S(1)}, s32[32,256]{1,0:T(8,128)S(1)}) %tuple.111, (s32[32,256]{1,0:T(8,128)S(1)}, ...), branch_computations={%region_2.3_spmd, %region_3.8_spmd} | conditional | flops 1856398592 | bytes 219619936 | solution.py:843
  86.1 2.8 %finish.1 = f32[2,24,32,256]{3,2,1,0:T(8,128)} custom-call(f32[2,24,32,256]{3,2,1,0:T(8,128)} %get-tuple-element.102.x_ref, bf16[2,8,2,2,16,256]{5,4,3,2,1,0:T(8,128)(2,1)S(1)} %bitcast.154, f32[32,256]{1,0:T(8,128)S(1)} %get-tuple-element.104.place_ref, s32[32,256]{1,0:T(8,128)S(1)} %get-tuple-element.105.land_ref, s32[32,256]{1,0:T(8,128)S(1)} %get-tuple-element.106.bottom_ref), custom_call_target="tpu_custom_call" | custom-call | flops 134217728 | bytes 4000000 | tf_op jit(solution)/shard_map/cond/branch_0_fun/finish/pallas_call | solution.py:823
  (66 shorter events, 1.5 us)
Async XLA Ops:
  0.0 15.2 %copy-start.23 = (s32[32,256]{1,0:T(8,128)S(1)}, s32[32,256]{1,0:T(8,128)}, u32[]{:S(2)}) copy-start(s32[32,256]{1,0:T(8,128)} %bottom_hbm.1) | copy-start | bytes 98308
  0.0 15.2 %copy-start.26 = (s32[32,256]{1,0:T(8,128)S(1)}, s32[32,256]{1,0:T(8,128)}, u32[]{:S(2)}) copy-start(s32[32,256]{1,0:T(8,128)} %land_hbm.1) | copy-start | bytes 98308
  3.9 18.0 %copy-start.34 = (bf16[32,512]{1,0:T(8,128)(2,1)S(1)}, bf16[32,512]{1,0:T(8,128)(2,1)}, u32[]{:S(2)}) copy-start(bf16[32,512]{1,0:T(8,128)(2,1)} %param.21) | copy-start | bytes 98308
  3.9 28.4 %all-to-all-start.4 = ((bf16[16,2,2,16,256]{4,3,2,1,0:T(8,128)(2,1)}), bf16[16,2,2,16,256]{4,3,2,1,0:T(8,128)(2,1)S(1)}, u32[]{:S(2)}, u32[]{:S(2)}) async-start(bf16[16,2,2,16,256]{4,3,2,1,0:T(8,128)(2,1)} %bitcast.26), calls=%async_computation.4 | async-start | bytes 1048576 | tf_op jit(solution)/shard_map/all_to_all | solution.py:703
  15.1 6.8 %copy-start.36 = (f32[512]{0:T(512)S(1)}, f32[512]{0:T(512)}, u32[]{:S(2)}) copy-start(f32[512]{0:T(512)} %param.22) | copy-start | bytes 6148
  15.1 6.8 %copy-start.28 = (bf16[512,512]{1,0:T(8,128)(2,1)S(1)}, bf16[512,512]{1,0:T(8,128)(2,1)}, u32[]{:S(2)}) copy-start(bf16[512,512]{1,0:T(8,128)(2,1)} %param.23) | copy-start | bytes 1572868
  17.1 5.2 %copy-start.37 = (f32[512]{0:T(512)S(1)}, f32[512]{0:T(512)}, u32[]{:S(2)}) copy-start(f32[512]{0:T(512)} %param.24) | copy-start | bytes 6148
  17.2 7.7 %collective-permute-start.6 = (f32[8,2,256]{2,1,0:T(2,128)S(1)}, f32[8,2,256]{2,1,0:T(2,128)S(1)}, u32[]{:S(2)}, u32[]{:S(2)}) collective-permute-start(f32[8,2,256]{2,1,0:T(2,128)S(1)} %pad_maximum_fusion.9), channel_id=1, source_target_pairs={{8,16},{24,32},{40,48},{56,64},{72,80},{88,96},{104,112},{120,128}... | collective-permute-start | bytes 49160 | tf_op jit(solution)/shard_map/ppermute | solution.py:739
  25.3 15.5 %copy-start.31 = (bf16[512,32]{0,1:T(8,128)(2,1)S(1)}, bf16[512,32]{0,1:T(8,128)(2,1)}, u32[]{:S(2)}) copy-start(bf16[512,32]{0,1:T(8,128)(2,1)} %param.25) | copy-start | bytes 98308
  32.7 18.5 %collective-permute-start.7 = (bf16[4,32,256]{2,1,0:T(8,128)(2,1)S(1)}, bf16[4,32,256]{2,1,0:T(8,128)(2,1)S(1)}, u32[]{:S(2)}, u32[]{:S(2)}) collective-permute-start(bf16[4,32,256]{2,1,0:T(8,128)(2,1)S(1)} %get-tuple-element.162), channel_id=1, source_target_pairs={{0,8},{16,24},{32,40},{48,56},{64,72},{80,88},{96,104},{112,120},{... | collective-permute-start | bytes 196616 | tf_op jit(solution)/shard_map/ppermute | solution.py:783
  35.3 15.9 %collective-permute-start.8 = (bf16[4,32,256]{2,1,0:T(8,128)(2,1)S(1)}, bf16[4,32,256]{2,1,0:T(8,128)(2,1)S(1)}, u32[]{:S(2)}, u32[]{:S(2)}) collective-permute-start(bf16[4,32,256]{2,1,0:T(8,128)(2,1)S(1)} %get-tuple-element.163), channel_id=1, source_target_pairs={{8,0},{24,16},{40,32},{56,48},{72,64},{88,80},{104,96},{120,112},{... | collective-permute-start | bytes 196616 | tf_op jit(solution)/shard_map/ppermute | solution.py:784
  64.7 21.4 %all-to-all-start.5 = ((bf16[16,2,2,16,256]{4,3,2,1,0:T(8,128)(2,1)}), bf16[16,2,2,16,256]{4,3,2,1,0:T(8,128)(2,1)S(1)}, u32[]{:S(2)}, u32[]{:S(2)}) async-start(bf16[16,2,2,16,256]{4,3,2,1,0:T(8,128)(2,1)} %bitcast.60), calls=%async_computation.5 | async-start | bytes 1048576 | tf_op jit(solution)/shard_map/all_to_all | solution.py:819
  69.0 3.4 %collective-permute-start.11 = (f32[8,32]{1,0:T(8,128)S(1)}, f32[8,32]{1,0:T(8,128)S(1)}, u32[]{:S(2)}, u32[]{:S(2)}) collective-permute-start(f32[8,32]{1,0:T(8,128)S(1)} %slice_add_fusion), channel_id=1, source_target_pairs={{0,48},{16,32},{32,16},{48,0},{64,112},{80,96},{96,80},{112,64},{1... | collective-permute-start | bytes 3080 | tf_op jit(solution)/shard_map/ppermute | solution.py:814
  69.3 3.7 %collective-permute-start.10 = (f32[8,32]{1,0:T(8,128)S(1)}, f32[8,32]{1,0:T(8,128)S(1)}, u32[]{:S(2)}, u32[]{:S(2)}) collective-permute-start(f32[8,32]{1,0:T(8,128)S(1)} %slice_add_fusion), channel_id=1, source_target_pairs={{0,32},{16,48},{32,0},{48,16},{64,96},{80,112},{96,64},{112,80},{1... | collective-permute-start | bytes 3080 | tf_op jit(solution)/shard_map/ppermute | solution.py:814
  70.5 2.5 %collective-permute-start.9 = (f32[8,32]{1,0:T(8,128)S(1)}, f32[8,32]{1,0:T(8,128)S(1)}, u32[]{:S(2)}, u32[]{:S(2)}) collective-permute-start(f32[8,32]{1,0:T(8,128)S(1)} %slice_add_fusion), channel_id=1, source_target_pairs={{0,16},{16,0},{32,48},{48,32},{64,80},{80,64},{96,112},{112,96},{1... | collective-permute-start | bytes 3080 | tf_op jit(solution)/shard_map/ppermute | solution.py:814
  73.0 6.1 %collective-permute-start.14 = (f32[8,32]{1,0:T(8,128)S(1)}, f32[8,32]{1,0:T(8,128)S(1)}, u32[]{:S(2)}, u32[]{:S(2)}) collective-permute-start(f32[8,32]{1,0:T(8,128)S(1)} %maximum_maximum_fusion), channel_id=1, source_target_pairs={{0,192},{16,208},{32,224},{48,240},{64,128},{80,144},{96,160},{112... | collective-permute-start | bytes 3080 | tf_op jit(solution)/shard_map/ppermute | solution.py:814
  75.3 3.8 %collective-permute-start.13 = (f32[8,32]{1,0:T(8,128)S(1)}, f32[8,32]{1,0:T(8,128)S(1)}, u32[]{:S(2)}, u32[]{:S(2)}) collective-permute-start(f32[8,32]{1,0:T(8,128)S(1)} %maximum_maximum_fusion), channel_id=1, source_target_pairs={{0,128},{16,144},{32,160},{48,176},{64,192},{80,208},{96,224},{112... | collective-permute-start | bytes 3080 | tf_op jit(solution)/shard_map/ppermute | solution.py:814
  76.7 5.1 %collective-permute-start.12 = (f32[8,32]{1,0:T(8,128)S(1)}, f32[8,32]{1,0:T(8,128)S(1)}, u32[]{:S(2)}, u32[]{:S(2)}) collective-permute-start(f32[8,32]{1,0:T(8,128)S(1)} %maximum_maximum_fusion), channel_id=1, source_target_pairs={{0,64},{16,80},{32,96},{48,112},{64,0},{80,16},{96,32},{112,48},{1... | collective-permute-start | bytes 3080 | tf_op jit(solution)/shard_map/ppermute | solution.py:814

commit v7 on v6

--- a/solution.py
+++ b/solution.py
@@ -35,7 +35,7 @@
     for level in range(levels):
         for part in range(scratch.shape[0]):
             block = x_ref[:, level, :, part * 128 : (part + 1) * 128]
-            scratch[part] = block.astype(F32).reshape(kinds * rows, 128)
+            scratch[part, : kinds * rows] = block.astype(F32).reshape(kinds * rows, 128)
         for row in range(rows):
             picked = [scratch[part, pl.ds(row, kinds, stride=rows), :] for part in range(scratch.shape[0])]
             piece = jnp.concatenate(picked, axis=1).astype(BF16)
@@ -685,9 +685,9 @@
             pltpu.VMEM((length, columns), F32),
             pltpu.VMEM((length * 32, 2 * columns), BF16),
             pltpu.VMEM((2 * columns, columns), BF16),
-            pltpu.VMEM((parts, kinds * thin * length, 128), F32),
+            pltpu.VMEM((parts, (kinds * thin + 1) * length, 128), F32),
             pltpu.VMEM((kinds, stacks * length, columns), F32),
-            pltpu.VMEM((parts, kinds * stacks * length, 128), F32),
+            pltpu.VMEM((parts, (kinds * stacks + 1) * length, 128), F32),
             pltpu.VMEM((length, columns), jnp.int32),
             pltpu.VMEM((length, columns), jnp.int32),
             pltpu.VMEM((halves, stacks, kinds, 2, rows, columns), BF16),
@@ -776,7 +776,7 @@
             jax.ShapeDtypeStruct((4, all_kinds, columns), BF16),
             jax.ShapeDtypeStruct((4, all_kinds, columns), BF16),
         ],
-        [pltpu.VMEM((parts, all_kinds * rows, 128), F32)],
+        [pltpu.VMEM((parts, (all_kinds + 1) * rows, 128), F32)],
         1_000_000,
         "turn",
     )(cells)
@@ -800,7 +800,7 @@
             pltpu.VMEM((3 * (rows + 2), all_kinds, columns), F32),
             pltpu.VMEM((rows, all_kinds, columns), BF16),
             pltpu.VMEM((rows // 2, all_kinds, 4 * columns), BF16),
-            pltpu.VMEM((parts, 2 * rows * all_kinds, 128), F32),
+            pltpu.VMEM((parts, (2 * all_kinds + 1) * rows, 128), F32),
         ],
         pieces * per_piece,
         "steps",
@@ -824,8 +824,8 @@
             finish_kernel,
             jax.ShapeDtypeStruct(tracers.shape, F32),
             [
-                pltpu.VMEM((parts, group * kinds * rows, 128), F32),
-                pltpu.VMEM((parts, kinds * thin * length, 128), F32),
+                pltpu.VMEM((parts, (group + 1) * kinds * rows, 128), F32),
+                pltpu.VMEM((parts, (kinds * thin + 1) * length, 128), F32),
                 pltpu.VMEM(tracers.shape, F32),
                 pltpu.SemaphoreType.DMA((kinds,)),
                 pltpu.SemaphoreType.DMA((kinds * levels // stacks,)),

time: 90 us -> 90 us (level)
  no operation moved by 1% of the time
where the time goes in v7:
time: 90 us; the launch traced here: 89.4 us
  starting transfers between devices  34.8 us (39%)
  Pallas kernels  30.9 us (34%)
  waiting for transfers between devices  16.5 us (18%)
  local copies, waits for them, and re-layouts  3.74 us (4%)
  other arithmetic  1.63 us (2%)
  between operations  1.51 us (2%)
    pallas_call x1, Pallas kernels, body(): kernel_call(functools.partial(step_kernel, rows), jax.ShapeDtypeStruct(ce...  13.5 us
    all_to_all x1, starting transfers between devices, body(): lax.all_to_all(sent, 'tracer', split_axis=0, concat_axis=0, tiled=True)  11.2 us
    pallas_call x1, Pallas kernels, body(): kernel_call(functools.partial(source_kernel, rows), [jax.ShapeDtypeStruct...  10.4 us
    ppermute x6, starting transfers between devices, body(): others.append(lax.ppermute(fullest, 'tile', pairs))  7.26 us
    all_to_all x1, waiting for transfers between devices, body(): lax.all_to_all(sent, 'tracer', split_axis=0, concat_axis=0, tiled=True)  5.67 us
    ppermute x6, waiting for transfers between devices, body(): others.append(lax.ppermute(fullest, 'tile', pairs))  5.53 us
    ppermute x1, starting transfers between devices, body(): bottom = lax.ppermute(first, axes, [(j, i) for i, j in within] + back)  5.33 us
    all_to_all x1, starting transfers between devices, body(): lax.all_to_all(change, 'tracer', split_axis=0, concat_axis=0, tiled=True)  4.21 us
  transfers between devices with their start and end apart: 11, of which 7 were waited for; matrix products, arithmetic and copies ran while one was open for 6% of the time, Pallas kernels for 12%

profile of v7, /device:TPU:2, one launch (start us, length us, event | category | flops | bytes accessed | tf_op | source)
XLA Modules:
  0.0 89.4 jit_solution(697401242392674673)
XLA Ops:
  0.0 3.9 %pack.1 = (bf16[2,8,2,2,16,256]{5,4,3,2,1,0:T(8,128)(2,1)}, f32[32,256]{1,0:T(8,128)S(1)}) custom-call(f32[2,768,256]{2,1,0:T(8,128)} %bitcast.141, s32[32,256]{1,0:T(8,128)} %land_hbm.1, s32[32,256]{1,0:T(8,128)} %bottom_hbm.1), custom_call_target="tpu_custom_call" | custom-call | flops 402653184 | bytes 4000000 | tf_op jit(solution)/shard_map/pack/pallas_call | solution.py:678
  3.9 11.2 %all-to-all-start.4 = ((bf16[16,2,2,16,256]{4,3,2,1,0:T(8,128)(2,1)}), bf16[16,2,2,16,256]{4,3,2,1,0:T(8,128)(2,1)S(1)}, u32[]{:S(2)}, u32[]{:S(2)}) async-start(bf16[16,2,2,16,256]{4,3,2,1,0:T(8,128)(2,1)} %bitcast.26), calls=%async_computation.4 | async-start | bytes 1048576 | tf_op jit(solution)/shard_map/all_to_all | solution.py:703
  15.3 0.9 %dynamic-slice_bitcast_fusion.2 = (f32[1,32,256]{2,1,0:T(8,128)S(1)}, f32[1,32,256]{2,1,0:T(8,128)S(1)}, f32[1,32,256]{2,1,0:T(8,128)S(1)}, f32[1,32,256]{2,1,0:...) fusion(f32[6,4,32,256]{3,2,1,0:T(8,128)} %bitcast.155, s32[]{:T(128)S(6)} %add.154, s32[]{:T(128)S(6)} %select_n.87, ...), kind=kLoop, calls=%fused_computation.112 | loop fusion | bytes 393240 | tf_op jit(solution)/shard_map/slice | solution.py:720
  16.2 0.9 dynamic-slice_bitcast_fusion.8
  17.2 4.2 %collective-permute-start.6 = (f32[8,2,256]{2,1,0:T(2,128)S(1)}, f32[8,2,256]{2,1,0:T(2,128)S(1)}, u32[]{:S(2)}, u32[]{:S(2)}) collective-permute-start(f32[8,2,256]{2,1,0:T(2,128)S(1)} %pad_maximum_fusion.9), channel_id=1, source_target_pairs={{8,16},{24,32},{40,48},{56,64},{72,80},{88,96},{104,112},{120,128}... | collective-permute-start | bytes 49160 | tf_op jit(solution)/shard_map/ppermute | solution.py:739
  21.4 0.2 convert_reduce_fusion
  22.0 0.2 copy.113
  22.6 2.3 %collective-permute-done.6 = f32[8,2,256]{2,1,0:T(2,128)S(1)} collective-permute-done((f32[8,2,256]{2,1,0:T(2,128)S(1)}, f32[8,2,256]{2,1,0:T(2,128)S(1)}, u32[]{:S(2)}, u32[]{:S(2)}) %collective-permute-start.6) | collective-permute-done | bytes 16416 | tf_op jit(solution)/shard_map/ppermute | solution.py:739
  25.1 0.2 fusion.33
  25.9 0.7 stack.81.factors_ref
  26.6 5.7 %all-to-all-done.4 = bf16[16,2,2,16,256]{4,3,2,1,0:T(8,128)(2,1)S(1)} async-done(((bf16[16,2,2,16,256]{4,3,2,1,0:T(8,128)(2,1)}), bf16[16,2,2,16,256]{4,3,2,1,0:T(8,128)(2,1)S(1)}, u32[]{:S(2)}, u32[]{:S(2)}) %all-to-all-start.4) | async-done | bytes 524320 | tf_op jit(solution)/shard_map/all_to_all | solution.py:703
  32.3 0.4 turn.1
  32.7 2.6 %collective-permute-start.7 = (bf16[4,32,256]{2,1,0:T(8,128)(2,1)S(1)}, bf16[4,32,256]{2,1,0:T(8,128)(2,1)S(1)}, u32[]{:S(2)}, u32[]{:S(2)}) collective-permute-start(bf16[4,32,256]{2,1,0:T(8,128)(2,1)S(1)} %get-tuple-element.162), channel_id=1, source_target_pairs={{0,8},{16,24},{32,40},{48,56},{64,72},{80,88},{96,104},{112,120},{... | collective-permute-start | bytes 196616 | tf_op jit(solution)/shard_map/ppermute | solution.py:783
  35.3 5.3 %collective-permute-start.8 = (bf16[4,32,256]{2,1,0:T(8,128)(2,1)S(1)}, bf16[4,32,256]{2,1,0:T(8,128)(2,1)S(1)}, u32[]{:S(2)}, u32[]{:S(2)}) collective-permute-start(bf16[4,32,256]{2,1,0:T(8,128)(2,1)S(1)} %get-tuple-element.163), channel_id=1, source_target_pairs={{8,0},{24,16},{40,32},{56,48},{72,64},{88,80},{104,96},{120,112},{... | collective-permute-start | bytes 196616 | tf_op jit(solution)/shard_map/ppermute | solution.py:784
  40.7 0.1 broadcast_in_dim.22.bias_ref
  40.8 10.4 %sources.1 = (f32[48,32,256]{2,1,0:T(8,128)S(1)}, bf16[32,32,256]{2,1,0:T(8,128)(2,1)S(1)}, bf16[20,256,256]{2,1,0:T(8,128)(2,1)S(1)}) custom-call(bf16[32,32,256]{2,1,0:T(8,128)(2,1)S(1)} %get-tuple-element.156.cells_ref, f32[20,256]{1,0:T(8,128)S(1)} %maximum_select_fusion.2.place_ref, f32[54,8,256]{2,1,0:T(8,128)S(1)} %stack.81.factors_ref, ...), custom_call_target="tpu_custom_call" | custom-call | flops 4831838208 | bytes 4000000 | tf_op jit(solution)/shard_map/sources/pallas_call | solution.py:785
  51.2 13.5 %steps.1 = bf16[32,2,16,256]{3,2,1,0:T(8,128)(2,1)} custom-call(bf16[32,32,256]{2,1,0:T(8,128)(2,1)S(1)} %get-tuple-element.156.cells_ref, bf16[32,32,256]{2,1,0:T(8,128)(2,1)S(1)} %get-tuple-element.160.spread_ref, f32[48,32,256]{2,1,0:T(8,128)S(1)} %get-tuple-element.161.partial_ref, bf16[4,32,256]{2,1,0:T(8,128)(2,1)S(1)} %collective-permute-done.7.top_ref, ...), custom_call_target="tpu_custom_call" | custom-call | flops 4831838208 | bytes 4000000 | tf_op jit(solution)/shard_map/steps/pallas_call | solution.py:796
  64.8 4.2 %all-to-all-start.5 = ((bf16[16,2,2,16,256]{4,3,2,1,0:T(8,128)(2,1)}), bf16[16,2,2,16,256]{4,3,2,1,0:T(8,128)(2,1)S(1)}, u32[]{:S(2)}, u32[]{:S(2)}) async-start(bf16[16,2,2,16,256]{4,3,2,1,0:T(8,128)(2,1)} %bitcast.60), calls=%async_computation.5 | async-start | bytes 1048576 | tf_op jit(solution)/shard_map/all_to_all | solution.py:819
  69.0 0.3 collective-permute-start.11
  69.3 1.2 %collective-permute-start.10 = (f32[8,32]{1,0:T(8,128)S(1)}, f32[8,32]{1,0:T(8,128)S(1)}, u32[]{:S(2)}, u32[]{:S(2)}) collective-permute-start(f32[8,32]{1,0:T(8,128)S(1)} %slice_add_fusion), channel_id=1, source_target_pairs={{0,32},{16,48},{32,0},{48,16},{64,96},{80,112},{96,64},{112,80},{1... | collective-permute-start | bytes 3080 | tf_op jit(solution)/shard_map/ppermute | solution.py:814
  70.5 0.7 collective-permute-start.9
  71.2 1.2 %collective-permute-done.11 = f32[8,32]{1,0:T(8,128)S(1)} collective-permute-done((f32[8,32]{1,0:T(8,128)S(1)}, f32[8,32]{1,0:T(8,128)S(1)}, u32[]{:S(2)}, u32[]{:S(2)}) %collective-permute-start.11) | collective-permute-done | bytes 1056 | tf_op jit(solution)/shard_map/ppermute | solution.py:814
  72.3 0.7 collective-permute-done.10
  73.0 2.3 %collective-permute-start.14 = (f32[8,32]{1,0:T(8,128)S(1)}, f32[8,32]{1,0:T(8,128)S(1)}, u32[]{:S(2)}, u32[]{:S(2)}) collective-permute-start(f32[8,32]{1,0:T(8,128)S(1)} %maximum_maximum_fusion), channel_id=1, source_target_pairs={{0,192},{16,208},{32,224},{48,240},{64,128},{80,144},{96,160},{112... | collective-permute-start | bytes 3080 | tf_op jit(solution)/shard_map/ppermute | solution.py:814
  75.3 1.3 %collective-permute-start.13 = (f32[8,32]{1,0:T(8,128)S(1)}, f32[8,32]{1,0:T(8,128)S(1)}, u32[]{:S(2)}, u32[]{:S(2)}) collective-permute-start(f32[8,32]{1,0:T(8,128)S(1)} %maximum_maximum_fusion), channel_id=1, source_target_pairs={{0,128},{16,144},{32,160},{48,176},{64,192},{80,208},{96,224},{112... | collective-permute-start | bytes 3080 | tf_op jit(solution)/shard_map/ppermute | solution.py:814
  76.7 1.4 %collective-permute-start.12 = (f32[8,32]{1,0:T(8,128)S(1)}, f32[8,32]{1,0:T(8,128)S(1)}, u32[]{:S(2)}, u32[]{:S(2)}) collective-permute-start(f32[8,32]{1,0:T(8,128)S(1)} %maximum_maximum_fusion), channel_id=1, source_target_pairs={{0,64},{16,80},{32,96},{48,112},{64,0},{80,16},{96,32},{112,48},{1... | collective-permute-start | bytes 3080 | tf_op jit(solution)/shard_map/ppermute | solution.py:814
  78.1 1.0 %collective-permute-done.14 = f32[8,32]{1,0:T(8,128)S(1)} collective-permute-done((f32[8,32]{1,0:T(8,128)S(1)}, f32[8,32]{1,0:T(8,128)S(1)}, u32[]{:S(2)}, u32[]{:S(2)}) %collective-permute-start.14) | collective-permute-done | bytes 1056 | tf_op jit(solution)/shard_map/ppermute | solution.py:814
  79.1 2.7 %collective-permute-done.12 = f32[8,32]{1,0:T(8,128)S(1)} collective-permute-done((f32[8,32]{1,0:T(8,128)S(1)}, f32[8,32]{1,0:T(8,128)S(1)}, u32[]{:S(2)}, u32[]{:S(2)}) %collective-permute-start.12) | collective-permute-done | bytes 1056 | tf_op jit(solution)/shard_map/ppermute | solution.py:814
  81.8 0.7 maximum_reduce_fusion
  83.1 3.0 %all-to-all-done.5 = bf16[16,2,2,16,256]{4,3,2,1,0:T(8,128)(2,1)S(1)} async-done(((bf16[16,2,2,16,256]{4,3,2,1,0:T(8,128)(2,1)}), bf16[16,2,2,16,256]{4,3,2,1,0:T(8,128)(2,1)S(1)}, u32[]{:S(2)}, u32[]{:S(2)}) %all-to-all-start.5) | async-done | bytes 524320 | tf_op jit(solution)/shard_map/all_to_all | solution.py:819
  86.1 3.1 %conditional.1 = (f32[2,24,32,256]{3,2,1,0:T(8,128)}) conditional(s32[]{:T(128)} %convert_element_type.157, (f32[2,24,32,256]{3,2,1,0:T(8,128)}, bf16[16,2,2,16,256]{4,3,2,1,0:T(8,128)(2,1)S(1)}, f32[32,256]{1,0:T(8,128)S(1)}, s32[32,256]{1,0:T(8,128)S(1)}, s32[32,256]{1,0:T(8,128)S(1)}) %tuple.111, (s32[32,256]{1,0:T(8,128)S(1)}, ...), branch_computations={%region_2.3_spmd, %region_3.8_spmd} | conditional | flops 1856398592 | bytes 219619936 | solution.py:843
  86.1 2.8 %finish.1 = f32[2,24,32,256]{3,2,1,0:T(8,128)} custom-call(f32[2,24,32,256]{3,2,1,0:T(8,128)} %get-tuple-element.102.x_ref, bf16[2,8,2,2,16,256]{5,4,3,2,1,0:T(8,128)(2,1)S(1)} %bitcast.154, f32[32,256]{1,0:T(8,128)S(1)} %get-tuple-element.104.place_ref, s32[32,256]{1,0:T(8,128)S(1)} %get-tuple-element.105.land_ref, s32[32,256]{1,0:T(8,128)S(1)} %get-tuple-element.106.bottom_ref), custom_call_target="tpu_custom_call" | custom-call | flops 134217728 | bytes 4000000 | tf_op jit(solution)/shard_map/cond/branch_0_fun/finish/pallas_call | solution.py:823
  (66 shorter events, 1.5 us)
Async XLA Ops:
  0.0 15.2 %copy-start.23 = (s32[32,256]{1,0:T(8,128)S(1)}, s32[32,256]{1,0:T(8,128)}, u32[]{:S(2)}) copy-start(s32[32,256]{1,0:T(8,128)} %bottom_hbm.1) | copy-start | bytes 98308
  0.0 15.2 %copy-start.26 = (s32[32,256]{1,0:T(8,128)S(1)}, s32[32,256]{1,0:T(8,128)}, u32[]{:S(2)}) copy-start(s32[32,256]{1,0:T(8,128)} %land_hbm.1) | copy-start | bytes 98308
  3.9 18.0 %copy-start.34 = (bf16[32,512]{1,0:T(8,128)(2,1)S(1)}, bf16[32,512]{1,0:T(8,128)(2,1)}, u32[]{:S(2)}) copy-start(bf16[32,512]{1,0:T(8,128)(2,1)} %param.21) | copy-start | bytes 98308
  3.9 28.4 %all-to-all-start.4 = ((bf16[16,2,2,16,256]{4,3,2,1,0:T(8,128)(2,1)}), bf16[16,2,2,16,256]{4,3,2,1,0:T(8,128)(2,1)S(1)}, u32[]{:S(2)}, u32[]{:S(2)}) async-start(bf16[16,2,2,16,256]{4,3,2,1,0:T(8,128)(2,1)} %bitcast.26), calls=%async_computation.4 | async-start | bytes 1048576 | tf_op jit(solution)/shard_map/all_to_all | solution.py:703
  15.1 6.8 %copy-start.36 = (f32[512]{0:T(512)S(1)}, f32[512]{0:T(512)}, u32[]{:S(2)}) copy-start(f32[512]{0:T(512)} %param.22) | copy-start | bytes 6148
  15.1 6.8 %copy-start.28 = (bf16[512,512]{1,0:T(8,128)(2,1)S(1)}, bf16[512,512]{1,0:T(8,128)(2,1)}, u32[]{:S(2)}) copy-start(bf16[512,512]{1,0:T(8,128)(2,1)} %param.23) | copy-start | bytes 1572868
  17.1 5.2 %copy-start.37 = (f32[512]{0:T(512)S(1)}, f32[512]{0:T(512)}, u32[]{:S(2)}) copy-start(f32[512]{0:T(512)} %param.24) | copy-start | bytes 6148
  17.2 7.7 %collective-permute-start.6 = (f32[8,2,256]{2,1,0:T(2,128)S(1)}, f32[8,2,256]{2,1,0:T(2,128)S(1)}, u32[]{:S(2)}, u32[]{:S(2)}) collective-permute-start(f32[8,2,256]{2,1,0:T(2,128)S(1)} %pad_maximum_fusion.9), channel_id=1, source_target_pairs={{8,16},{24,32},{40,48},{56,64},{72,80},{88,96},{104,112},{120,128}... | collective-permute-start | bytes 49160 | tf_op jit(solution)/shard_map/ppermute | solution.py:739
  25.3 15.5 %copy-start.31 = (bf16[512,32]{0,1:T(8,128)(2,1)S(1)}, bf16[512,32]{0,1:T(8,128)(2,1)}, u32[]{:S(2)}) copy-start(bf16[512,32]{0,1:T(8,128)(2,1)} %param.25) | copy-start | bytes 98308
  32.7 18.5 %collective-permute-start.7 = (bf16[4,32,256]{2,1,0:T(8,128)(2,1)S(1)}, bf16[4,32,256]{2,1,0:T(8,128)(2,1)S(1)}, u32[]{:S(2)}, u32[]{:S(2)}) collective-permute-start(bf16[4,32,256]{2,1,0:T(8,128)(2,1)S(1)} %get-tuple-element.162), channel_id=1, source_target_pairs={{0,8},{16,24},{32,40},{48,56},{64,72},{80,88},{96,104},{112,120},{... | collective-permute-start | bytes 196616 | tf_op jit(solution)/shard_map/ppermute | solution.py:783
  35.3 15.9 %collective-permute-start.8 = (bf16[4,32,256]{2,1,0:T(8,128)(2,1)S(1)}, bf16[4,32,256]{2,1,0:T(8,128)(2,1)S(1)}, u32[]{:S(2)}, u32[]{:S(2)}) collective-permute-start(bf16[4,32,256]{2,1,0:T(8,128)(2,1)S(1)} %get-tuple-element.163), channel_id=1, source_target_pairs={{8,0},{24,16},{40,32},{56,48},{72,64},{88,80},{104,96},{120,112},{... | collective-permute-start | bytes 196616 | tf_op jit(solution)/shard_map/ppermute | solution.py:784
  64.8 21.4 %all-to-all-start.5 = ((bf16[16,2,2,16,256]{4,3,2,1,0:T(8,128)(2,1)}), bf16[16,2,2,16,256]{4,3,2,1,0:T(8,128)(2,1)S(1)}, u32[]{:S(2)}, u32[]{:S(2)}) async-start(bf16[16,2,2,16,256]{4,3,2,1,0:T(8,128)(2,1)} %bitcast.60), calls=%async_computation.5 | async-start | bytes 1048576 | tf_op jit(solution)/shard_map/all_to_all | solution.py:819
  69.0 3.4 %collective-permute-start.11 = (f32[8,32]{1,0:T(8,128)S(1)}, f32[8,32]{1,0:T(8,128)S(1)}, u32[]{:S(2)}, u32[]{:S(2)}) collective-permute-start(f32[8,32]{1,0:T(8,128)S(1)} %slice_add_fusion), channel_id=1, source_target_pairs={{0,48},{16,32},{32,16},{48,0},{64,112},{80,96},{96,80},{112,64},{1... | collective-permute-start | bytes 3080 | tf_op jit(solution)/shard_map/ppermute | solution.py:814
  69.3 3.7 %collective-permute-start.10 = (f32[8,32]{1,0:T(8,128)S(1)}, f32[8,32]{1,0:T(8,128)S(1)}, u32[]{:S(2)}, u32[]{:S(2)}) collective-permute-start(f32[8,32]{1,0:T(8,128)S(1)} %slice_add_fusion), channel_id=1, source_target_pairs={{0,32},{16,48},{32,0},{48,16},{64,96},{80,112},{96,64},{112,80},{1... | collective-permute-start | bytes 3080 | tf_op jit(solution)/shard_map/ppermute | solution.py:814
  70.5 2.5 %collective-permute-start.9 = (f32[8,32]{1,0:T(8,128)S(1)}, f32[8,32]{1,0:T(8,128)S(1)}, u32[]{:S(2)}, u32[]{:S(2)}) collective-permute-start(f32[8,32]{1,0:T(8,128)S(1)} %slice_add_fusion), channel_id=1, source_target_pairs={{0,16},{16,0},{32,48},{48,32},{64,80},{80,64},{96,112},{112,96},{1... | collective-permute-start | bytes 3080 | tf_op jit(solution)/shard_map/ppermute | solution.py:814
  73.0 6.1 %collective-permute-start.14 = (f32[8,32]{1,0:T(8,128)S(1)}, f32[8,32]{1,0:T(8,128)S(1)}, u32[]{:S(2)}, u32[]{:S(2)}) collective-permute-start(f32[8,32]{1,0:T(8,128)S(1)} %maximum_maximum_fusion), channel_id=1, source_target_pairs={{0,192},{16,208},{32,224},{48,240},{64,128},{80,144},{96,160},{112... | collective-permute-start | bytes 3080 | tf_op jit(solution)/shard_map/ppermute | solution.py:814
  75.3 3.8 %collective-permute-start.13 = (f32[8,32]{1,0:T(8,128)S(1)}, f32[8,32]{1,0:T(8,128)S(1)}, u32[]{:S(2)}, u32[]{:S(2)}) collective-permute-start(f32[8,32]{1,0:T(8,128)S(1)} %maximum_maximum_fusion), channel_id=1, source_target_pairs={{0,128},{16,144},{32,160},{48,176},{64,192},{80,208},{96,224},{112... | collective-permute-start | bytes 3080 | tf_op jit(solution)/shard_map/ppermute | solution.py:814
  76.7 5.1 %collective-permute-start.12 = (f32[8,32]{1,0:T(8,128)S(1)}, f32[8,32]{1,0:T(8,128)S(1)}, u32[]{:S(2)}, u32[]{:S(2)}) collective-permute-start(f32[8,32]{1,0:T(8,128)S(1)} %maximum_maximum_fusion), channel_id=1, source_target_pairs={{0,64},{16,80},{32,96},{48,112},{64,0},{80,16},{96,32},{112,48},{1... | collective-permute-start | bytes 3080 | tf_op jit(solution)/shard_map/ppermute | solution.py:814
